TPU v7x, 32 devices: a whole 2x2x4 slice. The times are simulated.
32 devices in a mesh: gx: 8 (over z, x), gy: 4 (over y, core).
Axes of the slice: x: 2, y: 2, z: 4, core: 2. Of those that a mesh axis runs over, the one named last changes fastest.
Arguments:
- displacement: float32 [64, 16, 3, 128], P('gx', 'gy'), may hold values from -6 to 6
- volume: float32 [64, 16, 128], P('gx', 'gy'), may hold values from 0.5 to 2
- health: float32 [64, 16, 128], P('gx', 'gy'), may hold values from 0.2 to 1
- damage: int32 [64, 16, 128], P('gx', 'gy'), may hold values 0 or 1
- block_pairs: int32 [8, 4, 162, 4], P('gx', 'gy'), may hold values from -1 to 9, as said below
Outputs:
- deform_grad: float32 [64, 16, 9, 128], P('gx', 'gy')
- force_density: float32 [64, 16, 3, 128], P('gx', 'gy')
Inputs may be any that keep to these rules, and one draw needn't show every extreme that they name: `block_pairs`: every row is (ax, ay, bx, by) with blocks in a device's frame: its own blocks at 1 to 8 and 1 to 4, the blocks beside them at 0 and 9, 0 and 5; (bx - ax, by - ay) is (1, 0), (0, 1), (1, 1) or (1, -1); both blocks lie inside the plate and at least one is the device's own. A pair of adjacent plate blocks is named at most once over all devices; pairs named nowhere are severed. Live rows come first, then rows of -1. In every draw some device names all 162 pairs that touch its blocks.
All inputs are finite; a program needn't handle non-finite values. No bound on the sum of `damage` on one device may be relied on, other than what follows from the above.
Results may differ from a plain program's by a relative error of at most 0.0003.
Values sent between devices are 32-bit elements; how exact they have to be, the bound alone decides.
No kernel may reach another device: no remote copies, remote signals or barrier semaphores. Data moves between devices by JAX's collectives and lax.ppermute only.
A program may use at most 64 MiB of HBM per device.

v0:
```python
import jax
import jax.numpy as jnp
import numpy as np
from jax import lax
from jax.sharding import PartitionSpec as P

highest = lax.Precision.HIGHEST
lame_first = 24.0
shear_modulus = 16.0
transpose_order = np.array([0, 3, 6, 1, 4, 7, 2, 5, 8])


def with_halo(block, sides, width):
    for axis, dim in sides:
        count = lax.axis_size(axis)
        forward = [(i, i + 1) for i in range(count - 1)]
        backward = [(target, source) for source, target in forward]
        low = lax.ppermute(
            lax.slice_in_dim(block, block.shape[dim] - width, None, axis=dim), axis, forward
        )
        high = lax.ppermute(lax.slice_in_dim(block, 0, width, axis=dim), axis, backward)
        block = jnp.concatenate([low, block, high], axis=dim)
    return block


def lattice(points):
    index = jnp.arange(points, dtype=jnp.int32)
    return jnp.stack([index % 4, index // 4 % 4, index // 16])


def block_offset(step_x, step_y):
    return jnp.stack([4 * step_x, 4 * step_y, jnp.zeros_like(step_x)], axis=1)


def bond_weights(health_first, health_second, step_x, step_y):
    points = health_first.shape[-1]
    lattice_grid = lattice(points)
    shifted = lattice_grid[None] + block_offset(step_x, step_y)[:, :, None]
    distance = jnp.zeros((step_x.shape[0], points, points), jnp.int32)
    for comp_index in range(3):
        gap_comp = shifted[:, comp_index, None, :] - lattice_grid[None, comp_index, :, None]
        distance = distance + gap_comp * gap_comp
    linked = (distance <= 9) & (distance > 0)
    lower_health = jnp.minimum(health_first[:, :, None], health_second[:, None, :])
    return jnp.where(linked, lower_health, jnp.zeros_like(lower_health))


def positions(point_pack, step_x, step_y):
    reference_pos = (
        lattice(point_pack.shape[-1])[None] + block_offset(step_x, step_y)[:, :, None]
    ).astype(jnp.float32)
    return (reference_pos, reference_pos + point_pack[:, 0:3], point_pack[:, 3], point_pack[:, 4])


def shape_features(ref_pos, cur_pos, vol_pts):
    slot_count, points = (ref_pos.shape[0], ref_pos.shape[-1])
    outer_rr = (ref_pos[:, :, None] * ref_pos[:, None]).reshape(slot_count, 9, points)
    outer_cr = (cur_pos[:, :, None] * ref_pos[:, None]).reshape(slot_count, 9, points)
    ones_row = jnp.ones((slot_count, 1, points), jnp.float32)
    return (
        jnp.concatenate([outer_rr, outer_cr, ref_pos, cur_pos, ones_row], axis=1) * vol_pts[:, None]
    )


def shape_terms(tile_sums, ref_pos, cur_pos):
    slot_count, points = (ref_pos.shape[0], ref_pos.shape[-1])
    sum_rr = tile_sums[:, 0:9].reshape(slot_count, 3, 3, points)
    sum_cr = tile_sums[:, 9:18].reshape(slot_count, 3, 3, points)
    sum_r = tile_sums[:, 18:21]
    sum_c = tile_sums[:, 21:24]
    sum_one = tile_sums[:, 24][:, None, None]
    shape_k = (
        sum_rr
        - ref_pos[:, :, None] * sum_r[:, None]
        - sum_r[:, :, None] * ref_pos[:, None]
        + sum_one * ref_pos[:, :, None] * ref_pos[:, None]
    )
    shape_n = (
        sum_cr
        - cur_pos[:, :, None] * sum_r[:, None]
        - sum_c[:, :, None] * ref_pos[:, None]
        + sum_one * cur_pos[:, :, None] * ref_pos[:, None]
    )
    return jnp.concatenate(
        [shape_k.reshape(slot_count, 9, points), shape_n.reshape(slot_count, 9, points)], axis=1
    )


def force_features(ref_pos, stress_map, vol_pts):
    slot_count, points = (ref_pos.shape[0], ref_pos.shape[-1])
    mapped = jnp.sum(stress_map * ref_pos[:, None], axis=2)
    ones_row = jnp.ones((slot_count, 1, points), jnp.float32)
    return (
        jnp.concatenate(
            [mapped, stress_map.reshape(slot_count, 9, points), ref_pos, ones_row], axis=1
        )
        * vol_pts[:, None]
    )


def force_terms(tile_sums, ref_pos, stress_map):
    slot_count, points = (ref_pos.shape[0], ref_pos.shape[-1])
    sum_ar = tile_sums[:, 0:3]
    sum_a = tile_sums[:, 3:12].reshape(slot_count, 3, 3, points)
    spread = tile_sums[:, 12:15] - tile_sums[:, 15][:, None] * ref_pos
    return (
        jnp.sum(stress_map * spread[:, None], axis=2)
        + sum_ar
        - jnp.sum(sum_a * ref_pos[:, None], axis=2)
    )


def tile_terms(pack_first, pack_second, map_first, map_second, step_x, step_y, section):
    zero_step = jnp.zeros_like(step_x)
    ref_a, cur_a, vol_a, health_a = positions(pack_first, zero_step, zero_step)
    ref_b, cur_b, vol_b, health_b = positions(pack_second, step_x, step_y)
    weights = bond_weights(health_a, health_b, step_x, step_y)
    if section == "shape":
        feat_a = shape_features(ref_a, cur_a, vol_a)
        feat_b = shape_features(ref_b, cur_b, vol_b)
    else:
        feat_a = force_features(ref_a, map_first, vol_a)
        feat_b = force_features(ref_b, map_second, vol_b)
    sums_a = jnp.einsum("gcj,gij->gci", feat_b, weights, precision=highest)
    sums_b = jnp.einsum("gci,gij->gcj", feat_a, weights, precision=highest)
    if section == "shape":
        return (shape_terms(sums_a, ref_a, cur_a), shape_terms(sums_b, ref_b, cur_b))
    return (force_terms(sums_a, ref_a, map_first), force_terms(sums_b, ref_b, map_second))


def block_sums(row_pack, row_map, section):
    rows_count, points = (row_pack.shape[0], row_pack.shape[-1])
    zero_step = jnp.zeros((rows_count,), jnp.int32)
    ref_pos, cur_pos, vol_pts, health_pts = positions(row_pack, zero_step, zero_step)
    weights = bond_weights(health_pts, health_pts, zero_step, zero_step)
    if section == "shape":
        feats = shape_features(ref_pos, cur_pos, vol_pts)
        return shape_terms(
            jnp.einsum("gcj,gij->gci", feats, weights, precision=highest), ref_pos, cur_pos
        )
    stress_map = row_map.reshape(rows_count, 3, 3, points)
    feats = force_features(ref_pos, stress_map, vol_pts)
    return force_terms(
        jnp.einsum("gcj,gij->gci", feats, weights, precision=highest), ref_pos, stress_map
    )


def pair_sums(ext_pack, ext_map, slot_list, section):
    ext_x, ext_y, fields, points = ext_pack.shape
    blocks = ext_x * ext_y
    flat_pack = ext_pack.reshape(blocks, fields, points)
    slot_count = slot_list.shape[0]
    turn_count = min(slot_count, 20)
    group_size = -(-slot_count // turn_count)
    filler = jnp.full((group_size * turn_count - slot_count, 4), -1, jnp.int32)
    padded_slots = jnp.concatenate([slot_list, filler], axis=0)
    comp_width = 18 if section == "shape" else 3
    block_ids = jnp.arange(blocks, dtype=jnp.int32)

    def one_group(running, group_slots):
        usable = group_slots[:, 0] >= 0
        first_block = jnp.where(usable, group_slots[:, 0] * ext_y + group_slots[:, 1], 0)
        second_block = jnp.where(usable, group_slots[:, 2] * ext_y + group_slots[:, 3], 0)
        step_x = jnp.where(usable, group_slots[:, 2] - group_slots[:, 0], 0)
        step_y = jnp.where(usable, group_slots[:, 3] - group_slots[:, 1], 0)
        if section == "shape":
            map_first, map_second = (None, None)
        else:
            flat_map = ext_map.reshape(blocks, 3, 3, points)
            map_first, map_second = (flat_map[first_block], flat_map[second_block])
        to_first, to_second = tile_terms(
            flat_pack[first_block],
            flat_pack[second_block],
            map_first,
            map_second,
            step_x,
            step_y,
            section,
        )
        hit_first = ((first_block[:, None] == block_ids[None]) & usable[:, None]).astype(
            jnp.float32
        )
        hit_second = ((second_block[:, None] == block_ids[None]) & usable[:, None]).astype(
            jnp.float32
        )
        running = running + jnp.dot(
            hit_first.T,
            to_first.reshape(group_size, comp_width * points),
            precision=highest,
            preferred_element_type=jnp.float32,
        )
        running = running + jnp.dot(
            hit_second.T,
            to_second.reshape(group_size, comp_width * points),
            precision=highest,
            preferred_element_type=jnp.float32,
        )
        return (running, None)

    running, _ = lax.scan(
        one_group,
        jnp.zeros((blocks, comp_width * points), jnp.float32),
        padded_slots.reshape(turn_count, group_size, 4),
    )
    return running.reshape(ext_x, ext_y, comp_width, points)


def product_three(left_mat, right_mat):
    entry_list = []
    for row_index in range(3):
        for col_index in range(3):
            entry_list.append(
                left_mat[..., 3 * row_index, :] * right_mat[..., col_index, :]
                + left_mat[..., 3 * row_index + 1, :] * right_mat[..., 3 + col_index, :]
                + left_mat[..., 3 * row_index + 2, :] * right_mat[..., 6 + col_index, :]
            )
    return jnp.stack(entry_list, axis=-2)


def invert_three(matrix):
    entry = [matrix[..., slot_index, :] for slot_index in range(9)]
    cof_00 = entry[4] * entry[8] - entry[5] * entry[7]
    cof_01 = entry[5] * entry[6] - entry[3] * entry[8]
    cof_02 = entry[3] * entry[7] - entry[4] * entry[6]
    cof_10 = entry[2] * entry[7] - entry[1] * entry[8]
    cof_11 = entry[0] * entry[8] - entry[2] * entry[6]
    cof_12 = entry[1] * entry[6] - entry[0] * entry[7]
    cof_20 = entry[1] * entry[5] - entry[2] * entry[4]
    cof_21 = entry[2] * entry[3] - entry[0] * entry[5]
    cof_22 = entry[0] * entry[4] - entry[1] * entry[3]
    determinant = entry[0] * cof_00 + entry[1] * cof_01 + entry[2] * cof_02
    adjugate = jnp.stack(
        [cof_00, cof_10, cof_20, cof_01, cof_11, cof_21, cof_02, cof_12, cof_22], axis=-2
    )
    return adjugate / determinant[..., None, :]


def material(shape_sums, damage):
    identity = jnp.eye(3, dtype=jnp.float32).reshape(9)[:, None]
    inverse = invert_three(shape_sums[..., 0:9, :] + identity)
    deform_grad = product_three(shape_sums[..., 9:18, :], inverse)
    strain = 0.5 * (product_three(deform_grad[..., transpose_order, :], deform_grad) - identity)
    strain_trace = strain[..., 0, :] + strain[..., 4, :] + strain[..., 8, :]
    second_pk = lame_first * strain_trace[..., None, :] * identity + 2.0 * shear_modulus * strain
    first_pk = (
        product_three(deform_grad, second_pk) * (1.0 - damage.astype(jnp.float32))[..., None, :]
    )
    return (deform_grad, product_three(first_pk, inverse))


def touching_rows(block_pairs, inner_x, inner_y):
    slot_count = block_pairs.shape[2]
    raised = block_pairs + 1
    cycle_rows = with_halo(raised, (("gx", 0), ("gy", 1)), 1) - 1
    offset_x = (jnp.arange(3, dtype=jnp.int32) - 1) * inner_x
    offset_y = (jnp.arange(3, dtype=jnp.int32) - 1) * inner_y
    grid_x = jnp.broadcast_to(offset_x[:, None], (3, 3))
    grid_y = jnp.broadcast_to(offset_y[None, :], (3, 3))
    offsets = jnp.stack([grid_x, grid_y, grid_x, grid_y], axis=-1)[:, :, None, :]
    live = cycle_rows[..., 0] >= 0
    framed = cycle_rows + offsets
    own_first = (
        (framed[..., 0] >= 1)
        & (framed[..., 0] <= inner_x)
        & (framed[..., 1] >= 1)
        & (framed[..., 1] <= inner_y)
    )
    own_second = (
        (framed[..., 2] >= 1)
        & (framed[..., 2] <= inner_x)
        & (framed[..., 3] >= 1)
        & (framed[..., 3] <= inner_y)
    )
    keep = (live & (own_first | own_second)).reshape(9 * slot_count)
    flat_rows = framed.reshape(9 * slot_count, 4)
    order_key = jnp.where(keep, 0, 9 * slot_count) + jnp.arange(9 * slot_count, dtype=jnp.int32)
    order = jnp.argsort(order_key, stable=True)[:slot_count]
    picked = flat_rows[order]
    kept = keep[order]
    return jnp.where(kept[:, None], picked, -1)


def local(displacement, volume, health, damage, block_pairs):
    inner_x = displacement.shape[0]
    inner_y = displacement.shape[1]
    point_pack = jnp.concatenate([displacement, volume[:, :, None], health[:, :, None]], axis=2)
    ext_pack = with_halo(point_pack, (("gx", 0), ("gy", 1)), 1)
    own_shape = lax.map(lambda row_pack: block_sums(row_pack, None, "shape"), point_pack)
    slot_list = touching_rows(block_pairs, inner_x, inner_y)
    shape_sums = (
        pair_sums(ext_pack, None, slot_list, "shape")[1 : inner_x + 1, 1 : inner_y + 1] + own_shape
    )
    deform_grad, stress_map = material(shape_sums, damage)
    ext_map = with_halo(stress_map, (("gx", 0), ("gy", 1)), 1)
    own_force = lax.map(
        lambda row_items: block_sums(row_items[0], row_items[1], "force"), (point_pack, stress_map)
    )
    force_density = (
        pair_sums(ext_pack, ext_map, slot_list, "force")[1 : inner_x + 1, 1 : inner_y + 1]
        + own_force
    )
    return (deform_grad, force_density)


def solution(mesh):
    in_specs = (
        P("gx", "gy", None, None),
        P("gx", "gy", None),
        P("gx", "gy", None),
        P("gx", "gy", None),
        P("gx", "gy", None, None),
    )
    out_specs = (P("gx", "gy", None, None), P("gx", "gy", None, None))
    return jax.shard_map(local, mesh=mesh, in_specs=in_specs, out_specs=out_specs, check_vma=False)
```

profile of v0, /device:TPU:0, one launch (start us, length us, event | category | flops | bytes accessed | tf_op | source)
XLA Modules:
  0.0 350.2 jit_solution(1019852410540172457)
XLA Ops:
  1.3 4.8 %collective-permute-start = (s32[1,1,162,4]{2,3,1,0:T(4,128)S(1)}, s32[1,1,162,4]{2,3,1,0:T(4,128)S(1)}, u32[]{:S(2)}, u32[]{:S(2)}) collective-permute-start(s32[1,1,162,4]{2,3,1,0:T(4,128)S(1)} %broadcast_add_fusion.3), channel_id=1, source_target_pairs={{0,4},{4,8},{8,12},{12,16},{16,20},{20,24},{24,28},{1,5},{5,9},{9,... | collective-permute-start | bytes 7784 | tf_op jit(solution)/shard_map/ppermute | solution.py:18
  6.2 1.3 collective-permute-start.1
  8.3 4.5 %collective-permute-start.4 = (f32[1,4,5,128]{3,1,2,0:T(4,128)S(1)}, f32[1,4,5,128]{3,1,2,0:T(4,128)S(1)}, u32[]{:S(2)}, u32[]{:S(2)}) collective-permute-start(f32[1,4,5,128]{3,1,2,0:T(4,128)S(1)} %get-tuple-element.687), channel_id=1, source_target_pairs={{0,4},{4,8},{8,12},{12,16},{16,20},{20,24},{24,28},{1,5},{5,9},{9,... | collective-permute-start | bytes 30728 | tf_op jit(solution)/shard_map/ppermute | solution.py:18
  12.9 1.3 collective-permute-start.5
  14.2 27.4 %while.57 = (s32[]{:T(128)}, f32[8,4,18,128]{3,0,1,2:T(8,128)S(1)}, f32[8,4,5,128]{3,1,2,0:T(4,128)S(1)}, s32[]{:T(128)}, f32[]{:T(128)}, /*index=5*/s32[]{:T(128)}) while((s32[]{:T(128)}, f32[8,4,18,128]{3,0,1,2:T(8,128)S(1)}, f32[8,4,5,128]{3,1,2,0:T(4,128)S(1)}, s32[]{:T(128)}, f32[]{:T(128)}, /*index=5*/s32[]{:T(128)}) %tuple.308), condition=%wide.region_4.5_spmd, body=%wide.region_3.4_spmd.sunk | while | flops 20611072 | bytes 1072721 | solution.py:288
  15.6 2.1 dynamic_update_slice.19
  19.0 2.1 dynamic_update_slice.19
  22.4 2.1 dynamic_update_slice.19
  25.9 2.1 dynamic_update_slice.19
  29.3 2.1 dynamic_update_slice.19
  32.7 2.1 dynamic_update_slice.19
  36.1 2.1 dynamic_update_slice.19
  39.6 2.1 dynamic_update_slice.19
  43.2 1.3 collective-permute-start.3
  44.6 4.8 %collective-permute-start.6 = (f32[10,1,5,128]{3,1,2,0:T(1,128)S(1)}, f32[10,1,5,128]{3,1,2,0:T(1,128)S(1)}, u32[]{:S(2)}, u32[]{:S(2)}) collective-permute-start(f32[10,1,5,128]{3,1,2,0:T(1,128)S(1)} %get-tuple-element.685), channel_id=1, source_target_pairs={{0,1},{1,2},{2,3},{4,5},{5,6},{6,7},{8,9},{9,10},{10,11},{12,13},{... | collective-permute-start | bytes 76808 | tf_op jit(solution)/shard_map/ppermute | solution.py:18
  51.0 5.1 %sort.17 = (s32[1458]{0:T(1024)}, s32[1458]{0:T(1024)S(1)}) sort(s32[1458]{0:T(1024)S(1)} %iota_add_fusion, s32[1458]{0:T(1024)S(1)} %iota.301), dimensions={0}, to_apply=%region_0.1 | sort | flops 16038 | bytes 23328 | tf_op jit(solution)/shard_map/jit(argsort)/sort | solution.py:277
  56.8 1.6 gather_fusion.6
  59.9 129.7 %while.59 = (s32[]{:T(128)}, f32[60,2304]{1,0:T(8,128)S(1)}, s32[20,9,4]{1,2,0:T(4,128)S(1)}, f32[60,5,128]{2,1,0:T(8,128)S(1)}, s32[]{:T(128)}, /*index=5*/f32[]{:T(128)}, s32[]{:T(128)}, f32[]{:T(128)}) while((s32[]{:T(128)}, f32[60,2304]{1,0:T(8,128)S(1)}, s32[20,9,4]{1,2,0:T(4,128)S(1)}, ...), condition=%wide.region_2.3_spmd.clone.clone, body=%wide.region_1.2_spmd.clone.clone.sunk | while | flops 123013720 | bytes 8238270 | solution.py:200
  191.7 5.0 %collective-permute-start.8 = (f32[1,4,9,128]{3,0,1,2:T(1,128)S(1)}, f32[1,4,9,128]{3,0,1,2:T(1,128)S(1)}, u32[]{:S(2)}, u32[]{:S(2)}) collective-permute-start(f32[1,4,9,128]{3,0,1,2:T(1,128)S(1)} %get-tuple-element.683), channel_id=1, source_target_pairs={{0,4},{4,8},{8,12},{12,16},{16,20},{20,24},{24,28},{1,5},{5,9},{9,... | collective-permute-start | bytes 55304 | tf_op jit(solution)/shard_map/ppermute | solution.py:18
  198.1 5.1 %collective-permute-done.9 = f32[1,4,9,128]{3,0,1,2:T(1,128)S(1)} collective-permute-done((f32[1,4,9,128]{3,0,1,2:T(1,128)S(1)}, f32[1,4,9,128]{3,0,1,2:T(1,128)S(1)}, u32[]{:S(2)}, u32[]{:S(2)}) %collective-permute-start.9) | collective-permute-done | bytes 18464 | tf_op jit(solution)/shard_map/ppermute | solution.py:21
  203.3 3.1 collective-permute-start.10
  206.4 1.5 collective-permute-start.11
  207.9 8.8 %while.58 = (s32[]{:T(128)}, f32[8,4,3,128]{3,2,1,0:T(4,128)S(1)}, f32[8,4,9,128]{3,0,1,2:T(8,128)S(1)}, f32[8,4,5,128]{3,1,2,0:T(4,128)S(1)}, s32[]{:T(128)}, /*index=5*/f32[]{:T(128)}, f32[]{:T(128)}) while((s32[]{:T(128)}, f32[8,4,3,128]{3,2,1,0:T(4,128)S(1)}, f32[8,4,9,128]{3,0,1,2:T(8,128)S(1)}, f32[8,4,5,128]{3,1,2,0:T(4,128)S(1)}, ...), condition=%wide.region_17.18_spmd, body=%wide.region_13.17_spmd.sunk | while | flops 13505922 | bytes 431841 | solution.py:295
  218.4 131.1 %while.60 = (s32[]{:T(128)}, f32[60,384]{1,0:T(8,128)S(1)}, s32[20,9,4]{1,2,0:T(4,128)S(1)}, f32[10,6,9,128]{3,1,0,2:T(8,128)}, f32[60,5,128]{2,1,0:T(8,128)S(1)...) while((s32[]{:T(128)}, f32[60,384]{1,0:T(8,128)S(1)}, ...), condition=%wide.wide.region_12.13_spmd.clone.clone, body=%wide.wide.region_5.12_spmd.clone.clone.sunk | while | flops 65808856 | bytes 2965474 | solution.py:200
  (3273 shorter events, 271.5 us)
Async XLA Ops:
  1.3 40.6 %collective-permute-start = (s32[1,1,162,4]{2,3,1,0:T(4,128)S(1)}, s32[1,1,162,4]{2,3,1,0:T(4,128)S(1)}, u32[]{:S(2)}, u32[]{:S(2)}) collective-permute-start(s32[1,1,162,4]{2,3,1,0:T(4,128)S(1)} %broadcast_add_fusion.3), channel_id=1, source_target_pairs={{0,4},{4,8},{8,12},{12,16},{16,20},{20,24},{24,28},{1,5},{5,9},{9,... | collective-permute-start | bytes 7784 | tf_op jit(solution)/shard_map/ppermute | solution.py:18
  6.2 35.7 %collective-permute-start.1 = (s32[1,1,162,4]{2,3,1,0:T(4,128)S(1)}, s32[1,1,162,4]{2,3,1,0:T(4,128)S(1)}, u32[]{:S(2)}, u32[]{:S(2)}) collective-permute-start(s32[1,1,162,4]{2,3,1,0:T(4,128)S(1)} %broadcast_add_fusion.3), channel_id=1, source_target_pairs={{4,0},{8,4},{12,8},{16,12},{20,16},{24,20},{28,24},{5,1},{9,5},{13... | collective-permute-start | bytes 7784 | tf_op jit(solution)/shard_map/ppermute | solution.py:21
  8.3 36.2 %collective-permute-start.4 = (f32[1,4,5,128]{3,1,2,0:T(4,128)S(1)}, f32[1,4,5,128]{3,1,2,0:T(4,128)S(1)}, u32[]{:S(2)}, u32[]{:S(2)}) collective-permute-start(f32[1,4,5,128]{3,1,2,0:T(4,128)S(1)} %get-tuple-element.687), channel_id=1, source_target_pairs={{0,4},{4,8},{8,12},{12,16},{16,20},{20,24},{24,28},{1,5},{5,9},{9,... | collective-permute-start | bytes 30728 | tf_op jit(solution)/shard_map/ppermute | solution.py:18
  12.9 31.7 %collective-permute-start.5 = (f32[1,4,5,128]{3,1,2,0:T(4,128)S(1)}, f32[1,4,5,128]{3,1,2,0:T(4,128)S(1)}, u32[]{:S(2)}, u32[]{:S(2)}) collective-permute-start(f32[1,4,5,128]{3,1,2,0:T(4,128)S(1)} %get-tuple-element.688), channel_id=1, source_target_pairs={{4,0},{8,4},{12,8},{16,12},{20,16},{24,20},{28,24},{5,1},{9,5},{13... | collective-permute-start | bytes 30728 | tf_op jit(solution)/shard_map/ppermute | solution.py:21
  14.2 27.4 %copy-start.4 = (s32[8,4,128]{2,1,0:T(4,128)S(1)}, s32[8,4,128]{2,1,0:T(4,128)}, u32[]{:S(2)}) copy-start(s32[8,4,128]{2,1,0:T(4,128)} %param.18) | copy-start | bytes 49156
  14.2 30.3 %copy-start.3 = (f32[8,4,128]{2,1,0:T(4,128)S(1)}, f32[8,4,128]{2,1,0:T(4,128)}, u32[]{:S(2)}) copy-start(f32[8,4,128]{2,1,0:T(4,128)} %param.16) | copy-start | bytes 49156
  41.7 2.8 copy-start.1
  41.9 2.7 copy-start.2
  41.9 8.8 %collective-permute-start.2 = (s32[3,1,162,4]{2,1,3,0:T(1,128)S(1)}, s32[3,1,162,4]{2,1,3,0:T(1,128)S(1)}, u32[]{:S(2)}, u32[]{:S(2)}) collective-permute-start(s32[3,1,162,4]{2,1,3,0:T(1,128)S(1)} %copy.205), channel_id=1, source_target_pairs={{0,1},{1,2},{2,3},{4,5},{5,6},{6,7},{8,9},{9,10},{10,11},{12,13},{... | collective-permute-start | bytes 23336 | tf_op jit(solution)/shard_map/ppermute | solution.py:18
  43.2 7.5 %collective-permute-start.3 = (s32[3,1,162,4]{2,1,3,0:T(1,128)S(1)}, s32[3,1,162,4]{2,1,3,0:T(1,128)S(1)}, u32[]{:S(2)}, u32[]{:S(2)}) collective-permute-start(s32[3,1,162,4]{2,1,3,0:T(1,128)S(1)} %copy.205), channel_id=1, source_target_pairs={{1,0},{2,1},{3,2},{5,4},{6,5},{7,6},{9,8},{10,9},{11,10},{13,12},{... | collective-permute-start | bytes 23336 | tf_op jit(solution)/shard_map/ppermute | solution.py:21
  44.6 15.1 %collective-permute-start.6 = (f32[10,1,5,128]{3,1,2,0:T(1,128)S(1)}, f32[10,1,5,128]{3,1,2,0:T(1,128)S(1)}, u32[]{:S(2)}, u32[]{:S(2)}) collective-permute-start(f32[10,1,5,128]{3,1,2,0:T(1,128)S(1)} %get-tuple-element.685), channel_id=1, source_target_pairs={{0,1},{1,2},{2,3},{4,5},{5,6},{6,7},{8,9},{9,10},{10,11},{12,13},{... | collective-permute-start | bytes 76808 | tf_op jit(solution)/shard_map/ppermute | solution.py:18
  49.4 10.4 %collective-permute-start.7 = (f32[10,1,5,128]{3,1,2,0:T(1,128)S(1)}, f32[10,1,5,128]{3,1,2,0:T(1,128)S(1)}, u32[]{:S(2)}, u32[]{:S(2)}) collective-permute-start(f32[10,1,5,128]{3,1,2,0:T(1,128)S(1)} %get-tuple-element.686), channel_id=1, source_target_pairs={{1,0},{2,1},{3,2},{5,4},{6,5},{7,6},{9,8},{10,9},{11,10},{13,12},{... | collective-permute-start | bytes 76808 | tf_op jit(solution)/shard_map/ppermute | solution.py:21
  56.1 0.7 copy-start.5
  191.7 6.4 %collective-permute-start.8 = (f32[1,4,9,128]{3,0,1,2:T(1,128)S(1)}, f32[1,4,9,128]{3,0,1,2:T(1,128)S(1)}, u32[]{:S(2)}, u32[]{:S(2)}) collective-permute-start(f32[1,4,9,128]{3,0,1,2:T(1,128)S(1)} %get-tuple-element.683), channel_id=1, source_target_pairs={{0,4},{4,8},{8,12},{12,16},{16,20},{20,24},{24,28},{1,5},{5,9},{9,... | collective-permute-start | bytes 55304 | tf_op jit(solution)/shard_map/ppermute | solution.py:18
  196.7 6.6 %collective-permute-start.9 = (f32[1,4,9,128]{3,0,1,2:T(1,128)S(1)}, f32[1,4,9,128]{3,0,1,2:T(1,128)S(1)}, u32[]{:S(2)}, u32[]{:S(2)}) collective-permute-start(f32[1,4,9,128]{3,0,1,2:T(1,128)S(1)} %get-tuple-element.684), channel_id=1, source_target_pairs={{4,0},{8,4},{12,8},{16,12},{20,16},{24,20},{28,24},{5,1},{9,5},{13... | collective-permute-start | bytes 55304 | tf_op jit(solution)/shard_map/ppermute | solution.py:21
  203.3 14.2 %collective-permute-start.10 = (f32[10,1,9,128]{3,0,1,2:T(8,128)S(1)}, f32[10,1,9,128]{3,0,1,2:T(8,128)S(1)}, u32[]{:S(2)}, u32[]{:S(2)}) collective-permute-start(f32[10,1,9,128]{3,0,1,2:T(8,128)S(1)} %get-tuple-element.681), channel_id=1, source_target_pairs={{0,1},{1,2},{2,3},{4,5},{5,6},{6,7},{8,9},{9,10},{10,11},{12,13},{... | collective-permute-start | bytes 138248 | tf_op jit(solution)/shard_map/ppermute | solution.py:18
  206.4 11.0 %collective-permute-start.11 = (f32[10,1,9,128]{3,0,1,2:T(8,128)S(1)}, f32[10,1,9,128]{3,0,1,2:T(8,128)S(1)}, u32[]{:S(2)}, u32[]{:S(2)}) collective-permute-start(f32[10,1,9,128]{3,0,1,2:T(8,128)S(1)} %get-tuple-element.682), channel_id=1, source_target_pairs={{1,0},{2,1},{3,2},{5,4},{6,5},{7,6},{9,8},{10,9},{11,10},{13,12},{... | collective-permute-start | bytes 138248 | tf_op jit(solution)/shard_map/ppermute | solution.py:21
  217.6 0.7 copy-start
where the time goes:
time: 354 us; the launch traced here: 350 us
  matrix products  131 us (37%)
  local copies, waits for them, and re-layouts  129 us (36%)
  starting transfers between devices  31.5 us (9%)
  other arithmetic  31 us (9%)
  loops' own time  21.1 us (6%)
  waiting for transfers between devices  5.27 us (1%)
    dot_general x40, matrix products, tile_terms(): sums_a = jnp.einsum('gcj,gij->gci', feat_b, weights, precision=highest)  50.9 us
    dot_general x40, matrix products, tile_terms(): sums_b = jnp.einsum('gci,gij->gcj', feat_a, weights, precision=highest)  35.8 us
    ppermute x6, starting transfers between devices, with_halo(): lax.ppermute(lax.slice_in_dim(block, block.shape[dim] - width, None, axis...  23.6 us
    gather x40, local copies, waits for them, and re-layouts, one_group(): map_first, map_second = (flat_map[first_block], flat_map[second_block])  23.4 us
    gather x40, local copies, waits for them, and re-layouts, one_group(): flat_pack[first_block]  22.2 us
    gather x40, local copies, waits for them, and re-layouts, one_group(): flat_pack[second_block]  22.2 us
    another operation x2, loops' own time, pair_sums(): lax.scan(one_group, jnp.zeros((blocks, comp_width * points), jnp.float32)...  17.9 us
    dot_general x40, matrix products, one_group(): jnp.dot(hit_first.T, to_first.reshape(group_size, comp_width * points), p...  17 us
  transfers between devices with their start and end apart: 12, of which 2 were waited for; matrix products, arithmetic and copies ran while one was open for 12% of the time, Pallas kernels for 0%

commit v1 on v0

v1 whole, which is shorter than its diff:
```python
import functools

import jax
import jax.numpy as jnp
from jax import lax
from jax.experimental import pallas as pl
from jax.experimental.pallas import tpu as pltpu
from jax.sharding import PartitionSpec as P

LANES = 128
ROWS = 8
SIDE = 4
REACH = 3
REACH_SQ = 9
RING = 2
FIELDS = 6
VOL, HEALTH, DAMAGE = 3, 4, 5
LAME = 24.0
SHEAR = 16.0
KINDS = ((1, 0), (0, 1), (1, 1), (1, -1))
SITES = 2 * SIDE
PATCH_X = SIDE + 2 * REACH
PATCH_Y = 2 + 2 * REACH
ENTRIES = PATCH_X * PATCH_Y


def iota(shape, dim):
    return lax.broadcasted_iota(jnp.int32, shape, dim)


def divide(value, step, top):
    total = jnp.zeros_like(value)
    for k in range(1, top):
        total = total + jnp.where(value >= step * k, 1, 0)
    return total


def lanes_of(value, index):
    return jnp.take_along_axis(value, index, axis=1, mode="promise_in_bounds")


def even_odd(array, axis):
    count = lax.axis_size(axis)
    even = [(i, i ^ 1) for i in range(count) if i ^ 1 < count]
    odd = [(i, ((i + 1) ^ 1) - 1) for i in range(1, count) if ((i + 1) ^ 1) - 1 < count]
    return even, odd


def entry_used(x_at, y_at):
    return any(
        (x_at - i) ** 2 + (y_at - j) ** 2 <= REACH_SQ for i in range(SIDE) for j in range(2)
    )


ENTRY_LIST = [
    (x_at, y_at)
    for x_at in range(-REACH, SIDE + REACH)
    for y_at in range(-REACH, 2 + REACH)
    if entry_used(x_at, y_at)
]


def entry_index(x_at, y_at):
    return (x_at + REACH) * PATCH_Y + y_at + REACH


def own_row(raw, field, x, y):
    disp, vol, health, damage = raw
    if field < 3:
        return disp[x, y, field : field + 1, :]
    if field == VOL:
        return vol[x, pl.ds(y, 1), :]
    if field == HEALTH:
        return health[x, pl.ds(y, 1), :]
    return damage[x, pl.ds(y, 1), :].astype(jnp.float32)


def pack_kernel(nx, ny, disp, vol, health, damage, pairs, to_even, to_odd):
    raw = (disp, vol, health, damage)
    odd_here = lax.rem(lax.axis_index("gy"), 2)
    ext_x = nx + 2 * RING
    slots = pairs.shape[0]
    ax, ay = pairs[:, 0:1], pairs[:, 1:2]
    bx, by = pairs[:, 2:3], pairs[:, 3:4]
    kind = jnp.where(bx == ax, 1, jnp.where(by == ay, 0, jnp.where(by > ay, 2, 3)))
    code = jnp.where(ax >= 0, kind * ext_x + ax + 1, -1)
    hit_x = jnp.where(code == iota((slots, LANES), 1), 1.0, 0.0).astype(jnp.bfloat16)
    hit_y = jnp.where(ay + 1 == iota((slots, LANES), 1), 1.0, 0.0).astype(jnp.bfloat16)
    table = lax.dot_general(
        hit_y, hit_x, (((0,), (0,)), ((), ())), preferred_element_type=jnp.float32
    )[0:ROWS]
    for target, start in ((to_even, (1 - odd_here) * (ny - RING)), (to_odd, odd_here * (ny - RING))):
        for field in range(FIELDS):
            for x in range(nx):
                for y in range(RING):
                    row = (field * nx + x) * RING + y
                    target[row : row + 1, :] = own_row(raw, field, x, start + y)
        target[FIELDS * nx * RING :, :] = table


def sides(from_even, from_odd, odd_here):
    low = jnp.where(odd_here == 1, from_even[...], from_odd[...])
    high = jnp.where(odd_here == 1, from_odd[...], from_even[...])
    return low, high


def middle_kernel(nx, ny, disp, vol, health, damage, y_mine, y_even, y_odd, to_even, to_odd):
    raw = (disp, vol, health, damage)
    odd_x, odd_y = lax.rem(lax.axis_index("gx"), 2), lax.rem(lax.axis_index("gy"), 2)
    ext_y = ny + 2 * RING
    halo_rows = FIELDS * nx * RING
    is_odd = odd_y == 1
    at_row = iota((ROWS, LANES), 0)
    table = y_mine[halo_rows:, :]
    even_table = y_even[halo_rows:, :]
    odd_table = y_odd[halo_rows:, :]
    low_table = jnp.where(is_odd, even_table, odd_table)
    high_table = jnp.where(is_odd, odd_table, even_table)
    table = table + jnp.where(at_row >= ny, pltpu.roll(high_table, ny, 0), 0.0)
    table = table + jnp.where(at_row < 2 * RING, pltpu.roll(low_table, ROWS - ny, 0), 0.0)
    for target, start in ((to_even, (1 - odd_x) * (nx - RING)), (to_odd, odd_x * (nx - RING))):
        for field in range(FIELDS):
            for x in range(RING):
                base = (field * RING + x) * ext_y
                for y in range(ny):
                    target[base + RING + y : base + RING + y + 1, :] = own_row(
                        raw, field, start + x, y
                    )
                for y in range(RING):
                    halo = pl.ds((field * nx + start + x) * RING + y, 1)
                    even_row, odd_row = y_even[halo, :], y_odd[halo, :]
                    at = base + y
                    target[at : at + 1, :] = jnp.where(is_odd, even_row, odd_row)
                    at = base + RING + ny + y
                    target[at : at + 1, :] = jnp.where(is_odd, odd_row, even_row)
        target[FIELDS * RING * ext_y :, :] = table


def bond_steps(dz):
    left = REACH_SQ - dz * dz
    for dx in range(-REACH, REACH + 1):
        steps = [
            dy
            for dy in range(-REACH, REACH + 1)
            if dx * dx + dy * dy <= left and (dx, dy, dz) != (0, 0, 0)
        ]
        if steps:
            yield dx, steps


def plus(total, term):
    return term if total is None else total + term


def scaled(value, factor):
    if factor == 0 or value is None:
        return None
    if factor == 1:
        return value
    if factor == -1:
        return -value
    return value * float(factor)


def add_scaled(total, value, factor):
    if factor == 0 or value is None:
        return total
    if total is None:
        return scaled(value, factor)
    if factor == 1:
        return total + value
    if factor == -1:
        return total - value
    return total + value * float(factor)


def signed_sums(terms, order):
    even, odd = {}, {}
    for dy in sorted({abs(dy) for dy in terms}):
        if dy == 0:
            even[0] = terms[0]
        else:
            even[dy] = terms[dy] + terms[-dy]
            odd[dy] = terms[dy] - terms[-dy]
    sums = [None] * (order + 1)
    for dy, value in even.items():
        sums[0] = plus(sums[0], value)
    for dy, value in odd.items():
        sums[1] = add_scaled(sums[1], value, dy)
    if order == 2:
        for dy, value in even.items():
            sums[2] = add_scaled(sums[2], value, dy * dy)
    return sums


def product(left, right):
    return [
        sum(left[3 * a + k] * right[3 * k + b] for k in range(1, 3)) + left[3 * a] * right[b]
        for a in range(3)
        for b in range(3)
    ]


def material(shape, moment, alive):
    e = shape
    cof_00 = e[4] * e[8] - e[5] * e[7]
    cof_01 = e[5] * e[6] - e[3] * e[8]
    cof_02 = e[3] * e[7] - e[4] * e[6]
    cof_11 = e[0] * e[8] - e[2] * e[6]
    cof_12 = e[1] * e[6] - e[0] * e[7]
    cof_22 = e[0] * e[4] - e[1] * e[3]
    scale = 1.0 / (e[0] * cof_00 + e[1] * cof_01 + e[2] * cof_02)
    i00, i01, i02 = cof_00 * scale, cof_01 * scale, cof_02 * scale
    i11, i12, i22 = cof_11 * scale, cof_12 * scale, cof_22 * scale
    inverse = [i00, i01, i02, i01, i11, i12, i02, i12, i22]
    grad = product(moment, inverse)
    strain = {}
    for a in range(3):
        for b in range(a, 3):
            value = grad[a] * grad[b] + grad[3 + a] * grad[3 + b] + grad[6 + a] * grad[6 + b]
            strain[a, b] = value - 1.0 if a == b else value
    trace = strain[0, 0] + strain[1, 1] + strain[2, 2]
    second = [None] * 9
    for (a, b), value in strain.items():
        entry = value * SHEAR
        if a == b:
            entry = entry + trace * (0.5 * LAME)
        second[3 * a + b] = second[3 * b + a] = entry
    inverse = [value * alive for value in inverse]
    return grad, product(product(grad, second), inverse)


def main_kernel(
    nx, ny, disp, vol, health, damage, x_mine, y_even, y_odd, x_even, x_odd, out_grad, out_force,
    ext, turned, weighted, patch, tall, site, stress, spread, result, gathered, rows_out
):
    raw = (disp, vol, health, damage)
    odd_x, odd_y = lax.rem(lax.axis_index("gx"), 2), lax.rem(lax.axis_index("gy"), 2)
    ext_x, ext_y = nx + 2 * RING, ny + 2 * RING
    ring_y = ny + 2
    wide = 2 * ring_y
    tile = (ROWS, LANES)
    lane = iota(tile, 1)
    at_row = iota(tile, 0)
    at_x = divide(lane, wide, nx + 4)
    at_half = lane - wide * at_x
    at_y = lax.shift_right_logical(at_half, 1)
    upper = (at_half & 1) == 1

    y_low, y_high = sides(y_even, y_odd, odd_y)
    x_low, x_high = sides(x_even, x_odd, odd_x)
    side_rows = RING * ext_y
    for field in range(FIELDS):
        base = field * LANES
        ext[base : base + side_rows, :] = x_low[field * side_rows : (field + 1) * side_rows]
        high_at = base + (RING + nx) * ext_y
        ext[high_at : high_at + side_rows, :] = x_high[field * side_rows : (field + 1) * side_rows]
        for x in range(nx):
            at = base + (RING + x) * ext_y
            halo = (field * nx + x) * RING
            ext[at : at + RING, :] = y_low[halo : halo + RING]
            ext[at + RING + ny : at + 2 * RING + ny, :] = y_high[halo : halo + RING]
            for y in range(ny):
                ext[at + RING + y : at + RING + y + 1, :] = own_row(raw, field, x, y)

    for field in range(FIELDS):
        turned[field * LANES : (field + 1) * LANES, :] = ext[
            field * LANES : (field + 1) * LANES, :
        ].T
    for comp in range(3):
        weighted[comp * LANES : (comp + 1) * LANES, :] = (
            turned[comp * LANES : (comp + 1) * LANES, :]
            * turned[VOL * LANES : (VOL + 1) * LANES, :]
        )

    table = x_mine[FIELDS * side_rows :, :]
    at_e = lane - ext_x * divide(lane, ext_x, LANES // ext_x + 1)
    table = table + jnp.where(
        at_e >= nx, pltpu.roll(x_high[FIELDS * side_rows :], nx, 1), 0.0
    )
    table = table + jnp.where(
        at_e < 2 * RING, pltpu.roll(x_low[FIELDS * side_rows :], LANES - nx, 1), 0.0
    )
    link = {}
    for kind, step in enumerate(KINDS):
        for sign in (1, -1):
            move = (0, 0) if sign == 1 else (-step[0], -step[1])
            picked = lanes_of(table, kind * ext_x + at_x + 1 + move[0])
            picked = jnp.where(at_row == at_y + 1 + move[1], picked, 0.0)
            link[sign * step[0], sign * step[1]] = jnp.broadcast_to(
                jnp.sum(picked, axis=0, keepdims=True), tile
            )

    index = {
        (sx, sy): (at_x + 1 + sx) * ext_y + at_y + 1 + sy for sx in (-1, 0, 1) for sy in (-1, 0, 1)
    }

    def half_blocks(source, field, x_at, y_at):
        sx, sy0, sy1 = x_at // SIDE, y_at // SIDE, (y_at + 2) // SIDE
        i, j0, j1 = x_at % SIDE, y_at % SIDE, (y_at + 2) % SIDE
        first = source[pl.ds(field * LANES + SIDE * j0 + i, ROWS, stride=SIDE * SIDE), :]
        second = source[pl.ds(field * LANES + SIDE * j1 + i, ROWS, stride=SIDE * SIDE), :]
        return jnp.where(
            upper, lanes_of(second, index[sx, sy1]), lanes_of(first, index[sx, sy0])
        )

    masks = {}
    for x_at, y_at in ENTRY_LIST:
        sx, sy0, sy1 = x_at // SIDE, y_at // SIDE, (y_at + 2) // SIDE
        at = entry_index(x_at, y_at)
        strength = half_blocks(turned, HEALTH, x_at, y_at)
        if (sx, sy0, sy1) != (0, 0, 0):
            if (sx, sy0, sy1) not in masks:
                one = jnp.ones(tile, jnp.float32)
                masks[sx, sy0, sy1] = jnp.where(
                    upper, link.get((sx, sy1), one), link.get((sx, sy0), one)
                )
            strength = strength * masks[sx, sy0, sy1]
        patch[at] = strength
        patch[ENTRIES + at] = half_blocks(turned, VOL, x_at, y_at)
        for comp in range(3):
            patch[(2 + comp) * ENTRIES + at] = half_blocks(weighted, comp, x_at, y_at)
    for i in range(SIDE):
        for j in range(2):
            at = 2 * i + j
            tall[24 * at : 24 * at + 8, :] = jnp.zeros(tile, jnp.float32)
            tall[24 * at + 8 : 24 * at + 16, :] = patch[entry_index(i, j)]
            tall[24 * at + 16 : 24 * at + 24, :] = jnp.zeros(tile, jnp.float32)
            for comp in range(3):
                site[comp * SITES + at] = half_blocks(turned, comp, i, j)
            site[3 * SITES + at] = 1.0 - half_blocks(turned, DAMAGE, i, j)

    def shape_site(at, carry):
        base = lax.shift_right_logical(at, 1) * PATCH_Y + (at & 1)
        shape = {}
        moment = {}
        first = {}
        for dz in range(-REACH, REACH + 1):
            here = tall[pl.ds(24 * at + 8 - dz, ROWS), :]
            acc = {}
            acc_u = [{}, {}, {}]

            def gain(store, key, value, factor=1):
                store[key] = add_scaled(store.get(key), value, factor)

            for dx, steps in bond_steps(dz):
                terms = {}
                terms_u = [{}, {}, {}]
                for dy in steps:
                    k = base + (dx + REACH) * PATCH_Y + dy + REACH
                    strength = jnp.minimum(here, patch[k])
                    terms[dy] = strength * patch[ENTRIES + k]
                    for comp in range(3):
                        terms_u[comp][dy] = strength * patch[(2 + comp) * ENTRIES + k]
                t0, t1, t2 = signed_sums(terms, 2)
                if dz:
                    gain(acc, "1", t0)
                gain(acc, "x", t0, dx)
                gain(acc, "xx", t0, dx * dx)
                gain(acc, "y", t1)
                gain(acc, "xy", t1, dx)
                gain(acc, "yy", t2)
                for comp in range(3):
                    s0, s1 = signed_sums(terms_u[comp], 1)
                    if dz:
                        gain(acc_u[comp], "1", s0)
                    gain(acc_u[comp], "x", s0, dx)
                    gain(acc_u[comp], "y", s1)

            def back(value):
                if value is None or dz == 0:
                    return value
                return pltpu.roll(value, (-dz) % ROWS, 0)

            moved = {key: back(value) for key, value in acc.items()}
            for key in ("xx", "xy", "yy"):
                gain(shape, key, moved.get(key))
            gain(shape, "xz", moved.get("x"), dz)
            gain(shape, "yz", moved.get("y"), dz)
            gain(shape, "zz", moved.get("1"), dz * dz)
            gain(first, "x", moved.get("x"))
            gain(first, "y", moved.get("y"))
            gain(first, "z", moved.get("1"), dz)
            for comp in range(3):
                moved_u = {key: back(value) for key, value in acc_u[comp].items()}
                gain(moment, (comp, 0), moved_u.get("x"))
                gain(moment, (comp, 1), moved_u.get("y"))
                gain(moment, (comp, 2), moved_u.get("1"), dz)
        kxx, kxy, kyy = shape["xx"], shape["xy"], shape["yy"]
        kxz, kyz, kzz = shape["xz"], shape["yz"], shape["zz"]
        plain = [kxx, kxy, kxz, kxy, kyy, kyz, kxz, kyz, kzz]
        arm = [first["x"], first["y"], first["z"]]
        moments = []
        for a in range(3):
            here_u = site[a * SITES + at]
            for b in range(3):
                moments.append(moment[a, b] + plain[3 * a + b] - here_u * arm[b])
        full = [value + 1.0 if k in (0, 4, 8) else value for k, value in enumerate(plain)]
        grad, carried = material(full, moments, site[3 * SITES + at])
        here_vol = patch[ENTRIES + base + REACH * PATCH_Y + REACH]
        for k in range(9):
            result[k * SITES + at] = grad[k]
            stress[k * SITES + at] = carried[k] * here_vol
        for a in range(3):
            result[(9 + a) * SITES + at] = (
                carried[3 * a] * arm[0] + carried[3 * a + 1] * arm[1] + carried[3 * a + 2] * arm[2]
            )
        return carry

    lax.fori_loop(0, SITES, shape_site, 0)

    for k in range(9):
        for x_at, y_at in ENTRY_LIST:
            sx, i = x_at // SIDE, x_at % SIDE
            half, j = y_at // 2, y_at % 2
            value = stress[k * SITES + 2 * i + j]
            move = (-(wide * sx + half)) % LANES
            if move:
                value = pltpu.roll(value, move, 1)
            spread[k * ENTRIES + entry_index(x_at, y_at)] = value

    def force_site(at, carry):
        base = lax.shift_right_logical(at, 1) * PATCH_Y + (at & 1)
        here = {
            dz: tall[pl.ds(24 * at + 8 - dz, ROWS), :] for dz in range(-REACH, REACH + 1)
        }
        acc = {}
        for dx in range(-REACH, REACH + 1):
            for dy in range(-REACH, REACH + 1):
                if dx * dx + dy * dy > REACH_SQ:
                    continue
                k = base + (dx + REACH) * PATCH_Y + dy + REACH
                deep = [
                    dz
                    for dz in range(-REACH, REACH + 1)
                    if dx * dx + dy * dy + dz * dz <= REACH_SQ and (dx, dy, dz) != (0, 0, 0)
                ]
                strength = {dz: jnp.minimum(here[dz], patch[k]) for dz in deep}
                for a in range(3):
                    flat = None
                    if dx:
                        flat = add_scaled(flat, spread[3 * a * ENTRIES + k], dx)
                    if dy:
                        flat = add_scaled(flat, spread[(3 * a + 1) * ENTRIES + k], dy)
                    upright = spread[(3 * a + 2) * ENTRIES + k]
                    for dz in deep:
                        value = add_scaled(flat, upright, dz)
                        acc[a, dz] = plus(acc.get((a, dz)), strength[dz] * value)
        for a in range(3):
            total = result[(9 + a) * SITES + at]
            for dz in range(-REACH, REACH + 1):
                value = acc[a, dz]
                total = total + (pltpu.roll(value, (-dz) % ROWS, 0) if dz else value)
            result[(9 + a) * SITES + at] = total
        return carry

    lax.fori_loop(0, SITES, force_site, 0)

    blocks = nx * ny
    per_group = LANES // blocks
    slot = divide(lane, blocks, per_group + 1)
    block = lane - blocks * slot
    block_x = divide(block, ny, nx)
    block_y = block - ny * block_x
    comps = 12
    for jh in range(2):
        pick = (block_x + 1) * wide + 2 * (block_y + 1) + jh
        for i in range(SIDE):
            for j in range(2):
                for group in range(comps // per_group):
                    merged = None
                    for part in range(per_group):
                        value = lanes_of(result[(group * per_group + part) * SITES + 2 * i + j], pick)
                        merged = value if merged is None else jnp.where(slot == part, value, merged)
                    start = group * LANES + (2 * jh + j) * SIDE + i
                    gathered[pl.ds(start, ROWS, stride=SIDE * SIDE), :] = merged
    for group in range(comps // per_group):
        rows_out[group * LANES : (group + 1) * LANES, :] = gathered[
            group * LANES : (group + 1) * LANES, :
        ].T
    for x in range(nx):
        for y in range(ny):
            at = x * ny + y
            out_grad[x, y, 0:8, :] = rows_out[pl.ds(at, 8, stride=blocks), :]
            out_grad[x, y, 8:9, :] = rows_out[8 * blocks + at : 8 * blocks + at + 1, :]
            for a in range(3):
                source = (9 + a) * blocks + at
                out_force[x, y, a : a + 1, :] = rows_out[source : source + 1, :]


def local(displacement, volume, health, damage, block_pairs):
    nx, ny, points = volume.shape
    ext_y = ny + 2 * RING
    f32 = jnp.float32
    pairs = block_pairs.reshape(block_pairs.shape[2:])
    raw = (displacement, volume, health, damage)
    params = pltpu.CompilerParams(vmem_limit_bytes=48 * 1024 * 1024)
    y_shape = jax.ShapeDtypeStruct((FIELDS * nx * RING + ROWS, points), f32)
    y_to_even, y_to_odd = pl.pallas_call(
        functools.partial(pack_kernel, nx, ny),
        out_shape=(y_shape, y_shape),
        compiler_params=params,
        name="pack",
    )(*raw, pairs)
    even, odd = even_odd(None, "gy")
    y_odd = lax.ppermute(y_to_odd, "gy", odd)
    y_even = lax.ppermute(y_to_even, "gy", even)
    x_shape = jax.ShapeDtypeStruct((FIELDS * RING * ext_y + ROWS, points), f32)
    x_to_even, x_to_odd = pl.pallas_call(
        functools.partial(middle_kernel, nx, ny),
        out_shape=(x_shape, x_shape),
        compiler_params=params,
        name="middle",
    )(*raw, y_to_even, y_even, y_odd)
    even, odd = even_odd(None, "gx")
    x_odd = lax.ppermute(x_to_odd, "gx", odd)
    x_even = lax.ppermute(x_to_even, "gx", even)
    tiles = lambda count: pltpu.VMEM((count, ROWS, LANES), f32)
    rows = lambda count: pltpu.VMEM((count * LANES, LANES), f32)
    return pl.pallas_call(
        functools.partial(main_kernel, nx, ny),
        out_shape=(
            jax.ShapeDtypeStruct((nx, ny, 9, points), f32),
            jax.ShapeDtypeStruct((nx, ny, 3, points), f32),
        ),
        scratch_shapes=[
            rows(FIELDS),
            rows(FIELDS),
            rows(3),
            tiles(5 * ENTRIES),
            pltpu.VMEM((24 * SITES, LANES), f32),
            tiles(4 * SITES),
            tiles(9 * SITES),
            tiles(9 * ENTRIES),
            tiles(12 * SITES),
            rows(3),
            rows(3),
        ],
        compiler_params=params,
        name="main",
    )(*raw, x_to_even, y_even, y_odd, x_even, x_odd)


def solution(mesh):
    in_specs = (
        P("gx", "gy", None, None),
        P("gx", "gy", None),
        P("gx", "gy", None),
        P("gx", "gy", None),
        P("gx", "gy", None, None),
    )
    out_specs = (P("gx", "gy", None, None), P("gx", "gy", None, None))
    return jax.shard_map(local, mesh=mesh, in_specs=in_specs, out_specs=out_specs, check_vma=False)
```

time: 354 us -> 24.3 us (0.07)
  matrix products: 131 us -> 0 us
  local copies, waits for them, and re-layouts: 129 us -> 2.9 us
  other arithmetic: 31 us -> 0 us
  starting transfers between devices: 31.5 us -> 10.1 us
  loops' own time: 21.1 us -> 0 us
  Pallas kernels: 0 us -> 6.77 us
    dot_general x176 -> x0, matrix products: 131 us -> none  [the longest x40 50.9 us: tile_terms(): sums_a = jnp.einsum('gcj,gij->gci', feat_b, weights, precision=highest)]
    gather x123 -> x0, local copies, waits for them, and re-layouts: 70.7 us -> none  [the longest x40 23.4 us: one_group(): map_first, map_second = (flat_map[first_block], flat_map[second_block])]
    ppermute x12 -> x4, starting transfers between devices: 31.5 us -> 10.1 us  [the longest x1 4.39 us: local(): y_even = lax.ppermute(y_to_even, 'gy', even)]
    another operation x4 -> x0, loops' own time: 21.1 us -> none  [the longest x2 17.9 us: pair_sums(): lax.scan(one_group, jnp.zeros((blocks, comp_width * points), jnp.float32)...]
    dynamic_update_slice x16 -> x0, local copies, waits for them, and re-layouts: 17 us -> none  [local(): lax.map(lambda row_pack: block_sums(row_pack, None, 'shape'), point_pack)]
    concatenate x79 -> x0, local copies, waits for them, and re-layouts: 12.1 us -> none  [the longest x48 9.93 us: shape_features(): jnp.concatenate([outer_rr, outer_cr, ref_pos, cur_pos, ones_row], axis=1)]
    mul x612 -> x0, local copies, waits for them, and re-layouts: 8.39 us -> none  [the longest x128 1.45 us: shape_terms(): ref_pos[:, :, None] * sum_r[:, None]]
    add x122 -> x0, other arithmetic: 6.82 us -> none  [the longest x40 3.05 us: positions(): lattice(point_pack.shape[-1])[None]]
  transfers between devices with their start and end apart: 12 -> 4, of which waited for: 2 -> 2; matrix products, arithmetic and copies ran while one was open for 12% -> 0% of each run, Pallas kernels for 0% -> 0%
where the time goes in v1:
time: 24.3 us; the launch traced here: 23.9 us
  starting transfers between devices  10.1 us (42%)
  Pallas kernels  6.77 us (28%)
  waiting for transfers between devices  3.46 us (14%)
  local copies, waits for them, and re-layouts  2.9 us (12%)
  between operations  0.72 us (3%)
    pallas_call x1, Pallas kernels, local(): pl.pallas_call(functools.partial(main_kernel, nx, ny), out_shape=(jax.Sha...  6.27 us
    ppermute x1, starting transfers between devices, local(): y_even = lax.ppermute(y_to_even, 'gy', even)  4.39 us
    ppermute x1, starting transfers between devices, local(): x_even = lax.ppermute(x_to_even, 'gx', even)  4.35 us
    ppermute x1, waiting for transfers between devices, local(): x_even = lax.ppermute(x_to_even, 'gx', even)  2.57 us
    unnamed x10, local copies, waits for them, and re-layouts  1.55 us
    pallas_call x2, local copies, waits for them, and re-layouts, local(): pl.pallas_call(functools.partial(main_kernel, nx, ny), out_shape=(jax.Sha...  1.35 us
    ppermute x1, waiting for transfers between devices, local(): y_even = lax.ppermute(y_to_even, 'gy', even)  0.88 us
    ppermute x1, starting transfers between devices, local(): y_odd = lax.ppermute(y_to_odd, 'gy', odd)  0.66 us
  transfers between devices with their start and end apart: 4, of which 2 were waited for; matrix products, arithmetic and copies ran while one was open for 0% of the time, Pallas kernels for 0%

profile of v1, /device:TPU:0, one launch (start us, length us, event | category | flops | bytes accessed | tf_op | source)
XLA Modules:
  0.0 23.9 jit_solution(14982704354700505833)
XLA Ops:
  0.6 0.0 copy-start.3
  0.6 0.8 %copy.10.disp = f32[8,4,3,128]{3,2,1,0:T(4,128)S(1)} copy(f32[8,4,3,128]{3,1,2,0:T(4,128)} %param.5) | data formatting | bytes 98304 | tf_op args[0]
  1.5 0.0 copy-done.3
  1.5 0.0 copy-start
  1.5 0.0 copy-start.1
  1.5 0.0 copy-start.2
  1.5 0.1 copy.7
  1.6 0.6 %copy-done = f32[8,4,128]{2,1,0:T(4,128)S(1)} copy-done((f32[8,4,128]{2,1,0:T(4,128)S(1)}, f32[8,4,128]{2,1,0:T(4,128)}, u32[]{:S(2)}) %copy-start) | copy-done | bytes 16408
  2.2 0.0 copy-done.1
  2.2 0.0 copy-done.2
  2.2 0.4 %pack.1 = (f32[104,128]{1,0:T(8,128)S(1)}, f32[104,128]{1,0:T(8,128)S(1)}) custom-call(f32[8,4,3,128]{3,2,1,0:T(4,128)S(1)} %copy.10.disp, f32[8,4,128]{2,1,0:T(4,128)S(1)} %copy-done, f32[8,4,128]{2,1,0:T(4,128)S(1)} %copy-done.1, s32[8,4,128]{2,1,0:T(4,128)S(1)} %copy-done.2, s32[162,4]{1,0:T(8,128)S(1)} %bitcast.1), custom_call_target="tpu_custom_call" | custom-call | tf_op jit(solution)/shard_map/pack/pallas_call | solution.py:499
  2.7 0.7 %collective-permute-start.1 = (f32[104,128]{1,0:T(8,128)S(1)}, f32[104,128]{1,0:T(8,128)S(1)}, u32[]{:S(2)}, u32[]{:S(2)}) collective-permute-start(f32[104,128]{1,0:T(8,128)S(1)} %get-tuple-element.7), channel_id=1, source_target_pairs={{1,2},{2,1},{5,6},{6,5},{9,10},{10,9},{13,14},{14,13},{17,18},{18,... | collective-permute-start | bytes 159752 | tf_op jit(solution)/shard_map/ppermute | solution.py:506
  3.3 4.4 %collective-permute-start = (f32[104,128]{1,0:T(8,128)S(1)}, f32[104,128]{1,0:T(8,128)S(1)}, u32[]{:S(2)}, u32[]{:S(2)}) collective-permute-start(f32[104,128]{1,0:T(8,128)S(1)} %get-tuple-element.6.y_mine), channel_id=1, source_target_pairs={{0,1},{1,0},{2,3},{3,2},{4,5},{5,4},{6,7},{7,6},{8,9},{9,8},{10,11... | collective-permute-start | bytes 159752 | tf_op jit(solution)/shard_map/ppermute | solution.py:507
  7.7 0.0 collective-permute-done.1.y_odd
  7.7 0.9 %collective-permute-done.y_even = f32[104,128]{1,0:T(8,128)S(1)} collective-permute-done((f32[104,128]{1,0:T(8,128)S(1)}, f32[104,128]{1,0:T(8,128)S(1)}, u32[]{:S(2)}, u32[]{:S(2)}) %collective-permute-start) | collective-permute-done | bytes 53280 | tf_op jit(solution)/shard_map/ppermute | solution.py:507
  8.6 0.1 middle.1
  8.7 0.7 %collective-permute-start.3 = (f32[104,128]{1,0:T(8,128)S(1)}, f32[104,128]{1,0:T(8,128)S(1)}, u32[]{:S(2)}, u32[]{:S(2)}) collective-permute-start(f32[104,128]{1,0:T(8,128)S(1)} %get-tuple-element.9), channel_id=1, source_target_pairs={{4,8},{8,4},{12,16},{16,12},{20,24},{24,20},{5,9},{9,5},{13,17},{1... | collective-permute-start | bytes 159752 | tf_op jit(solution)/shard_map/ppermute | solution.py:516
  9.4 4.3 %collective-permute-start.2 = (f32[104,128]{1,0:T(8,128)S(1)}, f32[104,128]{1,0:T(8,128)S(1)}, u32[]{:S(2)}, u32[]{:S(2)}) collective-permute-start(f32[104,128]{1,0:T(8,128)S(1)} %get-tuple-element.8.x_mine), channel_id=1, source_target_pairs={{0,4},{4,0},{8,12},{12,8},{16,20},{20,16},{24,28},{28,24},{1,5},{5... | collective-permute-start | bytes 159752 | tf_op jit(solution)/shard_map/ppermute | solution.py:517
  13.7 0.0 collective-permute-done.3.x_odd
  13.7 2.6 %collective-permute-done.2.x_even = f32[104,128]{1,0:T(8,128)S(1)} collective-permute-done((f32[104,128]{1,0:T(8,128)S(1)}, f32[104,128]{1,0:T(8,128)S(1)}, u32[]{:S(2)}, u32[]{:S(2)}) %collective-permute-start.2) | collective-permute-done | bytes 53280 | tf_op jit(solution)/shard_map/ppermute | solution.py:517
  16.3 6.3 %main.1 = (f32[8,4,9,128]{3,2,1,0:T(8,128)S(1)}, f32[8,4,3,128]{3,2,1,0:T(4,128)S(1)}) custom-call(f32[8,4,3,128]{3,2,1,0:T(4,128)S(1)} %copy.10.disp, f32[8,4,128]{2,1,0:T(4,128)S(1)} %copy-done, f32[8,4,128]{2,1,0:T(4,128)S(1)} %copy-done.1, s32[8,4,128]{2,1,0:T(4,128)S(1)} %copy-done.2, f32[104,128]{1,0:T(8,128)S(1)} %get-tuple-element.8.x_mine, ...), custom_call_target="tpu_custom_call" | custom-call | tf_op jit(solution)/shard_map/main/pallas_call | solution.py:520
  22.6 0.7 %copy.11 = f32[8,4,9,128]{3,1,2,0:T(4,128)} copy(f32[8,4,9,128]{3,2,1,0:T(8,128)S(1)} %get-tuple-element.10) | data formatting | bytes 294912 | tf_op jit(solution)/shard_map/main/pallas_call | solution.py:520
  23.3 0.6 %copy.12 = f32[8,4,3,128]{3,1,2,0:T(4,128)} copy(f32[8,4,3,128]{3,2,1,0:T(4,128)S(1)} %get-tuple-element.11) | data formatting | bytes 98304 | tf_op jit(solution)/shard_map/main/pallas_call | solution.py:520
Async XLA Ops:
  0.6 0.8 %copy-start.3 = (s32[1,1,162,4]{2,3,1,0:T(4,128)S(1)}, s32[1,1,162,4]{2,3,1,0:T(4,128)}, u32[]{:S(2)}) copy-start(s32[1,1,162,4]{2,3,1,0:T(4,128)} %param.9) | copy-start | bytes 7780
  1.5 0.7 %copy-start = (f32[8,4,128]{2,1,0:T(4,128)S(1)}, f32[8,4,128]{2,1,0:T(4,128)}, u32[]{:S(2)}) copy-start(f32[8,4,128]{2,1,0:T(4,128)} %vol.5) | copy-start | bytes 49156
  1.5 0.7 %copy-start.1 = (f32[8,4,128]{2,1,0:T(4,128)S(1)}, f32[8,4,128]{2,1,0:T(4,128)}, u32[]{:S(2)}) copy-start(f32[8,4,128]{2,1,0:T(4,128)} %health.5) | copy-start | bytes 49156
  1.5 0.7 %copy-start.2 = (s32[8,4,128]{2,1,0:T(4,128)S(1)}, s32[8,4,128]{2,1,0:T(4,128)}, u32[]{:S(2)}) copy-start(s32[8,4,128]{2,1,0:T(4,128)} %damage.5) | copy-start | bytes 49156
  2.7 5.1 %collective-permute-start.1 = (f32[104,128]{1,0:T(8,128)S(1)}, f32[104,128]{1,0:T(8,128)S(1)}, u32[]{:S(2)}, u32[]{:S(2)}) collective-permute-start(f32[104,128]{1,0:T(8,128)S(1)} %get-tuple-element.7), channel_id=1, source_target_pairs={{1,2},{2,1},{5,6},{6,5},{9,10},{10,9},{13,14},{14,13},{17,18},{18,... | collective-permute-start | bytes 159752 | tf_op jit(solution)/shard_map/ppermute | solution.py:506
  3.3 5.3 %collective-permute-start = (f32[104,128]{1,0:T(8,128)S(1)}, f32[104,128]{1,0:T(8,128)S(1)}, u32[]{:S(2)}, u32[]{:S(2)}) collective-permute-start(f32[104,128]{1,0:T(8,128)S(1)} %get-tuple-element.6.y_mine), channel_id=1, source_target_pairs={{0,1},{1,0},{2,3},{3,2},{4,5},{5,4},{6,7},{7,6},{8,9},{9,8},{10,11... | collective-permute-start | bytes 159752 | tf_op jit(solution)/shard_map/ppermute | solution.py:507
  8.7 5.0 %collective-permute-start.3 = (f32[104,128]{1,0:T(8,128)S(1)}, f32[104,128]{1,0:T(8,128)S(1)}, u32[]{:S(2)}, u32[]{:S(2)}) collective-permute-start(f32[104,128]{1,0:T(8,128)S(1)} %get-tuple-element.9), channel_id=1, source_target_pairs={{4,8},{8,4},{12,16},{16,12},{20,24},{24,20},{5,9},{9,5},{13,17},{1... | collective-permute-start | bytes 159752 | tf_op jit(solution)/shard_map/ppermute | solution.py:516
  9.4 6.9 %collective-permute-start.2 = (f32[104,128]{1,0:T(8,128)S(1)}, f32[104,128]{1,0:T(8,128)S(1)}, u32[]{:S(2)}, u32[]{:S(2)}) collective-permute-start(f32[104,128]{1,0:T(8,128)S(1)} %get-tuple-element.8.x_mine), channel_id=1, source_target_pairs={{0,4},{4,0},{8,12},{12,8},{16,20},{20,16},{24,28},{28,24},{1,5},{5... | collective-permute-start | bytes 159752 | tf_op jit(solution)/shard_map/ppermute | solution.py:517

commit v2 on v1

--- a/solution.py
+++ b/solution.py
@@ -39,7 +39,7 @@
     return jnp.take_along_axis(value, index, axis=1, mode="promise_in_bounds")
 
 
-def even_odd(array, axis):
+def even_odd(axis):
     count = lax.axis_size(axis)
     even = [(i, i ^ 1) for i in range(count) if i ^ 1 < count]
     odd = [(i, ((i + 1) ^ 1) - 1) for i in range(1, count) if ((i + 1) ^ 1) - 1 < count]
@@ -64,76 +64,82 @@
     return (x_at + REACH) * PATCH_Y + y_at + REACH
 
 
-def own_row(raw, field, x, y):
-    disp, vol, health, damage = raw
-    if field < 3:
-        return disp[x, y, field : field + 1, :]
-    if field == VOL:
-        return vol[x, pl.ds(y, 1), :]
-    if field == HEALTH:
-        return health[x, pl.ds(y, 1), :]
-    return damage[x, pl.ds(y, 1), :].astype(jnp.float32)
-
-
-def pack_kernel(nx, ny, disp, vol, health, damage, pairs, to_even, to_odd):
-    raw = (disp, vol, health, damage)
-    odd_here = lax.rem(lax.axis_index("gy"), 2)
+def own_rows(own, nx, ny, field, x, start, count):
+    return own[pl.ds((field * nx + x) * ny + start, count), :]
+
+
+def pack_kernel(nx, ny, disp, vol, health, damage, pairs, own, to_even, to_odd, here, sems):
+    copies = []
+    for k, (source, target) in enumerate(zip((disp, vol, health, damage, pairs), here)):
+        copies.append(pltpu.make_async_copy(source, target, sems.at[k]))
+        copies[-1].start()
+    disp, vol, health, damage, pairs = here
+    odd_here = lax.rem(lax.axis_index("gx"), 2)
     ext_x = nx + 2 * RING
-    slots = pairs.shape[0]
-    ax, ay = pairs[:, 0:1], pairs[:, 1:2]
-    bx, by = pairs[:, 2:3], pairs[:, 3:4]
+    slots = pairs.shape[1]
+    copies[4].wait()
+    ax, ay = pairs[0:1, :], pairs[1:2, :]
+    bx, by = pairs[2:3, :], pairs[3:4, :]
     kind = jnp.where(bx == ax, 1, jnp.where(by == ay, 0, jnp.where(by > ay, 2, 3)))
     code = jnp.where(ax >= 0, kind * ext_x + ax + 1, -1)
-    hit_x = jnp.where(code == iota((slots, LANES), 1), 1.0, 0.0).astype(jnp.bfloat16)
-    hit_y = jnp.where(ay + 1 == iota((slots, LANES), 1), 1.0, 0.0).astype(jnp.bfloat16)
+    hit_x = jnp.where(code == iota((LANES, slots), 0), 1.0, 0.0).astype(jnp.bfloat16)
+    hit_y = jnp.where(ay + 1 == iota((2 * ROWS, slots), 0), 1.0, 0.0).astype(jnp.bfloat16)
     table = lax.dot_general(
-        hit_y, hit_x, (((0,), (0,)), ((), ())), preferred_element_type=jnp.float32
+        hit_y, hit_x, (((1,), (1,)), ((), ())), preferred_element_type=jnp.float32
     )[0:ROWS]
-    for target, start in ((to_even, (1 - odd_here) * (ny - RING)), (to_odd, odd_here * (ny - RING))):
+    for copy in copies[:4]:
+        copy.wait()
+    for x in range(nx):
         for field in range(FIELDS):
-            for x in range(nx):
-                for y in range(RING):
-                    row = (field * nx + x) * RING + y
-                    target[row : row + 1, :] = own_row(raw, field, x, start + y)
-        target[FIELDS * nx * RING :, :] = table
+            if field < 3:
+                value = disp[x, field, :, :]
+            elif field == VOL:
+                value = vol[x, :, :]
+            elif field == HEALTH:
+                value = health[x, :, :]
+            else:
+                value = damage[x, :, :].astype(jnp.float32)
+            row = (field * nx + x) * ny
+            own[row : row + ny, :] = value
+    for target, start in ((to_even, (1 - odd_here) * (nx - RING)), (to_odd, odd_here * (nx - RING))):
+        for field in range(FIELDS):
+            row = field * RING * ny
+            target[row : row + RING * ny, :] = own_rows(own, nx, ny, field, start, 0, RING * ny)
+        target[FIELDS * RING * ny :, :] = table
 
 
 def sides(from_even, from_odd, odd_here):
-    low = jnp.where(odd_here == 1, from_even[...], from_odd[...])
-    high = jnp.where(odd_here == 1, from_odd[...], from_even[...])
+    low = jnp.where(odd_here == 1, from_even, from_odd)
+    high = jnp.where(odd_here == 1, from_odd, from_even)
     return low, high
 
 
-def middle_kernel(nx, ny, disp, vol, health, damage, y_mine, y_even, y_odd, to_even, to_odd):
-    raw = (disp, vol, health, damage)
+def joined(table, low, high, count, axis, at, size):
+    table = table + jnp.where(at >= count, pltpu.roll(high, count, axis), 0.0)
+    return table + jnp.where(at < 2 * RING, pltpu.roll(low, size - count, axis), 0.0)
+
+
+def middle_kernel(nx, ny, own, x_mine, x_even, x_odd, to_even, to_odd):
     odd_x, odd_y = lax.rem(lax.axis_index("gx"), 2), lax.rem(lax.axis_index("gy"), 2)
-    ext_y = ny + 2 * RING
-    halo_rows = FIELDS * nx * RING
-    is_odd = odd_y == 1
-    at_row = iota((ROWS, LANES), 0)
-    table = y_mine[halo_rows:, :]
-    even_table = y_even[halo_rows:, :]
-    odd_table = y_odd[halo_rows:, :]
-    low_table = jnp.where(is_odd, even_table, odd_table)
-    high_table = jnp.where(is_odd, odd_table, even_table)
-    table = table + jnp.where(at_row >= ny, pltpu.roll(high_table, ny, 0), 0.0)
-    table = table + jnp.where(at_row < 2 * RING, pltpu.roll(low_table, ROWS - ny, 0), 0.0)
-    for target, start in ((to_even, (1 - odd_x) * (nx - RING)), (to_odd, odd_x * (nx - RING))):
+    ext_x = nx + 2 * RING
+    side_rows = RING * ny
+    lane = iota((ROWS, LANES), 1)
+    at_e = lane - ext_x * divide(lane, ext_x, LANES // ext_x + 1)
+    low, high = sides(x_even[FIELDS * side_rows :, :], x_odd[FIELDS * side_rows :, :], odd_x)
+    table = joined(x_mine[FIELDS * side_rows :, :], low, high, nx, 1, at_e, LANES)
+    for target, start in ((to_even, (1 - odd_y) * (ny - RING)), (to_odd, odd_y * (ny - RING))):
         for field in range(FIELDS):
             for x in range(RING):
-                base = (field * RING + x) * ext_y
-                for y in range(ny):
-                    target[base + RING + y : base + RING + y + 1, :] = own_row(
-                        raw, field, start + x, y
-                    )
-                for y in range(RING):
-                    halo = pl.ds((field * nx + start + x) * RING + y, 1)
-                    even_row, odd_row = y_even[halo, :], y_odd[halo, :]
-                    at = base + y
-                    target[at : at + 1, :] = jnp.where(is_odd, even_row, odd_row)
-                    at = base + RING + ny + y
-                    target[at : at + 1, :] = jnp.where(is_odd, odd_row, even_row)
-        target[FIELDS * RING * ext_y :, :] = table
+                halo = pl.ds((field * RING + x) * ny + start, RING)
+                low, high = sides(x_even[halo, :], x_odd[halo, :], odd_x)
+                row = (field * ext_x + x) * RING
+                target[row : row + RING, :] = low
+                row += (RING + nx) * RING
+                target[row : row + RING, :] = high
+            for x in range(nx):
+                row = (field * ext_x + RING + x) * RING
+                target[row : row + RING, :] = own_rows(own, nx, ny, field, x, start, RING)
+        target[FIELDS * ext_x * RING :, :] = table
 
 
 def bond_steps(dz):
@@ -231,10 +237,9 @@
 
 
 def main_kernel(
-    nx, ny, disp, vol, health, damage, x_mine, y_even, y_odd, x_even, x_odd, out_grad, out_force,
+    nx, ny, own, y_mine, x_even, x_odd, y_even, y_odd, out_grad, out_force,
     ext, turned, weighted, patch, tall, site, stress, spread, result, gathered, rows_out
 ):
-    raw = (disp, vol, health, damage)
     odd_x, odd_y = lax.rem(lax.axis_index("gx"), 2), lax.rem(lax.axis_index("gy"), 2)
     ext_x, ext_y = nx + 2 * RING, ny + 2 * RING
     ring_y = ny + 2
@@ -247,21 +252,27 @@
     at_y = lax.shift_right_logical(at_half, 1)
     upper = (at_half & 1) == 1
 
-    y_low, y_high = sides(y_even, y_odd, odd_y)
-    x_low, x_high = sides(x_even, x_odd, odd_x)
-    side_rows = RING * ext_y
+    low_x_at, low_y_at = nx * ny, nx * ny + 2 * RING * ny
+    side_x, side_y = RING * ny, ext_x * RING
+    x_low, x_high = sides(x_even[0 : FIELDS * side_x, :], x_odd[0 : FIELDS * side_x, :], odd_x)
+    y_low, y_high = sides(y_even[...], y_odd[...], odd_y)
     for field in range(FIELDS):
         base = field * LANES
-        ext[base : base + side_rows, :] = x_low[field * side_rows : (field + 1) * side_rows]
-        high_at = base + (RING + nx) * ext_y
-        ext[high_at : high_at + side_rows, :] = x_high[field * side_rows : (field + 1) * side_rows]
-        for x in range(nx):
-            at = base + (RING + x) * ext_y
-            halo = (field * nx + x) * RING
-            ext[at : at + RING, :] = y_low[halo : halo + RING]
-            ext[at + RING + ny : at + 2 * RING + ny, :] = y_high[halo : halo + RING]
-            for y in range(ny):
-                ext[at + RING + y : at + RING + y + 1, :] = own_row(raw, field, x, y)
+        ext[base : base + nx * ny, :] = own_rows(own, nx, ny, field, 0, 0, nx * ny)
+        at = base + low_x_at
+        ext[at : at + side_x, :] = x_low[field * side_x : (field + 1) * side_x]
+        ext[at + side_x : at + 2 * side_x, :] = x_high[field * side_x : (field + 1) * side_x]
+        at = base + low_y_at
+        ext[at : at + side_y, :] = y_low[field * side_y : (field + 1) * side_y]
+        ext[at + side_y : at + 2 * side_y, :] = y_high[field * side_y : (field + 1) * side_y]
+
+    def block_row(e, f):
+        own = (e - RING) * ny + f - RING
+        beside = low_x_at + jnp.where(e < RING, e, e - nx) * ny + f - RING
+        above = low_y_at + jnp.where(f < RING, 0, side_y) + e * RING + jnp.where(f < RING, f, f - RING - ny)
+        row = jnp.where((e < RING) | (e >= RING + nx), beside, own)
+        row = jnp.where((f < RING) | (f >= RING + ny), above, row)
+        return jnp.clip(row, 0, LANES - 1)
 
     for field in range(FIELDS):
         turned[field * LANES : (field + 1) * LANES, :] = ext[
@@ -273,13 +284,14 @@
             * turned[VOL * LANES : (VOL + 1) * LANES, :]
         )
 
-    table = x_mine[FIELDS * side_rows :, :]
-    at_e = lane - ext_x * divide(lane, ext_x, LANES // ext_x + 1)
-    table = table + jnp.where(
-        at_e >= nx, pltpu.roll(x_high[FIELDS * side_rows :], nx, 1), 0.0
-    )
-    table = table + jnp.where(
-        at_e < 2 * RING, pltpu.roll(x_low[FIELDS * side_rows :], LANES - nx, 1), 0.0
+    table = joined(
+        y_mine[FIELDS * side_y :, :],
+        y_low[FIELDS * side_y :],
+        y_high[FIELDS * side_y :],
+        ny,
+        0,
+        at_row,
+        ROWS,
     )
     link = {}
     for kind, step in enumerate(KINDS):
@@ -292,7 +304,7 @@
             )
 
     index = {
-        (sx, sy): (at_x + 1 + sx) * ext_y + at_y + 1 + sy for sx in (-1, 0, 1) for sy in (-1, 0, 1)
+        (sx, sy): block_row(at_x + 1 + sx, at_y + 1 + sy) for sx in (-1, 0, 1) for sy in (-1, 0, 1)
     }
 
     def half_blocks(source, field, x_at, y_at):
@@ -479,49 +491,54 @@
             group * LANES : (group + 1) * LANES, :
         ].T
     for x in range(nx):
-        for y in range(ny):
-            at = x * ny + y
-            out_grad[x, y, 0:8, :] = rows_out[pl.ds(at, 8, stride=blocks), :]
-            out_grad[x, y, 8:9, :] = rows_out[8 * blocks + at : 8 * blocks + at + 1, :]
-            for a in range(3):
-                source = (9 + a) * blocks + at
-                out_force[x, y, a : a + 1, :] = rows_out[source : source + 1, :]
+        for comp in range(comps):
+            row = comp * blocks + x * ny
+            value = rows_out[row : row + ny, :]
+            if comp < 9:
+                out_grad[x, comp, :, :] = value
+            else:
+                out_force[x, comp - 9, :, :] = value
 
 
 def local(displacement, volume, health, damage, block_pairs):
     nx, ny, points = volume.shape
-    ext_y = ny + 2 * RING
+    ext_x = nx + 2 * RING
     f32 = jnp.float32
-    pairs = block_pairs.reshape(block_pairs.shape[2:])
-    raw = (displacement, volume, health, damage)
+    pairs = block_pairs.reshape(block_pairs.shape[2:]).T
+    raw = (displacement.transpose(0, 2, 1, 3), volume, health, damage)
     params = pltpu.CompilerParams(vmem_limit_bytes=48 * 1024 * 1024)
-    y_shape = jax.ShapeDtypeStruct((FIELDS * nx * RING + ROWS, points), f32)
+    x_shape = jax.ShapeDtypeStruct((FIELDS * RING * ny + ROWS, points), f32)
+    own, x_to_even, x_to_odd = pl.pallas_call(
+        functools.partial(pack_kernel, nx, ny),
+        out_shape=(jax.ShapeDtypeStruct((FIELDS * nx * ny, points), f32), x_shape, x_shape),
+        in_specs=[pl.BlockSpec(memory_space=pltpu.HBM)] * 5,
+        scratch_shapes=[
+            [pltpu.VMEM(a.shape, a.dtype) for a in (*raw, pairs)],
+            pltpu.SemaphoreType.DMA((5,)),
+        ],
+        compiler_params=params,
+        name="pack",
+    )(*[pltpu.with_memory_space_constraint(a, pltpu.HBM) for a in (*raw, pairs)])
+    even, odd = even_odd("gx")
+    x_odd = lax.ppermute(x_to_odd, "gx", odd)
+    x_even = lax.ppermute(x_to_even, "gx", even)
+    y_shape = jax.ShapeDtypeStruct((FIELDS * ext_x * RING + ROWS, points), f32)
     y_to_even, y_to_odd = pl.pallas_call(
-        functools.partial(pack_kernel, nx, ny),
+        functools.partial(middle_kernel, nx, ny),
         out_shape=(y_shape, y_shape),
         compiler_params=params,
-        name="pack",
-    )(*raw, pairs)
-    even, odd = even_odd(None, "gy")
+        name="middle",
+    )(own, x_to_even, x_even, x_odd)
+    even, odd = even_odd("gy")
     y_odd = lax.ppermute(y_to_odd, "gy", odd)
     y_even = lax.ppermute(y_to_even, "gy", even)
-    x_shape = jax.ShapeDtypeStruct((FIELDS * RING * ext_y + ROWS, points), f32)
-    x_to_even, x_to_odd = pl.pallas_call(
-        functools.partial(middle_kernel, nx, ny),
-        out_shape=(x_shape, x_shape),
-        compiler_params=params,
-        name="middle",
-    )(*raw, y_to_even, y_even, y_odd)
-    even, odd = even_odd(None, "gx")
-    x_odd = lax.ppermute(x_to_odd, "gx", odd)
-    x_even = lax.ppermute(x_to_even, "gx", even)
     tiles = lambda count: pltpu.VMEM((count, ROWS, LANES), f32)
     rows = lambda count: pltpu.VMEM((count * LANES, LANES), f32)
-    return pl.pallas_call(
+    grad, force = pl.pallas_call(
         functools.partial(main_kernel, nx, ny),
         out_shape=(
-            jax.ShapeDtypeStruct((nx, ny, 9, points), f32),
-            jax.ShapeDtypeStruct((nx, ny, 3, points), f32),
+            jax.ShapeDtypeStruct((nx, 9, ny, points), f32),
+            jax.ShapeDtypeStruct((nx, 3, ny, points), f32),
         ),
         scratch_shapes=[
             rows(FIELDS),
@@ -538,7 +555,8 @@
         ],
         compiler_params=params,
         name="main",
-    )(*raw, x_to_even, y_even, y_odd, x_even, x_odd)
+    )(own, y_to_even, x_even, x_odd, y_even, y_odd)
+    return grad.transpose(0, 2, 1, 3), force.transpose(0, 2, 1, 3)
 
 
 def solution(mesh):

time: 24.3 us -> 22.2 us (0.914)
  the two profiles are of different devices: /device:TPU:0 before, /device:TPU:1 now
where the time goes in v2:
time: 22.2 us; the launch traced here: 22 us
  starting transfers between devices  10.2 us (46%)
  Pallas kernels  7.87 us (35%)
  waiting for transfers between devices  3.25 us (15%)
  between operations  0.67 us (3%)
    pallas_call x1, Pallas kernels, local(): pl.pallas_call(functools.partial(main_kernel, nx, ny), out_shape=(jax.Sha...  6.8 us
    ppermute x1, starting transfers between devices, local(): y_odd = lax.ppermute(y_to_odd, 'gy', odd)  4.86 us
    ppermute x1, starting transfers between devices, local(): x_even = lax.ppermute(x_to_even, 'gx', even)  4.62 us
    ppermute x1, waiting for transfers between devices, local(): y_odd = lax.ppermute(y_to_odd, 'gy', odd)  1.99 us
    ppermute x1, waiting for transfers between devices, local(): x_even = lax.ppermute(x_to_even, 'gx', even)  1.26 us
    pallas_call x1, Pallas kernels, local(): pl.pallas_call(functools.partial(pack_kernel, nx, ny), out_shape=(jax.Sha...  0.99 us
    ppermute x1, starting transfers between devices, local(): x_odd = lax.ppermute(x_to_odd, 'gx', odd)  0.66 us
  transfers between devices with their start and end apart: 4, of which 2 were waited for; matrix products, arithmetic and copies ran while one was open for 0% of the time, Pallas kernels for 0%

profile of v2, /device:TPU:1, one launch (start us, length us, event | category | flops | bytes accessed | tf_op | source)
XLA Modules:
  0.0 22.0 jit_solution(2909408294278081141)
XLA Ops:
  0.6 1.0 %pack.1 = (f32[192,128]{1,0:T(8,128)S(1)}, f32[56,128]{1,0:T(8,128)S(1)}, f32[56,128]{1,0:T(8,128)S(1)}) custom-call(f32[8,3,4,128]{3,2,1,0:T(4,128)} %bitcast.6, f32[8,4,128]{2,1,0:T(4,128)} %vol.1, f32[8,4,128]{2,1,0:T(4,128)} %health.1, s32[8,4,128]{2,1,0:T(4,128)} %damage.1, s32[4,162]{1,0:T(4,128)} %bitcast.7), custom_call_target="tpu_custom_call" | custom-call | tf_op jit(solution)/shard_map/pack/pallas_call | solution.py:511
  1.6 0.7 %collective-permute-start.1 = (f32[56,128]{1,0:T(8,128)S(1)}, f32[56,128]{1,0:T(8,128)S(1)}, u32[]{:S(2)}, u32[]{:S(2)}) collective-permute-start(f32[56,128]{1,0:T(8,128)S(1)} %get-tuple-element.11), channel_id=1, source_target_pairs={{4,8},{8,4},{12,16},{16,12},{20,24},{24,20},{5,9},{9,5},{13,17},{1... | collective-permute-start | bytes 86024 | tf_op jit(solution)/shard_map/ppermute | solution.py:523
  2.3 4.6 %collective-permute-start = (f32[56,128]{1,0:T(8,128)S(1)}, f32[56,128]{1,0:T(8,128)S(1)}, u32[]{:S(2)}, u32[]{:S(2)}) collective-permute-start(f32[56,128]{1,0:T(8,128)S(1)} %get-tuple-element.10.x_mine), channel_id=1, source_target_pairs={{0,4},{4,0},{8,12},{12,8},{16,20},{20,16},{24,28},{28,24},{1,5},{5... | collective-permute-start | bytes 86024 | tf_op jit(solution)/shard_map/ppermute | solution.py:524
  6.9 0.0 collective-permute-done.1.x_odd
  6.9 1.3 %collective-permute-done.x_even = f32[56,128]{1,0:T(8,128)S(1)} collective-permute-done((f32[56,128]{1,0:T(8,128)S(1)}, f32[56,128]{1,0:T(8,128)S(1)}, u32[]{:S(2)}, u32[]{:S(2)}) %collective-permute-start) | collective-permute-done | bytes 28704 | tf_op jit(solution)/shard_map/ppermute | solution.py:524
  8.2 0.1 middle.1
  8.3 4.9 %collective-permute-start.3 = (f32[152,128]{1,0:T(8,128)S(1)}, f32[152,128]{1,0:T(8,128)S(1)}, u32[]{:S(2)}, u32[]{:S(2)}) collective-permute-start(f32[152,128]{1,0:T(8,128)S(1)} %get-tuple-element.13), channel_id=1, source_target_pairs={{1,2},{2,1},{5,6},{6,5},{9,10},{10,9},{13,14},{14,13},{17,18},{18,... | collective-permute-start | bytes 233480 | tf_op jit(solution)/shard_map/ppermute | solution.py:533
  13.1 0.1 collective-permute-start.2
  13.2 2.0 %collective-permute-done.3.y_odd = f32[152,128]{1,0:T(8,128)S(1)} collective-permute-done((f32[152,128]{1,0:T(8,128)S(1)}, f32[152,128]{1,0:T(8,128)S(1)}, u32[]{:S(2)}, u32[]{:S(2)}) %collective-permute-start.3) | collective-permute-done | bytes 77856 | tf_op jit(solution)/shard_map/ppermute | solution.py:533
  15.2 0.0 collective-permute-done.2.y_even
  15.2 6.8 %main.1 = (f32[8,9,4,128]{3,2,1,0:T(4,128)}, f32[8,3,4,128]{3,2,1,0:T(4,128)}) custom-call(f32[192,128]{1,0:T(8,128)S(1)} %get-tuple-element.9.own, f32[152,128]{1,0:T(8,128)S(1)} %get-tuple-element.12.y_mine, f32[56,128]{1,0:T(8,128)S(1)} %collective-permute-done.x_even, f32[56,128]{1,0:T(8,128)S(1)} %collective-permute-done.1.x_odd, ...), custom_call_target="tpu_custom_call" | custom-call | tf_op jit(solution)/shard_map/main/pallas_call | solution.py:537
Async XLA Ops:
  1.6 5.3 %collective-permute-start.1 = (f32[56,128]{1,0:T(8,128)S(1)}, f32[56,128]{1,0:T(8,128)S(1)}, u32[]{:S(2)}, u32[]{:S(2)}) collective-permute-start(f32[56,128]{1,0:T(8,128)S(1)} %get-tuple-element.11), channel_id=1, source_target_pairs={{4,8},{8,4},{12,16},{16,12},{20,24},{24,20},{5,9},{9,5},{13,17},{1... | collective-permute-start | bytes 86024 | tf_op jit(solution)/shard_map/ppermute | solution.py:523
  2.3 5.9 %collective-permute-start = (f32[56,128]{1,0:T(8,128)S(1)}, f32[56,128]{1,0:T(8,128)S(1)}, u32[]{:S(2)}, u32[]{:S(2)}) collective-permute-start(f32[56,128]{1,0:T(8,128)S(1)} %get-tuple-element.10.x_mine), channel_id=1, source_target_pairs={{0,4},{4,0},{8,12},{12,8},{16,20},{20,16},{24,28},{28,24},{1,5},{5... | collective-permute-start | bytes 86024 | tf_op jit(solution)/shard_map/ppermute | solution.py:524
  8.3 6.9 %collective-permute-start.3 = (f32[152,128]{1,0:T(8,128)S(1)}, f32[152,128]{1,0:T(8,128)S(1)}, u32[]{:S(2)}, u32[]{:S(2)}) collective-permute-start(f32[152,128]{1,0:T(8,128)S(1)} %get-tuple-element.13), channel_id=1, source_target_pairs={{1,2},{2,1},{5,6},{6,5},{9,10},{10,9},{13,14},{14,13},{17,18},{18,... | collective-permute-start | bytes 233480 | tf_op jit(solution)/shard_map/ppermute | solution.py:533
  13.1 2.1 %collective-permute-start.2 = (f32[152,128]{1,0:T(8,128)S(1)}, f32[152,128]{1,0:T(8,128)S(1)}, u32[]{:S(2)}, u32[]{:S(2)}) collective-permute-start(f32[152,128]{1,0:T(8,128)S(1)} %get-tuple-element.12.y_mine), channel_id=1, source_target_pairs={{0,1},{1,0},{2,3},{3,2},{4,5},{5,4},{6,7},{7,6},{8,9},{9,8},{10,11... | collective-permute-start | bytes 233480 | tf_op jit(solution)/shard_map/ppermute | solution.py:534

commit v3 on v2

--- a/solution.py
+++ b/solution.py
@@ -39,11 +39,34 @@
     return jnp.take_along_axis(value, index, axis=1, mode="promise_in_bounds")
 
 
-def even_odd(axis):
-    count = lax.axis_size(axis)
-    even = [(i, i ^ 1) for i in range(count) if i ^ 1 < count]
-    odd = [(i, ((i + 1) ^ 1) - 1) for i in range(1, count) if ((i + 1) ^ 1) - 1 < count]
-    return even, odd
+def partner(index, count, odd):
+    other = ((index + 1) ^ 1) - 1 if odd else index ^ 1
+    return other if 0 <= other < count else None
+
+
+def swap(array, axis, odd):
+    nx, ny = lax.axis_size("gx"), lax.axis_size("gy")
+    to, left = {}, []
+    for i in range(nx):
+        for j in range(ny):
+            if axis == "gx":
+                other = (partner(i, nx, odd), j)
+            else:
+                other = (i, partner(j, ny, odd))
+            if None in other:
+                left.append((i, j))
+            else:
+                to[i, j] = other
+    while left:
+        one = left.pop(0)
+        if not left:
+            to[one] = one
+            break
+        other = min(left, key=lambda at: (abs(at[0] - one[0]) + abs(at[1] - one[1]), -at[0] - at[1]))
+        left.remove(other)
+        to[one], to[other] = other, one
+    pairs = [(i * ny + j, k * ny + l) for (i, j), (k, l) in sorted(to.items())]
+    return lax.ppermute(array, ("gx", "gy"), pairs)
 
 
 def entry_used(x_at, y_at):
@@ -108,10 +131,13 @@
         target[FIELDS * RING * ny :, :] = table
 
 
-def sides(from_even, from_odd, odd_here):
-    low = jnp.where(odd_here == 1, from_even, from_odd)
-    high = jnp.where(odd_here == 1, from_odd, from_even)
-    return low, high
+def sides(from_even, from_odd, axis):
+    here = lax.axis_index(axis)
+    odd_here = lax.rem(here, 2) == 1
+    low = jnp.where(odd_here, from_even, from_odd)
+    high = jnp.where(odd_here, from_odd, from_even)
+    low = jnp.where(here == 0, 0.0, low)
+    return low, jnp.where(here == lax.axis_size(axis) - 1, 0.0, high)
 
 
 def joined(table, low, high, count, axis, at, size):
@@ -120,18 +146,18 @@
 
 
 def middle_kernel(nx, ny, own, x_mine, x_even, x_odd, to_even, to_odd):
-    odd_x, odd_y = lax.rem(lax.axis_index("gx"), 2), lax.rem(lax.axis_index("gy"), 2)
+    odd_y = lax.rem(lax.axis_index("gy"), 2)
     ext_x = nx + 2 * RING
     side_rows = RING * ny
     lane = iota((ROWS, LANES), 1)
     at_e = lane - ext_x * divide(lane, ext_x, LANES // ext_x + 1)
-    low, high = sides(x_even[FIELDS * side_rows :, :], x_odd[FIELDS * side_rows :, :], odd_x)
+    low, high = sides(x_even[FIELDS * side_rows :, :], x_odd[FIELDS * side_rows :, :], "gx")
     table = joined(x_mine[FIELDS * side_rows :, :], low, high, nx, 1, at_e, LANES)
     for target, start in ((to_even, (1 - odd_y) * (ny - RING)), (to_odd, odd_y * (ny - RING))):
         for field in range(FIELDS):
             for x in range(RING):
                 halo = pl.ds((field * RING + x) * ny + start, RING)
-                low, high = sides(x_even[halo, :], x_odd[halo, :], odd_x)
+                low, high = sides(x_even[halo, :], x_odd[halo, :], "gx")
                 row = (field * ext_x + x) * RING
                 target[row : row + RING, :] = low
                 row += (RING + nx) * RING
@@ -240,7 +266,6 @@
     nx, ny, own, y_mine, x_even, x_odd, y_even, y_odd, out_grad, out_force,
     ext, turned, weighted, patch, tall, site, stress, spread, result, gathered, rows_out
 ):
-    odd_x, odd_y = lax.rem(lax.axis_index("gx"), 2), lax.rem(lax.axis_index("gy"), 2)
     ext_x, ext_y = nx + 2 * RING, ny + 2 * RING
     ring_y = ny + 2
     wide = 2 * ring_y
@@ -254,8 +279,8 @@
 
     low_x_at, low_y_at = nx * ny, nx * ny + 2 * RING * ny
     side_x, side_y = RING * ny, ext_x * RING
-    x_low, x_high = sides(x_even[0 : FIELDS * side_x, :], x_odd[0 : FIELDS * side_x, :], odd_x)
-    y_low, y_high = sides(y_even[...], y_odd[...], odd_y)
+    x_low, x_high = sides(x_even[0 : FIELDS * side_x, :], x_odd[0 : FIELDS * side_x, :], "gx")
+    y_low, y_high = sides(y_even[...], y_odd[...], "gy")
     for field in range(FIELDS):
         base = field * LANES
         ext[base : base + nx * ny, :] = own_rows(own, nx, ny, field, 0, 0, nx * ny)
@@ -519,9 +544,8 @@
         compiler_params=params,
         name="pack",
     )(*[pltpu.with_memory_space_constraint(a, pltpu.HBM) for a in (*raw, pairs)])
-    even, odd = even_odd("gx")
-    x_odd = lax.ppermute(x_to_odd, "gx", odd)
-    x_even = lax.ppermute(x_to_even, "gx", even)
+    x_odd = swap(x_to_odd, "gx", True)
+    x_even = swap(x_to_even, "gx", False)
     y_shape = jax.ShapeDtypeStruct((FIELDS * ext_x * RING + ROWS, points), f32)
     y_to_even, y_to_odd = pl.pallas_call(
         functools.partial(middle_kernel, nx, ny),
@@ -529,9 +553,8 @@
         compiler_params=params,
         name="middle",
     )(own, x_to_even, x_even, x_odd)
-    even, odd = even_odd("gy")
-    y_odd = lax.ppermute(y_to_odd, "gy", odd)
-    y_even = lax.ppermute(y_to_even, "gy", even)
+    y_odd = swap(y_to_odd, "gy", True)
+    y_even = swap(y_to_even, "gy", False)
     tiles = lambda count: pltpu.VMEM((count, ROWS, LANES), f32)
     rows = lambda count: pltpu.VMEM((count * LANES, LANES), f32)
     grad, force = pl.pallas_call(

time: 22.2 us -> 19.5 us (0.88)
  the two profiles are of different devices: /device:TPU:1 before, /device:TPU:0 now
where the time goes in v3:
time: 19.5 us; the launch traced here: 19.4 us
  Pallas kernels  7.87 us (40%)
  starting transfers between devices  6.64 us (34%)
  waiting for transfers between devices  4.22 us (22%)
  between operations  0.64 us (3%)
    pallas_call x1, Pallas kernels, local(): pl.pallas_call(functools.partial(main_kernel, nx, ny), out_shape=(jax.Sha...  6.8 us
    ppermute x4, starting transfers between devices, swap(): return lax.ppermute(array, ('gx', 'gy'), pairs)  6.64 us
    ppermute x4, waiting for transfers between devices, swap(): return lax.ppermute(array, ('gx', 'gy'), pairs)  4.22 us
    pallas_call x1, Pallas kernels, local(): pl.pallas_call(functools.partial(pack_kernel, nx, ny), out_shape=(jax.Sha...  0.99 us
  transfers between devices with their start and end apart: 4, of which 2 were waited for; matrix products, arithmetic and copies ran while one was open for 0% of the time, Pallas kernels for 0%

profile of v3, /device:TPU:0, one launch (start us, length us, event | category | flops | bytes accessed | tf_op | source)
XLA Modules:
  0.0 19.4 jit_solution(10718842591316166918)
XLA Ops:
  0.6 1.0 %pack.1 = (f32[192,128]{1,0:T(8,128)S(1)}, f32[56,128]{1,0:T(8,128)S(1)}, f32[56,128]{1,0:T(8,128)S(1)}) custom-call(f32[8,3,4,128]{3,2,1,0:T(4,128)} %bitcast.6, f32[8,4,128]{2,1,0:T(4,128)} %vol.1, f32[8,4,128]{2,1,0:T(4,128)} %health.1, s32[8,4,128]{2,1,0:T(4,128)} %damage.1, s32[4,162]{1,0:T(4,128)} %bitcast.7), custom_call_target="tpu_custom_call" | custom-call | tf_op jit(solution)/shard_map/pack/pallas_call | solution.py:536
  1.6 0.5 %collective-permute-start.1 = (f32[56,128]{1,0:T(8,128)S(1)}, f32[56,128]{1,0:T(8,128)S(1)}, u32[]{:S(2)}, u32[]{:S(2)}) collective-permute-start(f32[56,128]{1,0:T(8,128)S(1)} %get-tuple-element.11), channel_id=1, source_target_pairs={{0,1},{1,0},{2,3},{3,2},{4,8},{5,9},{6,10},{7,11},{8,4},{9,5},{10,... | collective-permute-start | bytes 86024 | tf_op jit(solution)/shard_map/ppermute | solution.py:69
  2.1 4.0 %collective-permute-start = (f32[56,128]{1,0:T(8,128)S(1)}, f32[56,128]{1,0:T(8,128)S(1)}, u32[]{:S(2)}, u32[]{:S(2)}) collective-permute-start(f32[56,128]{1,0:T(8,128)S(1)} %get-tuple-element.10.x_mine), channel_id=1, source_target_pairs={{0,4},{1,5},{2,6},{3,7},{4,0},{5,1},{6,2},{7,3},{8,12},{9,13},{10,... | collective-permute-start | bytes 86024 | tf_op jit(solution)/shard_map/ppermute | solution.py:69
  6.2 0.0 collective-permute-done.1.x_odd
  6.2 1.8 %collective-permute-done.x_even = f32[56,128]{1,0:T(8,128)S(1)} collective-permute-done((f32[56,128]{1,0:T(8,128)S(1)}, f32[56,128]{1,0:T(8,128)S(1)}, u32[]{:S(2)}, u32[]{:S(2)}) %collective-permute-start) | collective-permute-done | bytes 28704 | tf_op jit(solution)/shard_map/ppermute | solution.py:69
  8.0 0.1 middle.1
  8.1 2.1 %collective-permute-start.3 = (f32[152,128]{1,0:T(8,128)S(1)}, f32[152,128]{1,0:T(8,128)S(1)}, u32[]{:S(2)}, u32[]{:S(2)}) collective-permute-start(f32[152,128]{1,0:T(8,128)S(1)} %get-tuple-element.13), channel_id=1, source_target_pairs={{0,4},{1,2},{2,1},{3,7},{4,0},{5,6},{6,5},{7,3},{8,12},{9,10},{10,... | collective-permute-start | bytes 233480 | tf_op jit(solution)/shard_map/ppermute | solution.py:69
  10.2 0.0 collective-permute-start.2
  10.2 2.4 %collective-permute-done.3.y_odd = f32[152,128]{1,0:T(8,128)S(1)} collective-permute-done((f32[152,128]{1,0:T(8,128)S(1)}, f32[152,128]{1,0:T(8,128)S(1)}, u32[]{:S(2)}, u32[]{:S(2)}) %collective-permute-start.3) | collective-permute-done | bytes 77856 | tf_op jit(solution)/shard_map/ppermute | solution.py:69
  12.6 0.0 collective-permute-done.2.y_even
  12.6 6.8 %main.1 = (f32[8,9,4,128]{3,2,1,0:T(4,128)}, f32[8,3,4,128]{3,2,1,0:T(4,128)}) custom-call(f32[192,128]{1,0:T(8,128)S(1)} %get-tuple-element.9.own, f32[152,128]{1,0:T(8,128)S(1)} %get-tuple-element.12.y_mine, f32[56,128]{1,0:T(8,128)S(1)} %collective-permute-done.x_even, f32[56,128]{1,0:T(8,128)S(1)} %collective-permute-done.1.x_odd, ...), custom_call_target="tpu_custom_call" | custom-call | tf_op jit(solution)/shard_map/main/pallas_call | solution.py:560
Async XLA Ops:
  1.6 4.6 %collective-permute-start.1 = (f32[56,128]{1,0:T(8,128)S(1)}, f32[56,128]{1,0:T(8,128)S(1)}, u32[]{:S(2)}, u32[]{:S(2)}) collective-permute-start(f32[56,128]{1,0:T(8,128)S(1)} %get-tuple-element.11), channel_id=1, source_target_pairs={{0,1},{1,0},{2,3},{3,2},{4,8},{5,9},{6,10},{7,11},{8,4},{9,5},{10,... | collective-permute-start | bytes 86024 | tf_op jit(solution)/shard_map/ppermute | solution.py:69
  2.1 5.9 %collective-permute-start = (f32[56,128]{1,0:T(8,128)S(1)}, f32[56,128]{1,0:T(8,128)S(1)}, u32[]{:S(2)}, u32[]{:S(2)}) collective-permute-start(f32[56,128]{1,0:T(8,128)S(1)} %get-tuple-element.10.x_mine), channel_id=1, source_target_pairs={{0,4},{1,5},{2,6},{3,7},{4,0},{5,1},{6,2},{7,3},{8,12},{9,13},{10,... | collective-permute-start | bytes 86024 | tf_op jit(solution)/shard_map/ppermute | solution.py:69
  8.1 4.5 %collective-permute-start.3 = (f32[152,128]{1,0:T(8,128)S(1)}, f32[152,128]{1,0:T(8,128)S(1)}, u32[]{:S(2)}, u32[]{:S(2)}) collective-permute-start(f32[152,128]{1,0:T(8,128)S(1)} %get-tuple-element.13), channel_id=1, source_target_pairs={{0,4},{1,2},{2,1},{3,7},{4,0},{5,6},{6,5},{7,3},{8,12},{9,10},{10,... | collective-permute-start | bytes 233480 | tf_op jit(solution)/shard_map/ppermute | solution.py:69
  10.2 2.4 %collective-permute-start.2 = (f32[152,128]{1,0:T(8,128)S(1)}, f32[152,128]{1,0:T(8,128)S(1)}, u32[]{:S(2)}, u32[]{:S(2)}) collective-permute-start(f32[152,128]{1,0:T(8,128)S(1)} %get-tuple-element.12.y_mine), channel_id=1, source_target_pairs={{0,1},{1,0},{2,3},{3,2},{4,5},{5,4},{6,7},{7,6},{8,9},{9,8},{10,11... | collective-permute-start | bytes 233480 | tf_op jit(solution)/shard_map/ppermute | solution.py:69

commit v4 on v3

--- a/solution.py
+++ b/solution.py
@@ -22,6 +22,9 @@
 PATCH_X = SIDE + 2 * REACH
 PATCH_Y = 2 + 2 * REACH
 ENTRIES = PATCH_X * PATCH_Y
+QUARTERS = PATCH_Y * PATCH_Y
+COLUMN_ORDER = (0, 2, 1, 3)
+CHUNK = 2
 
 
 def iota(shape, dim):
@@ -37,6 +40,18 @@
 
 def lanes_of(value, index):
     return jnp.take_along_axis(value, index, axis=1, mode="promise_in_bounds")
+
+
+def pieces(value):
+    high = value.astype(jnp.bfloat16)
+    low = (value - high.astype(jnp.float32)).astype(jnp.bfloat16)
+    return jnp.concatenate([high, low], axis=0)
+
+
+def moved(halves, moves):
+    both = jnp.dot(halves, moves, preferred_element_type=jnp.float32)
+    rows = halves.shape[0] // 2
+    return both[0:rows] + both[rows:]
 
 
 def partner(index, count, odd):
@@ -69,18 +84,90 @@
     return lax.ppermute(array, ("gx", "gy"), pairs)
 
 
-def entry_used(x_at, y_at):
-    return any(
-        (x_at - i) ** 2 + (y_at - j) ** 2 <= REACH_SQ for i in range(SIDE) for j in range(2)
-    )
-
-
-ENTRY_LIST = [
-    (x_at, y_at)
-    for x_at in range(-REACH, SIDE + REACH)
-    for y_at in range(-REACH, 2 + REACH)
-    if entry_used(x_at, y_at)
-]
+def entry_list(wide, high):
+    return [
+        (x_at, y_at)
+        for x_at in range(-REACH, wide + REACH)
+        for y_at in range(-REACH, high + REACH)
+        if any(
+            (x_at - i) ** 2 + (y_at - j) ** 2 <= REACH_SQ for i in range(wide) for j in range(high)
+        )
+    ]
+
+
+ENTRY_LIST = entry_list(SIDE, 2)
+QUARTER_LIST = entry_list(2, 2)
+
+
+SIDE_MOVES = [(0, -3)] + [(sx, y_at) for sx in (0, -1, 1) for y_at in (-2, 0, 2)] + [(0, 4)]
+QUARTER_MOVES = [(x_at, half) for x_at in (-2, 0, 2) for half in (-1, 0, 1)]
+QUARTER_MOVES += [(0, -2), (0, 2), (-3, 0), (4, 0)]
+
+
+def lane_places(nx, ny):
+    lane = iota((ROWS, LANES), 1)
+    wide = 2 * (ny + 2)
+    at_x = divide(lane, wide, nx + 4)
+    at_half = lane - wide * at_x
+    return lane, wide, at_x, lax.shift_right_logical(at_half, 1), (at_half & 1) == 1
+
+
+def output_places(nx, ny):
+    lane = iota((ROWS, LANES), 1)
+    blocks = nx * ny
+    slot = divide(lane, blocks, LANES // blocks + 1)
+    block = lane - blocks * slot
+    block_x = divide(block, ny, nx)
+    return slot, block_x, block - ny * block_x
+
+
+def moves_kernel(nx, ny, after, side_moves, quarter_moves, grad_moves, force_moves):
+    lane, wide, at_x, at_y, upper = lane_places(nx, ny)
+    ext_x = nx + 2 * RING
+    low_x_at, low_y_at = nx * ny, nx * ny + 2 * RING * ny
+    side_y = ext_x * RING
+    rows = iota((2 * ROWS, LANES), 0)
+
+    def block_row(e, f):
+        own = (e - RING) * ny + f - RING
+        beside = low_x_at + jnp.where(e < RING, e, e - nx) * ny + f - RING
+        above = low_y_at + jnp.where(f < RING, 0, side_y) + e * RING
+        above = above + jnp.where(f < RING, f, f - RING - ny)
+        row = jnp.where((e < RING) | (e >= RING + nx), beside, own)
+        return jnp.where((f < RING) | (f >= RING + ny), above, row)
+
+    def fill(target, column, source):
+        source = jnp.concatenate([source, source], axis=0)
+        for row in range(0, target.shape[0], 2 * ROWS):
+            hit = jnp.where(source == rows + row, 1.0, 0.0).astype(jnp.bfloat16)
+            target[row : row + 2 * ROWS, column * LANES : (column + 1) * LANES] = hit
+
+    for column, (sx, y_at) in enumerate(SIDE_MOVES):
+        sources = []
+        for at in (y_at, y_at + 2):
+            part = (at % SIDE - y_at % 2) // 2
+            sources.append(part * LANES + block_row(at_x + 1 + sx, at_y + 1 + at // SIDE))
+        source = jnp.where(upper, sources[1], sources[0])
+        fill(side_moves, column, jnp.where(at_x < nx + 2, source, -1))
+
+    quarter_x = divide(lane, 2 * ny, 2 * nx)
+    quarter_y = lane - 2 * ny * quarter_x
+    right = (quarter_x & 1) == 1
+    owner = (lax.shift_right_logical(quarter_x, 1) + 1) * wide + quarter_y + 2
+    for column, (x_at, half) in enumerate(QUARTER_MOVES):
+        sources = []
+        for at in (x_at, x_at + 2):
+            part = (at % SIDE - x_at % 2) // 2
+            sources.append(part * LANES + owner + (wide * (at // SIDE) + half))
+        fill(quarter_moves, column, jnp.where(right, sources[1], sources[0]))
+
+    slot, block_x, block_y = output_places(nx, ny)
+    for jh in range(2):
+        fill(grad_moves, jh, slot * LANES + (block_x + 1) * wide + 2 * (block_y + 1) + jh)
+    for ih in range(2):
+        for jh in range(2):
+            source = slot * LANES + (2 * block_x + ih) * 2 * ny + 2 * block_y + jh
+            fill(force_moves, 2 * ih + jh, jnp.where(slot < 3, source, -1))
 
 
 def entry_index(x_at, y_at):
@@ -263,19 +350,14 @@
 
 
 def main_kernel(
-    nx, ny, own, y_mine, x_even, x_odd, y_even, y_odd, out_grad, out_force,
-    ext, turned, weighted, patch, tall, site, stress, spread, result, gathered, rows_out
+    nx, ny, own, y_mine, x_even, x_odd, y_even, y_odd, side_moves, quarter_moves, grad_moves,
+    force_moves, out_grad, out_force, ext, turned, weighted, patch, tall, site, stress, spread,
+    spread_health, tall_quarter, start_force, result, gathered, rows_out, hold_grad, hold_force, sems
 ):
     ext_x, ext_y = nx + 2 * RING, ny + 2 * RING
-    ring_y = ny + 2
-    wide = 2 * ring_y
     tile = (ROWS, LANES)
-    lane = iota(tile, 1)
     at_row = iota(tile, 0)
-    at_x = divide(lane, wide, nx + 4)
-    at_half = lane - wide * at_x
-    at_y = lax.shift_right_logical(at_half, 1)
-    upper = (at_half & 1) == 1
+    lane, wide, at_x, at_y, upper = lane_places(nx, ny)
 
     low_x_at, low_y_at = nx * ny, nx * ny + 2 * RING * ny
     side_x, side_y = RING * ny, ext_x * RING
@@ -290,14 +372,9 @@
         at = base + low_y_at
         ext[at : at + side_y, :] = y_low[field * side_y : (field + 1) * side_y]
         ext[at + side_y : at + 2 * side_y, :] = y_high[field * side_y : (field + 1) * side_y]
-
-    def block_row(e, f):
-        own = (e - RING) * ny + f - RING
-        beside = low_x_at + jnp.where(e < RING, e, e - nx) * ny + f - RING
-        above = low_y_at + jnp.where(f < RING, 0, side_y) + e * RING + jnp.where(f < RING, f, f - RING - ny)
-        row = jnp.where((e < RING) | (e >= RING + nx), beside, own)
-        row = jnp.where((f < RING) | (f >= RING + ny), above, row)
-        return jnp.clip(row, 0, LANES - 1)
+        at += 2 * side_y
+        if at < base + LANES:
+            ext[at : base + LANES, :] = jnp.zeros((base + LANES - at, LANES), jnp.float32)
 
     for field in range(FIELDS):
         turned[field * LANES : (field + 1) * LANES, :] = ext[
@@ -328,101 +405,142 @@
                 jnp.sum(picked, axis=0, keepdims=True), tile
             )
 
-    index = {
-        (sx, sy): block_row(at_x + 1 + sx, at_y + 1 + sy) for sx in (-1, 0, 1) for sy in (-1, 0, 1)
-    }
-
-    def half_blocks(source, field, x_at, y_at):
-        sx, sy0, sy1 = x_at // SIDE, y_at // SIDE, (y_at + 2) // SIDE
-        i, j0, j1 = x_at % SIDE, y_at % SIDE, (y_at + 2) % SIDE
-        first = source[pl.ds(field * LANES + SIDE * j0 + i, ROWS, stride=SIDE * SIDE), :]
-        second = source[pl.ds(field * LANES + SIDE * j1 + i, ROWS, stride=SIDE * SIDE), :]
-        return jnp.where(
-            upper, lanes_of(second, index[sx, sy1]), lanes_of(first, index[sx, sy0])
+    masks = {}
+
+    def mask_of(sx, sy0, sy1):
+        if (sx, sy0, sy1) not in masks:
+            one = jnp.ones(tile, jnp.float32)
+            masks[sx, sy0, sy1] = jnp.where(
+                upper, link.get((sx, sy1), one), link.get((sx, sy0), one)
+            )
+        return masks[sx, sy0, sy1]
+
+    def points(source, field, i, odd):
+        start = field * LANES + SIDE * odd + i
+        near = source[pl.ds(start, ROWS, stride=SIDE * SIDE), :]
+        far = source[pl.ds(start + 2 * SIDE, ROWS, stride=SIDE * SIDE), :]
+        return jnp.concatenate([near, far], axis=1)
+
+    def columns(moves, first, count):
+        return moves[:, first * LANES : (first + count) * LANES]
+
+    moving = ((turned, HEALTH), (turned, VOL), (weighted, 0), (weighted, 1), (weighted, 2))
+    parts = pieces(
+        jnp.concatenate(
+            [
+                points(source, field, i, odd)
+                for odd in range(2)
+                for i in range(SIDE)
+                for source, field in moving
+            ],
+            axis=0,
         )
-
-    masks = {}
-    for x_at, y_at in ENTRY_LIST:
-        sx, sy0, sy1 = x_at // SIDE, y_at // SIDE, (y_at + 2) // SIDE
-        at = entry_index(x_at, y_at)
-        strength = half_blocks(turned, HEALTH, x_at, y_at)
-        if (sx, sy0, sy1) != (0, 0, 0):
-            if (sx, sy0, sy1) not in masks:
-                one = jnp.ones(tile, jnp.float32)
-                masks[sx, sy0, sy1] = jnp.where(
-                    upper, link.get((sx, sy1), one), link.get((sx, sy0), one)
-                )
-            strength = strength * masks[sx, sy0, sy1]
-        patch[at] = strength
-        patch[ENTRIES + at] = half_blocks(turned, VOL, x_at, y_at)
-        for comp in range(3):
-            patch[(2 + comp) * ENTRIES + at] = half_blocks(weighted, comp, x_at, y_at)
+    )
+
+    def keep(values, step, sx, y_even):
+        row = 0
+        for odd in range(2):
+            y_at = y_even + odd
+            for i in range(SIDE):
+                x_at = i + SIDE * sx
+                for field in range(len(moving)):
+                    if (x_at, y_at) in ENTRY_LIST:
+                        value = values[row : row + ROWS, step * LANES : (step + 1) * LANES]
+                        links = (sx, y_at // SIDE, (y_at + 2) // SIDE)
+                        if field == 0 and links != (0, 0, 0):
+                            value = value * mask_of(*links)
+                        patch[field * ENTRIES + entry_index(x_at, y_at)] = value
+                    row += ROWS
+
+    for first in range(0, len(SIDE_MOVES), CHUNK):
+        chosen = SIDE_MOVES[first : first + CHUNK]
+        values = moved(parts, columns(side_moves, first, len(chosen)))
+        for step, (sx, y_at) in enumerate(chosen):
+            keep(values, step, sx, y_at - y_at % 2)
+
+    fixed = [0, 1, 2, DAMAGE]
+    values = moved(
+        pieces(
+            jnp.concatenate(
+                [points(turned, f, i, odd) for odd in range(2) for i in range(SIDE) for f in fixed],
+                axis=0,
+            )
+        ),
+        columns(side_moves, SIDE_MOVES.index((0, 0)), 1),
+    )
     for i in range(SIDE):
         for j in range(2):
             at = 2 * i + j
             tall[24 * at : 24 * at + 8, :] = jnp.zeros(tile, jnp.float32)
             tall[24 * at + 8 : 24 * at + 16, :] = patch[entry_index(i, j)]
             tall[24 * at + 16 : 24 * at + 24, :] = jnp.zeros(tile, jnp.float32)
-            for comp in range(3):
-                site[comp * SITES + at] = half_blocks(turned, comp, i, j)
-            site[3 * SITES + at] = 1.0 - half_blocks(turned, DAMAGE, i, j)
-
-    def shape_site(at, carry):
-        base = lax.shift_right_logical(at, 1) * PATCH_Y + (at & 1)
+            for k in range(4):
+                row = ((j * SIDE + i) * 4 + k) * ROWS
+                value = values[row : row + ROWS]
+                site[k * SITES + at] = value if k < 3 else 1.0 - value
+
+    def shape_site(i, j):
+        at = 2 * i + j
+        base = i * PATCH_Y + j
         shape = {}
         moment = {}
         first = {}
-        for dz in range(-REACH, REACH + 1):
-            here = tall[pl.ds(24 * at + 8 - dz, ROWS), :]
-            acc = {}
-            acc_u = [{}, {}, {}]
-
-            def gain(store, key, value, factor=1):
-                store[key] = add_scaled(store.get(key), value, factor)
-
-            for dx, steps in bond_steps(dz):
-                terms = {}
-                terms_u = [{}, {}, {}]
+        def gain(store, key, value, factor=1):
+            store[key] = add_scaled(store.get(key), value, factor)
+
+        for depths in ((0,), (1, -1), (2, -2), (3, -3)):
+            here = {dz: tall[pl.ds(24 * at + 8 - dz, ROWS), :] for dz in depths}
+            acc = {dz: {} for dz in depths}
+            acc_u = {dz: [{}, {}, {}] for dz in depths}
+            for dx, steps in bond_steps(depths[0]):
+                terms = {dz: {} for dz in depths}
+                terms_u = {dz: [{}, {}, {}] for dz in depths}
                 for dy in steps:
                     k = base + (dx + REACH) * PATCH_Y + dy + REACH
-                    strength = jnp.minimum(here, patch[k])
-                    terms[dy] = strength * patch[ENTRIES + k]
+                    limit = patch[k]
+                    amounts = [patch[(1 + c) * ENTRIES + k] for c in range(4)]
+                    for dz in depths:
+                        strength = jnp.minimum(here[dz], limit)
+                        terms[dz][dy] = strength * amounts[0]
+                        for comp in range(3):
+                            terms_u[dz][comp][dy] = strength * amounts[1 + comp]
+                for dz in depths:
+                    t0, t1, t2 = signed_sums(terms[dz], 2)
+                    if dz:
+                        gain(acc[dz], "1", t0)
+                    gain(acc[dz], "x", t0, dx)
+                    gain(acc[dz], "xx", t0, dx * dx)
+                    gain(acc[dz], "y", t1)
+                    gain(acc[dz], "xy", t1, dx)
+                    gain(acc[dz], "yy", t2)
                     for comp in range(3):
-                        terms_u[comp][dy] = strength * patch[(2 + comp) * ENTRIES + k]
-                t0, t1, t2 = signed_sums(terms, 2)
-                if dz:
-                    gain(acc, "1", t0)
-                gain(acc, "x", t0, dx)
-                gain(acc, "xx", t0, dx * dx)
-                gain(acc, "y", t1)
-                gain(acc, "xy", t1, dx)
-                gain(acc, "yy", t2)
+                        s0, s1 = signed_sums(terms_u[dz][comp], 1)
+                        if dz:
+                            gain(acc_u[dz][comp], "1", s0)
+                        gain(acc_u[dz][comp], "x", s0, dx)
+                        gain(acc_u[dz][comp], "y", s1)
+
+            for dz in depths:
+
+                def back(value):
+                    if value is None or dz == 0:
+                        return value
+                    return pltpu.roll(value, (-dz) % ROWS, 0)
+
+                moved = {key: back(value) for key, value in acc[dz].items()}
+                for key in ("xx", "xy", "yy"):
+                    gain(shape, key, moved.get(key))
+                gain(shape, "xz", moved.get("x"), dz)
+                gain(shape, "yz", moved.get("y"), dz)
+                gain(shape, "zz", moved.get("1"), dz * dz)
+                gain(first, "x", moved.get("x"))
+                gain(first, "y", moved.get("y"))
+                gain(first, "z", moved.get("1"), dz)
                 for comp in range(3):
-                    s0, s1 = signed_sums(terms_u[comp], 1)
-                    if dz:
-                        gain(acc_u[comp], "1", s0)
-                    gain(acc_u[comp], "x", s0, dx)
-                    gain(acc_u[comp], "y", s1)
-
-            def back(value):
-                if value is None or dz == 0:
-                    return value
-                return pltpu.roll(value, (-dz) % ROWS, 0)
-
-            moved = {key: back(value) for key, value in acc.items()}
-            for key in ("xx", "xy", "yy"):
-                gain(shape, key, moved.get(key))
-            gain(shape, "xz", moved.get("x"), dz)
-            gain(shape, "yz", moved.get("y"), dz)
-            gain(shape, "zz", moved.get("1"), dz * dz)
-            gain(first, "x", moved.get("x"))
-            gain(first, "y", moved.get("y"))
-            gain(first, "z", moved.get("1"), dz)
-            for comp in range(3):
-                moved_u = {key: back(value) for key, value in acc_u[comp].items()}
-                gain(moment, (comp, 0), moved_u.get("x"))
-                gain(moment, (comp, 1), moved_u.get("y"))
-                gain(moment, (comp, 2), moved_u.get("1"), dz)
+                    moved_u = {key: back(value) for key, value in acc_u[dz][comp].items()}
+                    gain(moment, (comp, 0), moved_u.get("x"))
+                    gain(moment, (comp, 1), moved_u.get("y"))
+                    gain(moment, (comp, 2), moved_u.get("1"), dz)
         kxx, kxy, kyy = shape["xx"], shape["xy"], shape["yy"]
         kxz, kyz, kzz = shape["xz"], shape["yz"], shape["zz"]
         plain = [kxx, kxy, kxz, kxy, kyy, kyz, kxz, kyz, kzz]
@@ -442,87 +560,163 @@
             result[(9 + a) * SITES + at] = (
                 carried[3 * a] * arm[0] + carried[3 * a + 1] * arm[1] + carried[3 * a + 2] * arm[2]
             )
-        return carry
-
-    lax.fori_loop(0, SITES, shape_site, 0)
-
-    for k in range(9):
-        for x_at, y_at in ENTRY_LIST:
-            sx, i = x_at // SIDE, x_at % SIDE
-            half, j = y_at // 2, y_at % 2
-            value = stress[k * SITES + 2 * i + j]
-            move = (-(wide * sx + half)) % LANES
-            if move:
-                value = pltpu.roll(value, move, 1)
-            spread[k * ENTRIES + entry_index(x_at, y_at)] = value
-
-    def force_site(at, carry):
-        base = lax.shift_right_logical(at, 1) * PATCH_Y + (at & 1)
+
+    def quarter_at(x_at, y_at):
+        return (x_at + REACH) * PATCH_Y + y_at + REACH
+
+    def site_pairs(source, first, odd, j, count):
+        return [
+            jnp.concatenate(
+                [source[first + k * SITES + 2 * i + j] for i in (odd, odd + 2)], axis=1
+            )
+            for k in range(count)
+        ]
+
+    def quarter_entries(odd):
+        parts = [part for j in range(2) for part in site_pairs(stress, 0, odd, j, 9)]
+        parts = pieces(jnp.concatenate(parts, axis=0))
+        for first in range(0, len(QUARTER_MOVES), CHUNK):
+            chosen = QUARTER_MOVES[first : first + CHUNK]
+            values = moved(parts, columns(quarter_moves, first, len(chosen)))
+            for step, (x_even, half) in enumerate(chosen):
+                row = 0
+                x_at = x_even - x_even % 2 + odd
+                for j in range(2):
+                    y_at = 2 * half + j
+                    for k in range(9):
+                        if (x_at, y_at) in QUARTER_LIST:
+                            value = values[row : row + ROWS, step * LANES : (step + 1) * LANES]
+                            spread[k * QUARTERS + quarter_at(x_at, y_at)] = value
+                        row += ROWS
+
+    own_moves = columns(quarter_moves, QUARTER_MOVES.index((0, 0)), 1)
+
+    def quarter_health():
+        values = moved(
+            pieces(jnp.concatenate(
+                [
+                    jnp.concatenate(
+                        [patch[entry_index(x_at, y_at)], patch[entry_index(x_at + 2, y_at)]], axis=1
+                    )
+                    for x_at, y_at in QUARTER_LIST
+                ],
+                axis=0,
+            )),
+            own_moves,
+        )
+        for k, (x_at, y_at) in enumerate(QUARTER_LIST):
+            value = values[k * ROWS : (k + 1) * ROWS]
+            spread_health[quarter_at(x_at, y_at)] = value
+            if 0 <= x_at < 2 and 0 <= y_at < 2:
+                row = 24 * (2 * x_at + y_at)
+                tall_quarter[row : row + 8, :] = jnp.zeros(tile, jnp.float32)
+                tall_quarter[row + 8 : row + 16, :] = value
+                tall_quarter[row + 16 : row + 24, :] = jnp.zeros(tile, jnp.float32)
+
+    blocks = nx * ny
+    per_group = LANES // blocks
+
+    def gather_grad(group, comps):
+        sites = [
+            jnp.concatenate([result[comp * SITES + at] for comp in comps], axis=1)
+            for at in range(SITES)
+        ]
+        values = moved(pieces(jnp.concatenate(sites, axis=0)), grad_moves[0 : len(comps) * LANES, :])
+        for at in range(SITES):
+            for jh in range(2):
+                start = group * LANES + (2 * jh + at % 2) * SIDE + at // 2
+                gathered[pl.ds(start, ROWS, stride=SIDE * SIDE), :] = values[
+                    at * ROWS : (at + 1) * ROWS, jh * LANES : (jh + 1) * LANES
+                ]
+
+    def group_out(group, comps, target, first):
+        rows_out[group * LANES : (group + 1) * LANES, :] = gathered[
+            group * LANES : (group + 1) * LANES, :
+        ].T
+        for part, comp in enumerate(comps):
+            for x in range(nx):
+                row = group * LANES + part * blocks + x * ny
+                target[x, comp - first, :, :] = rows_out[row : row + ny, :]
+
+    grad_groups = [list(range(9))[k : k + per_group] for k in range(0, 9, per_group)]
+
+    for i in COLUMN_ORDER:
+        for j in range(2):
+            shape_site(i, j)
+        if i == COLUMN_ORDER[1]:
+            quarter_entries(0)
+            quarter_health()
+    quarter_entries(1)
+    for group, comps in enumerate(grad_groups):
+        gather_grad(group, comps)
+        group_out(group, comps, hold_grad, 0)
+    grad_copy = pltpu.make_async_copy(hold_grad, out_grad, sems.at[0])
+    grad_copy.start()
+
+    parts = [
+        part for i in range(2) for j in range(2) for part in site_pairs(result, 9 * SITES, i, j, 3)
+    ]
+    values = moved(pieces(jnp.concatenate(parts, axis=0)), own_moves)
+    for k in range(12):
+        start_force[k] = values[k * ROWS : (k + 1) * ROWS]
+
+    def force_site(i, j):
+        at = 2 * i + j
+        base = (i + REACH) * PATCH_Y + j + REACH
         here = {
-            dz: tall[pl.ds(24 * at + 8 - dz, ROWS), :] for dz in range(-REACH, REACH + 1)
+            dz: tall_quarter[24 * at + 8 - dz : 24 * at + 16 - dz, :]
+            for dz in range(-REACH, REACH + 1)
         }
         acc = {}
         for dx in range(-REACH, REACH + 1):
             for dy in range(-REACH, REACH + 1):
                 if dx * dx + dy * dy > REACH_SQ:
                     continue
-                k = base + (dx + REACH) * PATCH_Y + dy + REACH
+                k = base + dx * PATCH_Y + dy
                 deep = [
                     dz
                     for dz in range(-REACH, REACH + 1)
                     if dx * dx + dy * dy + dz * dz <= REACH_SQ and (dx, dy, dz) != (0, 0, 0)
                 ]
-                strength = {dz: jnp.minimum(here[dz], patch[k]) for dz in deep}
+                strength = {dz: jnp.minimum(here[dz], spread_health[k]) for dz in deep}
                 for a in range(3):
                     flat = None
                     if dx:
-                        flat = add_scaled(flat, spread[3 * a * ENTRIES + k], dx)
+                        flat = add_scaled(flat, spread[3 * a * QUARTERS + k], dx)
                     if dy:
-                        flat = add_scaled(flat, spread[(3 * a + 1) * ENTRIES + k], dy)
-                    upright = spread[(3 * a + 2) * ENTRIES + k]
+                        flat = add_scaled(flat, spread[(3 * a + 1) * QUARTERS + k], dy)
+                    upright = spread[(3 * a + 2) * QUARTERS + k]
                     for dz in deep:
                         value = add_scaled(flat, upright, dz)
                         acc[a, dz] = plus(acc.get((a, dz)), strength[dz] * value)
         for a in range(3):
-            total = result[(9 + a) * SITES + at]
+            total = start_force[3 * at + a]
             for dz in range(-REACH, REACH + 1):
                 value = acc[a, dz]
                 total = total + (pltpu.roll(value, (-dz) % ROWS, 0) if dz else value)
-            result[(9 + a) * SITES + at] = total
-        return carry
-
-    lax.fori_loop(0, SITES, force_site, 0)
-
-    blocks = nx * ny
-    per_group = LANES // blocks
-    slot = divide(lane, blocks, per_group + 1)
-    block = lane - blocks * slot
-    block_x = divide(block, ny, nx)
-    block_y = block - ny * block_x
-    comps = 12
-    for jh in range(2):
-        pick = (block_x + 1) * wide + 2 * (block_y + 1) + jh
-        for i in range(SIDE):
-            for j in range(2):
-                for group in range(comps // per_group):
-                    merged = None
-                    for part in range(per_group):
-                        value = lanes_of(result[(group * per_group + part) * SITES + 2 * i + j], pick)
-                        merged = value if merged is None else jnp.where(slot == part, value, merged)
-                    start = group * LANES + (2 * jh + j) * SIDE + i
-                    gathered[pl.ds(start, ROWS, stride=SIDE * SIDE), :] = merged
-    for group in range(comps // per_group):
-        rows_out[group * LANES : (group + 1) * LANES, :] = gathered[
-            group * LANES : (group + 1) * LANES, :
-        ].T
-    for x in range(nx):
-        for comp in range(comps):
-            row = comp * blocks + x * ny
-            value = rows_out[row : row + ny, :]
-            if comp < 9:
-                out_grad[x, comp, :, :] = value
-            else:
-                out_force[x, comp - 9, :, :] = value
+            start_force[3 * at + a] = total
+
+    for i in range(2):
+        for j in range(2):
+            force_site(i, j)
+    group = len(grad_groups)
+    sites = [
+        jnp.concatenate([start_force[3 * at + a] for a in range(3)], axis=1) for at in range(4)
+    ]
+    values = moved(pieces(jnp.concatenate(sites, axis=0)), force_moves[...])
+    for at in range(4):
+        for ih in range(2):
+            for jh in range(2):
+                start = group * LANES + (2 * jh + at % 2) * SIDE + 2 * ih + at // 2
+                column = (2 * ih + jh) * LANES
+                gathered[pl.ds(start, ROWS, stride=SIDE * SIDE), :] = values[
+                    at * ROWS : (at + 1) * ROWS, column : column + LANES
+                ]
+    group_out(group, [9, 10, 11], hold_force, 9)
+    force_copy = pltpu.make_async_copy(hold_force, out_force, sems.at[1])
+    force_copy.start()
+    grad_copy.wait()
+    force_copy.wait()
 
 
 def local(displacement, volume, health, damage, block_pairs):
@@ -546,6 +740,22 @@
     )(*[pltpu.with_memory_space_constraint(a, pltpu.HBM) for a in (*raw, pairs)])
     x_odd = swap(x_to_odd, "gx", True)
     x_even = swap(x_to_even, "gx", False)
+    move_shapes = [
+        jax.ShapeDtypeStruct((height * LANES, width * LANES), jnp.bfloat16)
+        for height, width in (
+            (2, len(SIDE_MOVES)),
+            (2, len(QUARTER_MOVES)),
+            (LANES // (nx * ny), 2),
+            (3, 4),
+        )
+    ]
+    moves = pl.pallas_call(
+        functools.partial(moves_kernel, nx, ny),
+        out_shape=move_shapes,
+        in_specs=[pl.BlockSpec(memory_space=pl.ANY)],
+        compiler_params=params,
+        name="moves",
+    )(x_to_even)
     y_shape = jax.ShapeDtypeStruct((FIELDS * ext_x * RING + ROWS, points), f32)
     y_to_even, y_to_odd = pl.pallas_call(
         functools.partial(middle_kernel, nx, ny),
@@ -571,14 +781,21 @@
             pltpu.VMEM((24 * SITES, LANES), f32),
             tiles(4 * SITES),
             tiles(9 * SITES),
-            tiles(9 * ENTRIES),
+            tiles(9 * QUARTERS),
+            tiles(QUARTERS),
+            pltpu.VMEM((24 * 4, LANES), f32),
+            tiles(12),
             tiles(12 * SITES),
-            rows(3),
-            rows(3),
+            rows(4),
+            rows(4),
+            pltpu.VMEM((nx, 9, ny, points), f32),
+            pltpu.VMEM((nx, 3, ny, points), f32),
+            pltpu.SemaphoreType.DMA((2,)),
         ],
+        out_specs=(pl.BlockSpec(memory_space=pltpu.HBM),) * 2,
         compiler_params=params,
         name="main",
-    )(own, y_to_even, x_even, x_odd, y_even, y_odd)
+    )(own, y_to_even, x_even, x_odd, y_even, y_odd, *moves)
     return grad.transpose(0, 2, 1, 3), force.transpose(0, 2, 1, 3)
 
 

time: 19.5 us -> 18.2 us (0.933)
  Pallas kernels: 7.87 us -> 7.09 us
  waiting for transfers between devices: 4.22 us -> 3.68 us
    pallas_call x1, Pallas kernels: 6.8 us -> 5.49 us  [local(): pl.pallas_call(functools.partial(main_kernel, nx, ny), out_shape=(jax.Sha...]
    ppermute x4, waiting for transfers between devices: 4.22 us -> 3.68 us  [swap(): return lax.ppermute(array, ('gx', 'gy'), pairs)]
    pallas_call x0 -> x1, Pallas kernels: none -> 0.53 us  [local(): pl.pallas_call(functools.partial(moves_kernel, nx, ny), out_shape=move_sh...]
  transfers between devices with their start and end apart: 4 -> 4, of which waited for: 2 -> 2; matrix products, arithmetic and copies ran while one was open for 0% -> 0% of each run, Pallas kernels for 0% -> 3%
where the time goes in v4:
time: 18.2 us; the launch traced here: 18.1 us
  Pallas kernels  7.09 us (39%)
  starting transfers between devices  6.64 us (36%)
  waiting for transfers between devices  3.68 us (20%)
  between operations  0.65 us (4%)
    ppermute x4, starting transfers between devices, swap(): return lax.ppermute(array, ('gx', 'gy'), pairs)  6.64 us
    pallas_call x1, Pallas kernels, local(): pl.pallas_call(functools.partial(main_kernel, nx, ny), out_shape=(jax.Sha...  5.49 us
    ppermute x4, waiting for transfers between devices, swap(): return lax.ppermute(array, ('gx', 'gy'), pairs)  3.68 us
    pallas_call x1, Pallas kernels, local(): pl.pallas_call(functools.partial(pack_kernel, nx, ny), out_shape=(jax.Sha...  0.99 us
    pallas_call x1, Pallas kernels, local(): pl.pallas_call(functools.partial(moves_kernel, nx, ny), out_shape=move_sh...  0.53 us
  transfers between devices with their start and end apart: 4, of which 2 were waited for; matrix products, arithmetic and copies ran while one was open for 0% of the time, Pallas kernels for 3%

profile of v4, /device:TPU:0, one launch (start us, length us, event | category | flops | bytes accessed | tf_op | source)
XLA Modules:
  0.0 18.1 jit_solution(11944077368359514978)
XLA Ops:
  0.6 1.0 %pack.1 = (f32[192,128]{1,0:T(8,128)S(1)}, f32[56,128]{1,0:T(8,128)S(1)}, f32[56,128]{1,0:T(8,128)S(1)}) custom-call(f32[8,3,4,128]{3,2,1,0:T(4,128)} %bitcast.6, f32[8,4,128]{2,1,0:T(4,128)} %vol.1, f32[8,4,128]{2,1,0:T(4,128)} %health.1, s32[8,4,128]{2,1,0:T(4,128)} %damage.1, s32[4,162]{1,0:T(4,128)} %bitcast.7), custom_call_target="tpu_custom_call" | custom-call | tf_op jit(solution)/shard_map/pack/pallas_call | solution.py:730
  1.6 0.5 %collective-permute-start.1 = (f32[56,128]{1,0:T(8,128)S(1)}, f32[56,128]{1,0:T(8,128)S(1)}, u32[]{:S(2)}, u32[]{:S(2)}) collective-permute-start(f32[56,128]{1,0:T(8,128)S(1)} %get-tuple-element.15), channel_id=1, source_target_pairs={{0,1},{1,0},{2,3},{3,2},{4,8},{5,9},{6,10},{7,11},{8,4},{9,5},{10,... | collective-permute-start | bytes 86024 | tf_op jit(solution)/shard_map/ppermute | solution.py:84
  2.1 4.0 %collective-permute-start = (f32[56,128]{1,0:T(8,128)S(1)}, f32[56,128]{1,0:T(8,128)S(1)}, u32[]{:S(2)}, u32[]{:S(2)}) collective-permute-start(f32[56,128]{1,0:T(8,128)S(1)} %get-tuple-element.14.x_mine.after), channel_id=1, source_target_pairs={{0,4},{1,5},{2,6},{3,7},{4,0},{5,1},{6,2},{7,3},{8,12},{9,13},{10,... | collective-permute-start | bytes 86024 | tf_op jit(solution)/shard_map/ppermute | solution.py:84
  6.2 0.0 collective-permute-done.1.x_odd
  6.2 1.8 %collective-permute-done.x_even = f32[56,128]{1,0:T(8,128)S(1)} collective-permute-done((f32[56,128]{1,0:T(8,128)S(1)}, f32[56,128]{1,0:T(8,128)S(1)}, u32[]{:S(2)}, u32[]{:S(2)}) %collective-permute-start) | collective-permute-done | bytes 28704 | tf_op jit(solution)/shard_map/ppermute | solution.py:84
  8.0 0.1 middle.1
  8.1 2.1 %collective-permute-start.3 = (f32[152,128]{1,0:T(8,128)S(1)}, f32[152,128]{1,0:T(8,128)S(1)}, u32[]{:S(2)}, u32[]{:S(2)}) collective-permute-start(f32[152,128]{1,0:T(8,128)S(1)} %get-tuple-element.17), channel_id=1, source_target_pairs={{0,4},{1,2},{2,1},{3,7},{4,0},{5,6},{6,5},{7,3},{8,12},{9,10},{10,... | collective-permute-start | bytes 233480 | tf_op jit(solution)/shard_map/ppermute | solution.py:84
  10.2 0.0 collective-permute-start.2
  10.2 0.5 %moves.1 = (bf16[256,1408]{1,0:T(8,128)(2,1)S(1)}, bf16[256,1664]{1,0:T(8,128)(2,1)S(1)}, bf16[512,256]{1,0:T(8,128)(2,1)S(1)}, bf16[384,512]{1,0:T(8,128)(2,1)S(1)}) custom-call(f32[56,128]{1,0:T(8,128)S(1)} %get-tuple-element.14.x_mine.after), custom_call_target="tpu_custom_call" | custom-call | tf_op jit(solution)/shard_map/moves/pallas_call | solution.py:752
  10.7 1.8 %collective-permute-done.3.y_odd = f32[152,128]{1,0:T(8,128)S(1)} collective-permute-done((f32[152,128]{1,0:T(8,128)S(1)}, f32[152,128]{1,0:T(8,128)S(1)}, u32[]{:S(2)}, u32[]{:S(2)}) %collective-permute-start.3) | collective-permute-done | bytes 77856 | tf_op jit(solution)/shard_map/ppermute | solution.py:84
  12.6 0.0 collective-permute-done.2.y_even
  12.6 5.5 %main.1 = (f32[8,9,4,128]{3,2,1,0:T(4,128)}, f32[8,3,4,128]{3,2,1,0:T(4,128)}) custom-call(f32[192,128]{1,0:T(8,128)S(1)} %get-tuple-element.13.own, f32[152,128]{1,0:T(8,128)S(1)} %get-tuple-element.16.y_mine, f32[56,128]{1,0:T(8,128)S(1)} %collective-permute-done.x_even, f32[56,128]{1,0:T(8,128)S(1)} %collective-permute-done.1.x_odd, ...), custom_call_target="tpu_custom_call" | custom-call | tf_op jit(solution)/shard_map/main/pallas_call | solution.py:770
Async XLA Ops:
  1.6 4.6 %collective-permute-start.1 = (f32[56,128]{1,0:T(8,128)S(1)}, f32[56,128]{1,0:T(8,128)S(1)}, u32[]{:S(2)}, u32[]{:S(2)}) collective-permute-start(f32[56,128]{1,0:T(8,128)S(1)} %get-tuple-element.15), channel_id=1, source_target_pairs={{0,1},{1,0},{2,3},{3,2},{4,8},{5,9},{6,10},{7,11},{8,4},{9,5},{10,... | collective-permute-start | bytes 86024 | tf_op jit(solution)/shard_map/ppermute | solution.py:84
  2.1 5.9 %collective-permute-start = (f32[56,128]{1,0:T(8,128)S(1)}, f32[56,128]{1,0:T(8,128)S(1)}, u32[]{:S(2)}, u32[]{:S(2)}) collective-permute-start(f32[56,128]{1,0:T(8,128)S(1)} %get-tuple-element.14.x_mine.after), channel_id=1, source_target_pairs={{0,4},{1,5},{2,6},{3,7},{4,0},{5,1},{6,2},{7,3},{8,12},{9,13},{10,... | collective-permute-start | bytes 86024 | tf_op jit(solution)/shard_map/ppermute | solution.py:84
  8.1 4.5 %collective-permute-start.3 = (f32[152,128]{1,0:T(8,128)S(1)}, f32[152,128]{1,0:T(8,128)S(1)}, u32[]{:S(2)}, u32[]{:S(2)}) collective-permute-start(f32[152,128]{1,0:T(8,128)S(1)} %get-tuple-element.17), channel_id=1, source_target_pairs={{0,4},{1,2},{2,1},{3,7},{4,0},{5,6},{6,5},{7,3},{8,12},{9,10},{10,... | collective-permute-start | bytes 233480 | tf_op jit(solution)/shard_map/ppermute | solution.py:84
  10.2 2.4 %collective-permute-start.2 = (f32[152,128]{1,0:T(8,128)S(1)}, f32[152,128]{1,0:T(8,128)S(1)}, u32[]{:S(2)}, u32[]{:S(2)}) collective-permute-start(f32[152,128]{1,0:T(8,128)S(1)} %get-tuple-element.16.y_mine), channel_id=1, source_target_pairs={{0,1},{1,0},{2,3},{3,2},{4,5},{5,4},{6,7},{7,6},{8,9},{9,8},{10,11... | collective-permute-start | bytes 233480 | tf_op jit(solution)/shard_map/ppermute | solution.py:84

commit v5 on v4

--- a/solution.py
+++ b/solution.py
@@ -14,6 +14,7 @@
 REACH_SQ = 9
 RING = 2
 FIELDS = 6
+FAR = 5
 VOL, HEALTH, DAMAGE = 3, 4, 5
 LAME = 24.0
 SHEAR = 16.0
@@ -77,10 +78,10 @@
         if not left:
             to[one] = one
             break
-        other = min(left, key=lambda at: (abs(at[0] - one[0]) + abs(at[1] - one[1]), -at[0] - at[1]))
+        other = min(left, key=lambda at: (axis == "gy" and at != (one[0] ^ 2, one[1]), abs(at[0] - one[0]) + abs(at[1] - one[1]), -at[0] - at[1]))
         left.remove(other)
         to[one], to[other] = other, one
-    pairs = [(i * ny + j, k * ny + l) for (i, j), (k, l) in sorted(to.items())]
+    pairs = [(i * ny + j, k * ny + l) for (i, j), (k, l) in to.items()]
     return lax.ppermute(array, ("gx", "gy"), pairs)
 
 
@@ -123,16 +124,16 @@
 
 def moves_kernel(nx, ny, after, side_moves, quarter_moves, grad_moves, force_moves):
     lane, wide, at_x, at_y, upper = lane_places(nx, ny)
-    ext_x = nx + 2 * RING
+    ext_x, ext_y = nx + 2 * RING, ny + 2 * RING
     low_x_at, low_y_at = nx * ny, nx * ny + 2 * RING * ny
-    side_y = ext_x * RING
     rows = iota((2 * ROWS, LANES), 0)
 
     def block_row(e, f):
         own = (e - RING) * ny + f - RING
-        beside = low_x_at + jnp.where(e < RING, e, e - nx) * ny + f - RING
-        above = low_y_at + jnp.where(f < RING, 0, side_y) + e * RING
-        above = above + jnp.where(f < RING, f, f - RING - ny)
+        column = jnp.where(e < RING, e, RING + ext_x - 1 - e)
+        beside = low_x_at + column * ny + f - RING
+        line = jnp.where(f < RING, f, RING + ext_y - 1 - f)
+        above = low_y_at + line * ext_x + e
         row = jnp.where((e < RING) | (e >= RING + nx), beside, own)
         return jnp.where((f < RING) | (f >= RING + ny), above, row)
 
@@ -182,7 +183,8 @@
     copies = []
     for k, (source, target) in enumerate(zip((disp, vol, health, damage, pairs), here)):
         copies.append(pltpu.make_async_copy(source, target, sems.at[k]))
-        copies[-1].start()
+    for k in (4, 0, 1, 2, 3):
+        copies[k].start()
     disp, vol, health, damage, pairs = here
     odd_here = lax.rem(lax.axis_index("gx"), 2)
     ext_x = nx + 2 * RING
@@ -211,11 +213,30 @@
                 value = damage[x, :, :].astype(jnp.float32)
             row = (field * nx + x) * ny
             own[row : row + ny, :] = value
-    for target, start in ((to_even, (1 - odd_here) * (nx - RING)), (to_odd, odd_here * (nx - RING))):
+    for target, high in ((to_even, 1 - odd_here), (to_odd, odd_here)):
+        target[0:ROWS, :] = table
         for field in range(FIELDS):
-            row = field * RING * ny
-            target[row : row + RING * ny, :] = own_rows(own, nx, ny, field, start, 0, RING * ny)
-        target[FIELDS * RING * ny :, :] = table
+            row = ROWS + field * ny
+            target[row : row + ny, :] = own_rows(own, nx, ny, field, high * (nx - 1), 0, ny)
+        outer = 1 + high * (nx - 3)
+        halves = [
+            jnp.concatenate(
+                [own_rows(own, nx, ny, field, outer, y, ny // 2) for field in range(FAR)], axis=0
+            )
+            for y in (0, ny // 2)
+        ]
+        target[ROWS + FIELDS * ny :, :] = folded(*halves, SIDE // 2, high)
+
+
+def folded(first, second, step, high):
+    keep = (iota(first.shape, 1) & step) != 0
+    of_high = jnp.where(keep, first, pltpu.roll(second, LANES - step, 1))
+    of_low = jnp.where(keep, pltpu.roll(second, step, 1), first)
+    return jnp.where(high == 1, of_high, of_low)
+
+
+def unfolded(rows, step, low):
+    return rows, pltpu.roll(rows, step if low else LANES - step, 1)
 
 
 def sides(from_even, from_odd, axis):
@@ -232,27 +253,49 @@
     return table + jnp.where(at < 2 * RING, pltpu.roll(low, size - count, axis), 0.0)
 
 
-def middle_kernel(nx, ny, own, x_mine, x_even, x_odd, to_even, to_odd):
+def middle_kernel(nx, ny, own, x_mine, x_even, x_odd, to_even, to_odd, beside, far):
     odd_y = lax.rem(lax.axis_index("gy"), 2)
     ext_x = nx + 2 * RING
-    side_rows = RING * ny
+    half = ny // 2
     lane = iota((ROWS, LANES), 1)
     at_e = lane - ext_x * divide(lane, ext_x, LANES // ext_x + 1)
-    low, high = sides(x_even[FIELDS * side_rows :, :], x_odd[FIELDS * side_rows :, :], "gx")
-    table = joined(x_mine[FIELDS * side_rows :, :], low, high, nx, 1, at_e, LANES)
-    for target, start in ((to_even, (1 - odd_y) * (ny - RING)), (to_odd, odd_y * (ny - RING))):
+    received = sides(x_even[...], x_odd[...], "gx")
+    table = joined(x_mine[0:ROWS, :], received[0][0:ROWS], received[1][0:ROWS], nx, 1, at_e, LANES)
+    for side, rows in enumerate(received):
+        outer = unfolded(rows[ROWS + FIELDS * ny :], SIDE // 2, side == 0)
         for field in range(FIELDS):
-            for x in range(RING):
-                halo = pl.ds((field * RING + x) * ny + start, RING)
-                low, high = sides(x_even[halo, :], x_odd[halo, :], "gx")
-                row = (field * ext_x + x) * RING
-                target[row : row + RING, :] = low
-                row += (RING + nx) * RING
-                target[row : row + RING, :] = high
-            for x in range(nx):
-                row = (field * ext_x + RING + x) * RING
-                target[row : row + RING, :] = own_rows(own, nx, ny, field, x, start, RING)
-        target[FIELDS * ext_x * RING :, :] = table
+            row = (field * 2 + side) * 2 * ny
+            for part in range(2):
+                if field < FAR:
+                    value = outer[part][field * half : (field + 1) * half]
+                else:
+                    value = jnp.zeros((half, LANES), jnp.float32)
+                beside[row + part * half : row + (part + 1) * half, :] = value
+            beside[row + ny : row + 2 * ny, :] = rows[ROWS + field * ny : ROWS + (field + 1) * ny]
+
+    def line(target, row, field, y):
+        base = field * 4 * ny
+        for e, column in ((0, 0), (1, 1), (nx + 2, 3), (nx + 3, 2)):
+            target[row + e : row + e + 1, :] = beside[pl.ds(base + column * ny + y, 1), :]
+        target[row + RING : row + RING + nx, :] = own[pl.ds(field * nx * ny + y, nx, stride=ny), :]
+
+    for target, high in ((to_even, 1 - odd_y), (to_odd, odd_y)):
+        target[0:ROWS, :] = table
+        for field in range(FIELDS):
+            line(target, ROWS + field * ext_x, field, high * (ny - 1))
+        for field in range(FAR):
+            line(far, field * ext_x, field, 1 + high * (ny - 3))
+        halves = [
+            jnp.concatenate(
+                [
+                    far[field * ext_x + e : field * ext_x + e + ext_x // 2, :]
+                    for field in range(FAR)
+                ],
+                axis=0,
+            )
+            for e in (0, ext_x // 2)
+        ]
+        target[ROWS + FIELDS * ext_x :, :] = folded(*halves, SIDE * SIDE // 2, high)
 
 
 def bond_steps(dz):
@@ -271,44 +314,55 @@
     return term if total is None else total + term
 
 
-def scaled(value, factor):
-    if factor == 0 or value is None:
-        return None
-    if factor == 1:
-        return value
-    if factor == -1:
-        return -value
-    return value * float(factor)
+def weighted_sum(values):
+    total = None
+    for k, value in sorted(values.items()):
+        total = plus(total, value if k == 1 else value * float(k))
+    return total
 
 
 def add_scaled(total, value, factor):
-    if factor == 0 or value is None:
+    if factor == 0:
         return total
+    if abs(factor) != 1:
+        value = value * float(abs(factor))
     if total is None:
-        return scaled(value, factor)
-    if factor == 1:
-        return total + value
-    if factor == -1:
-        return total - value
-    return total + value * float(factor)
-
-
-def signed_sums(terms, order):
-    even, odd = {}, {}
-    for dy in sorted({abs(dy) for dy in terms}):
-        if dy == 0:
-            even[0] = terms[0]
-        else:
-            even[dy] = terms[dy] + terms[-dy]
-            odd[dy] = terms[dy] - terms[-dy]
-    sums = [None] * (order + 1)
-    for dy, value in even.items():
-        sums[0] = plus(sums[0], value)
-    for dy, value in odd.items():
-        sums[1] = add_scaled(sums[1], value, dy)
-    if order == 2:
-        for dy, value in even.items():
-            sums[2] = add_scaled(sums[2], value, dy * dy)
+        return value if factor > 0 else -value
+    return total + value if factor > 0 else total - value
+
+
+def lattice_sums(terms, second):
+    row, slope, odd, even = {}, {}, {}, {}
+    for dx in sorted({dx for dx, _ in terms}, key=abs):
+        steps = {dy: terms[dx, dy] for x, dy in terms if x == dx}
+        differences = {}
+        for dy in sorted({abs(dy) for dy in steps}):
+            if dy:
+                summed = steps[dy] + steps[-dy]
+                differences[dy] = steps[dy] - steps[-dy]
+                even[dy] = plus(even.get(dy), summed)
+                if not second:
+                    odd[dy] = plus(odd.get(dy), differences[dy])
+            else:
+                summed = steps[0]
+            row[dx] = plus(row.get(dx), summed)
+        if second and differences:
+            slope[dx] = weighted_sum(differences)
+    rises = {dx: row[dx] - row[-dx] for dx in row if dx > 0}
+    pairs = {dx: row[dx] + row[-dx] for dx in row if dx > 0}
+    one = row.get(0)
+    for value in pairs.values():
+        one = plus(one, value)
+    sums = {"1": one, "x": weighted_sum(rises)}
+    if not second:
+        sums["y"] = weighted_sum(odd)
+        return sums
+    sums["y"] = None
+    for value in slope.values():
+        sums["y"] = plus(sums["y"], value)
+    sums["xx"] = weighted_sum({dx * dx: value for dx, value in pairs.items()})
+    sums["yy"] = weighted_sum({dy * dy: value for dy, value in even.items()})
+    sums["xy"] = weighted_sum({dx: slope[dx] - slope[-dx] for dx in slope if dx > 0})
     return sums
 
 
@@ -345,12 +399,13 @@
         if a == b:
             entry = entry + trace * (0.5 * LAME)
         second[3 * a + b] = second[3 * b + a] = entry
-    inverse = [value * alive for value in inverse]
+    i00, i01, i02, i11, i12, i22 = [value * alive for value in (i00, i01, i02, i11, i12, i22)]
+    inverse = [i00, i01, i02, i01, i11, i12, i02, i12, i22]
     return grad, product(product(grad, second), inverse)
 
 
 def main_kernel(
-    nx, ny, own, y_mine, x_even, x_odd, y_even, y_odd, side_moves, quarter_moves, grad_moves,
+    nx, ny, own, beside, y_mine, y_even, y_odd, side_moves, quarter_moves, grad_moves,
     force_moves, out_grad, out_force, ext, turned, weighted, patch, tall, site, stress, spread,
     spread_health, tall_quarter, start_force, result, gathered, rows_out, hold_grad, hold_force, sems
 ):
@@ -360,19 +415,30 @@
     lane, wide, at_x, at_y, upper = lane_places(nx, ny)
 
     low_x_at, low_y_at = nx * ny, nx * ny + 2 * RING * ny
-    side_x, side_y = RING * ny, ext_x * RING
-    x_low, x_high = sides(x_even[0 : FIELDS * side_x, :], x_odd[0 : FIELDS * side_x, :], "gx")
-    y_low, y_high = sides(y_even[...], y_odd[...], "gy")
+    side_x = 2 * RING * ny
+    received = sides(y_even[...], y_odd[...], "gy")
+    far = [
+        unfolded(rows[ROWS + FIELDS * ext_x :], SIDE * SIDE // 2, side == 0)
+        for side, rows in enumerate(received)
+    ]
+    half = ext_x // 2
     for field in range(FIELDS):
         base = field * LANES
         ext[base : base + nx * ny, :] = own_rows(own, nx, ny, field, 0, 0, nx * ny)
         at = base + low_x_at
-        ext[at : at + side_x, :] = x_low[field * side_x : (field + 1) * side_x]
-        ext[at + side_x : at + 2 * side_x, :] = x_high[field * side_x : (field + 1) * side_x]
+        ext[at : at + side_x, :] = beside[field * side_x : (field + 1) * side_x, :]
         at = base + low_y_at
-        ext[at : at + side_y, :] = y_low[field * side_y : (field + 1) * side_y]
-        ext[at + side_y : at + 2 * side_y, :] = y_high[field * side_y : (field + 1) * side_y]
-        at += 2 * side_y
+        for side in range(2):
+            for part in range(2):
+                if field < FAR:
+                    value = far[side][part][field * half : (field + 1) * half]
+                else:
+                    value = jnp.zeros((half, LANES), jnp.float32)
+                ext[at : at + half, :] = value
+                at += half
+            near = ROWS + field * ext_x
+            ext[at : at + ext_x, :] = received[side][near : near + ext_x]
+            at += ext_x
         if at < base + LANES:
             ext[at : base + LANES, :] = jnp.zeros((base + LANES - at, LANES), jnp.float32)
 
@@ -387,13 +453,7 @@
         )
 
     table = joined(
-        y_mine[FIELDS * side_y :, :],
-        y_low[FIELDS * side_y :],
-        y_high[FIELDS * side_y :],
-        ny,
-        0,
-        at_row,
-        ROWS,
+        y_mine[0:ROWS, :], received[0][0:ROWS], received[1][0:ROWS], ny, 0, at_row, ROWS
     )
     link = {}
     for kind, step in enumerate(KINDS):
@@ -486,39 +546,23 @@
         moment = {}
         first = {}
         def gain(store, key, value, factor=1):
-            store[key] = add_scaled(store.get(key), value, factor)
-
-        for depths in ((0,), (1, -1), (2, -2), (3, -3)):
-            here = {dz: tall[pl.ds(24 * at + 8 - dz, ROWS), :] for dz in depths}
-            acc = {dz: {} for dz in depths}
-            acc_u = {dz: [{}, {}, {}] for dz in depths}
+            if value is not None:
+                store[key] = add_scaled(store.get(key), value, factor)
+
+        for depths in ((0,), (1,), (-1,), (2,), (-2,), (3,), (-3,)):
+            here = {dz: tall[24 * at + 8 - dz : 24 * at + 16 - dz, :] for dz in depths}
+            terms = {dz: [{} for _ in range(4)] for dz in depths}
             for dx, steps in bond_steps(depths[0]):
-                terms = {dz: {} for dz in depths}
-                terms_u = {dz: [{}, {}, {}] for dz in depths}
                 for dy in steps:
                     k = base + (dx + REACH) * PATCH_Y + dy + REACH
                     limit = patch[k]
                     amounts = [patch[(1 + c) * ENTRIES + k] for c in range(4)]
                     for dz in depths:
                         strength = jnp.minimum(here[dz], limit)
-                        terms[dz][dy] = strength * amounts[0]
-                        for comp in range(3):
-                            terms_u[dz][comp][dy] = strength * amounts[1 + comp]
-                for dz in depths:
-                    t0, t1, t2 = signed_sums(terms[dz], 2)
-                    if dz:
-                        gain(acc[dz], "1", t0)
-                    gain(acc[dz], "x", t0, dx)
-                    gain(acc[dz], "xx", t0, dx * dx)
-                    gain(acc[dz], "y", t1)
-                    gain(acc[dz], "xy", t1, dx)
-                    gain(acc[dz], "yy", t2)
-                    for comp in range(3):
-                        s0, s1 = signed_sums(terms_u[dz][comp], 1)
-                        if dz:
-                            gain(acc_u[dz][comp], "1", s0)
-                        gain(acc_u[dz][comp], "x", s0, dx)
-                        gain(acc_u[dz][comp], "y", s1)
+                        for c in range(4):
+                            terms[dz][c][dx, dy] = strength * amounts[c]
+            acc = {dz: lattice_sums(terms[dz][0], True) for dz in depths}
+            acc_u = {dz: [lattice_sums(terms[dz][1 + c], False) for c in range(3)] for dz in depths}
 
             for dz in depths:
 
@@ -643,15 +687,9 @@
     for i in COLUMN_ORDER:
         for j in range(2):
             shape_site(i, j)
-        if i == COLUMN_ORDER[1]:
-            quarter_entries(0)
-            quarter_health()
+    quarter_health()
+    quarter_entries(0)
     quarter_entries(1)
-    for group, comps in enumerate(grad_groups):
-        gather_grad(group, comps)
-        group_out(group, comps, hold_grad, 0)
-    grad_copy = pltpu.make_async_copy(hold_grad, out_grad, sems.at[0])
-    grad_copy.start()
 
     parts = [
         part for i in range(2) for j in range(2) for part in site_pairs(result, 9 * SITES, i, j, 3)
@@ -686,8 +724,16 @@
                     if dy:
                         flat = add_scaled(flat, spread[(3 * a + 1) * QUARTERS + k], dy)
                     upright = spread[(3 * a + 2) * QUARTERS + k]
+                    lifts = {
+                        dz: upright if dz == 1 else upright * float(dz) for dz in deep if dz > 0
+                    }
                     for dz in deep:
-                        value = add_scaled(flat, upright, dz)
+                        if dz > 0:
+                            value = lifts[dz] if flat is None else flat + lifts[dz]
+                        elif dz < 0:
+                            value = -lifts[-dz] if flat is None else flat - lifts[-dz]
+                        else:
+                            value = flat
                         acc[a, dz] = plus(acc.get((a, dz)), strength[dz] * value)
         for a in range(3):
             total = start_force[3 * at + a]
@@ -696,9 +742,15 @@
                 total = total + (pltpu.roll(value, (-dz) % ROWS, 0) if dz else value)
             start_force[3 * at + a] = total
 
-    for i in range(2):
-        for j in range(2):
-            force_site(i, j)
+    force_site(0, 0)
+    for group, comps in enumerate(grad_groups):
+        gather_grad(group, comps)
+        group_out(group, comps, hold_grad, 0)
+    grad_copy = pltpu.make_async_copy(hold_grad, out_grad, sems.at[0])
+    grad_copy.start()
+    force_site(0, 1)
+    force_site(1, 0)
+    force_site(1, 1)
     group = len(grad_groups)
     sites = [
         jnp.concatenate([start_force[3 * at + a] for a in range(3)], axis=1) for at in range(4)
@@ -726,7 +778,7 @@
     pairs = block_pairs.reshape(block_pairs.shape[2:]).T
     raw = (displacement.transpose(0, 2, 1, 3), volume, health, damage)
     params = pltpu.CompilerParams(vmem_limit_bytes=48 * 1024 * 1024)
-    x_shape = jax.ShapeDtypeStruct((FIELDS * RING * ny + ROWS, points), f32)
+    x_shape = jax.ShapeDtypeStruct((ROWS + FIELDS * ny + FAR * ny // 2, points), f32)
     own, x_to_even, x_to_odd = pl.pallas_call(
         functools.partial(pack_kernel, nx, ny),
         out_shape=(jax.ShapeDtypeStruct((FIELDS * nx * ny, points), f32), x_shape, x_shape),
@@ -756,10 +808,11 @@
         compiler_params=params,
         name="moves",
     )(x_to_even)
-    y_shape = jax.ShapeDtypeStruct((FIELDS * ext_x * RING + ROWS, points), f32)
-    y_to_even, y_to_odd = pl.pallas_call(
+    y_shape = jax.ShapeDtypeStruct((ROWS + FIELDS * ext_x + FAR * ext_x // 2, points), f32)
+    y_to_even, y_to_odd, beside = pl.pallas_call(
         functools.partial(middle_kernel, nx, ny),
-        out_shape=(y_shape, y_shape),
+        out_shape=(y_shape, y_shape, jax.ShapeDtypeStruct((FIELDS * 2 * RING * ny, points), f32)),
+        scratch_shapes=[pltpu.VMEM((FAR * ext_x, points), f32)],
         compiler_params=params,
         name="middle",
     )(own, x_to_even, x_even, x_odd)
@@ -795,7 +848,7 @@
         out_specs=(pl.BlockSpec(memory_space=pltpu.HBM),) * 2,
         compiler_params=params,
         name="main",
-    )(own, y_to_even, x_even, x_odd, y_even, y_odd, *moves)
+    )(own, beside, y_to_even, y_even, y_odd, *moves)
     return grad.transpose(0, 2, 1, 3), force.transpose(0, 2, 1, 3)
 
 

time: 18.2 us -> 17.9 us (0.984)
    pallas_call x1, Pallas kernels: 5.49 us -> 5.3 us  [local(): pl.pallas_call(functools.partial(main_kernel, nx, ny), out_shape=(jax.Sha...]
where the time goes in v5:
time: 17.9 us; the launch traced here: 17.7 us
  Pallas kernels  7.01 us (39%)
  starting transfers between devices  6.56 us (37%)
  waiting for transfers between devices  3.51 us (20%)
  between operations  0.65 us (4%)
    ppermute x4, starting transfers between devices, swap(): return lax.ppermute(array, ('gx', 'gy'), pairs)  6.56 us
    pallas_call x1, Pallas kernels, local(): pl.pallas_call(functools.partial(main_kernel, nx, ny), out_shape=(jax.Sha...  5.3 us
    ppermute x4, waiting for transfers between devices, swap(): return lax.ppermute(array, ('gx', 'gy'), pairs)  3.51 us
    pallas_call x1, Pallas kernels, local(): pl.pallas_call(functools.partial(pack_kernel, nx, ny), out_shape=(jax.Sha...  1 us
    pallas_call x1, Pallas kernels, local(): pl.pallas_call(functools.partial(moves_kernel, nx, ny), out_shape=move_sh...  0.53 us
  transfers between devices with their start and end apart: 4, of which 2 were waited for; matrix products, arithmetic and copies ran while one was open for 0% of the time, Pallas kernels for 3%

profile of v5, /device:TPU:0, one launch (start us, length us, event | category | flops | bytes accessed | tf_op | source)
XLA Modules:
  0.0 17.7 jit_solution(248393353819900947)
XLA Ops:
  0.6 1.0 %pack.1 = (f32[192,128]{1,0:T(8,128)S(1)}, f32[42,128]{1,0:T(8,128)S(1)}, f32[42,128]{1,0:T(8,128)S(1)}) custom-call(f32[8,3,4,128]{3,2,1,0:T(4,128)} %bitcast.6, f32[8,4,128]{2,1,0:T(4,128)} %vol.1, f32[8,4,128]{2,1,0:T(4,128)} %health.1, s32[8,4,128]{2,1,0:T(4,128)} %damage.1, s32[4,162]{1,0:T(4,128)} %bitcast.7), custom_call_target="tpu_custom_call" | custom-call | tf_op jit(solution)/shard_map/pack/pallas_call | solution.py:782
  1.6 0.5 %collective-permute-start.1 = (f32[42,128]{1,0:T(8,128)S(1)}, f32[42,128]{1,0:T(8,128)S(1)}, u32[]{:S(2)}, u32[]{:S(2)}) collective-permute-start(f32[42,128]{1,0:T(8,128)S(1)} %get-tuple-element.16), channel_id=1, source_target_pairs={{4,8},{5,9},{6,10},{7,11},{8,4},{9,5},{10,6},{11,7},{12,16},{13,17... | collective-permute-start | bytes 64520 | tf_op jit(solution)/shard_map/ppermute | solution.py:85
  2.2 4.0 %collective-permute-start = (f32[42,128]{1,0:T(8,128)S(1)}, f32[42,128]{1,0:T(8,128)S(1)}, u32[]{:S(2)}, u32[]{:S(2)}) collective-permute-start(f32[42,128]{1,0:T(8,128)S(1)} %get-tuple-element.15.x_mine.after), channel_id=1, source_target_pairs={{0,4},{1,5},{2,6},{3,7},{4,0},{5,1},{6,2},{7,3},{8,12},{9,13},{10,... | collective-permute-start | bytes 64520 | tf_op jit(solution)/shard_map/ppermute | solution.py:85
  6.2 0.0 collective-permute-done.1.x_odd
  6.2 1.8 %collective-permute-done.x_even = f32[42,128]{1,0:T(8,128)S(1)} collective-permute-done((f32[42,128]{1,0:T(8,128)S(1)}, f32[42,128]{1,0:T(8,128)S(1)}, u32[]{:S(2)}, u32[]{:S(2)}) %collective-permute-start) | collective-permute-done | bytes 21536 | tf_op jit(solution)/shard_map/ppermute | solution.py:85
  8.0 0.2 %middle.1 = (f32[110,128]{1,0:T(8,128)S(1)}, f32[110,128]{1,0:T(8,128)S(1)}, f32[96,128]{1,0:T(8,128)S(1)}) custom-call(f32[192,128]{1,0:T(8,128)S(1)} %get-tuple-element.14.own, f32[42,128]{1,0:T(8,128)S(1)} %get-tuple-element.15.x_mine.after, f32[42,128]{1,0:T(8,128)S(1)} %collective-permute-done.x_even, f32[42,128]{1,0:T(8,128)S(1)} %collective-permute-done.1.x_odd), custom_call_target="tpu_custom_call" | custom-call | tf_op jit(solution)/shard_map/middle/pallas_call | solution.py:812
  8.2 2.0 %collective-permute-start.3 = (f32[110,128]{1,0:T(8,128)S(1)}, f32[110,128]{1,0:T(8,128)S(1)}, u32[]{:S(2)}, u32[]{:S(2)}) collective-permute-start(f32[110,128]{1,0:T(8,128)S(1)} %get-tuple-element.19), channel_id=1, source_target_pairs={{1,2},{2,1},{5,6},{6,5},{9,10},{10,9},{13,14},{14,13},{17,18},{18,... | collective-permute-start | bytes 168968 | tf_op jit(solution)/shard_map/ppermute | solution.py:85
  10.2 0.0 collective-permute-start.2
  10.2 0.5 %moves.1 = (bf16[256,1408]{1,0:T(8,128)(2,1)S(1)}, bf16[256,1664]{1,0:T(8,128)(2,1)S(1)}, bf16[512,256]{1,0:T(8,128)(2,1)S(1)}, bf16[384,512]{1,0:T(8,128)(2,1)S(1)}) custom-call(f32[42,128]{1,0:T(8,128)S(1)} %get-tuple-element.15.x_mine.after), custom_call_target="tpu_custom_call" | custom-call | tf_op jit(solution)/shard_map/moves/pallas_call | solution.py:804
  10.7 1.7 %collective-permute-done.3.y_odd = f32[110,128]{1,0:T(8,128)S(1)} collective-permute-done((f32[110,128]{1,0:T(8,128)S(1)}, f32[110,128]{1,0:T(8,128)S(1)}, u32[]{:S(2)}, u32[]{:S(2)}) %collective-permute-start.3) | collective-permute-done | bytes 56352 | tf_op jit(solution)/shard_map/ppermute | solution.py:85
  12.4 0.0 collective-permute-done.2.y_even
  12.4 5.3 %main.1 = (f32[8,9,4,128]{3,2,1,0:T(4,128)}, f32[8,3,4,128]{3,2,1,0:T(4,128)}) custom-call(f32[192,128]{1,0:T(8,128)S(1)} %get-tuple-element.14.own, f32[96,128]{1,0:T(8,128)S(1)} %get-tuple-element.17.beside, f32[110,128]{1,0:T(8,128)S(1)} %get-tuple-element.18.y_mine, f32[110,128]{1,0:T(8,128)S(1)} %collective-permute-done.2.y_even, ...), custom_call_target="tpu_custom_call" | custom-call | tf_op jit(solution)/shard_map/main/pallas_call | solution.py:823
Async XLA Ops:
  1.6 4.6 %collective-permute-start.1 = (f32[42,128]{1,0:T(8,128)S(1)}, f32[42,128]{1,0:T(8,128)S(1)}, u32[]{:S(2)}, u32[]{:S(2)}) collective-permute-start(f32[42,128]{1,0:T(8,128)S(1)} %get-tuple-element.16), channel_id=1, source_target_pairs={{4,8},{5,9},{6,10},{7,11},{8,4},{9,5},{10,6},{11,7},{12,16},{13,17... | collective-permute-start | bytes 64520 | tf_op jit(solution)/shard_map/ppermute | solution.py:85
  2.2 5.8 %collective-permute-start = (f32[42,128]{1,0:T(8,128)S(1)}, f32[42,128]{1,0:T(8,128)S(1)}, u32[]{:S(2)}, u32[]{:S(2)}) collective-permute-start(f32[42,128]{1,0:T(8,128)S(1)} %get-tuple-element.15.x_mine.after), channel_id=1, source_target_pairs={{0,4},{1,5},{2,6},{3,7},{4,0},{5,1},{6,2},{7,3},{8,12},{9,13},{10,... | collective-permute-start | bytes 64520 | tf_op jit(solution)/shard_map/ppermute | solution.py:85
  8.2 4.2 %collective-permute-start.3 = (f32[110,128]{1,0:T(8,128)S(1)}, f32[110,128]{1,0:T(8,128)S(1)}, u32[]{:S(2)}, u32[]{:S(2)}) collective-permute-start(f32[110,128]{1,0:T(8,128)S(1)} %get-tuple-element.19), channel_id=1, source_target_pairs={{1,2},{2,1},{5,6},{6,5},{9,10},{10,9},{13,14},{14,13},{17,18},{18,... | collective-permute-start | bytes 168968 | tf_op jit(solution)/shard_map/ppermute | solution.py:85
  10.2 2.2 %collective-permute-start.2 = (f32[110,128]{1,0:T(8,128)S(1)}, f32[110,128]{1,0:T(8,128)S(1)}, u32[]{:S(2)}, u32[]{:S(2)}) collective-permute-start(f32[110,128]{1,0:T(8,128)S(1)} %get-tuple-element.18.y_mine), channel_id=1, source_target_pairs={{0,1},{1,0},{2,3},{3,2},{4,5},{5,4},{6,7},{7,6},{8,9},{9,8},{10,11... | collective-permute-start | bytes 168968 | tf_op jit(solution)/shard_map/ppermute | solution.py:85

commit v6 on v5

--- a/solution.py
+++ b/solution.py
@@ -78,7 +78,7 @@
         if not left:
             to[one] = one
             break
-        other = min(left, key=lambda at: (axis == "gy" and at != (one[0] ^ 2, one[1]), abs(at[0] - one[0]) + abs(at[1] - one[1]), -at[0] - at[1]))
+        other = min(left, key=lambda at: (axis == "gy" and at[0] != one[0], abs(at[0] - one[0]) + abs(at[1] - one[1]), -at[0] - at[1]))
         left.remove(other)
         to[one], to[other] = other, one
     pairs = [(i * ny + j, k * ny + l) for (i, j), (k, l) in to.items()]
@@ -551,18 +551,22 @@
 
         for depths in ((0,), (1,), (-1,), (2,), (-2,), (3,), (-3,)):
             here = {dz: tall[24 * at + 8 - dz : 24 * at + 16 - dz, :] for dz in depths}
-            terms = {dz: [{} for _ in range(4)] for dz in depths}
+            strengths = {dz: {} for dz in depths}
             for dx, steps in bond_steps(depths[0]):
                 for dy in steps:
+                    limit = patch[base + (dx + REACH) * PATCH_Y + dy + REACH]
+                    for dz in depths:
+                        strengths[dz][dx, dy] = jnp.minimum(here[dz], limit)
+
+            def sums_of(dz, c):
+                terms = {}
+                for (dx, dy), strength in strengths[dz].items():
                     k = base + (dx + REACH) * PATCH_Y + dy + REACH
-                    limit = patch[k]
-                    amounts = [patch[(1 + c) * ENTRIES + k] for c in range(4)]
-                    for dz in depths:
-                        strength = jnp.minimum(here[dz], limit)
-                        for c in range(4):
-                            terms[dz][c][dx, dy] = strength * amounts[c]
-            acc = {dz: lattice_sums(terms[dz][0], True) for dz in depths}
-            acc_u = {dz: [lattice_sums(terms[dz][1 + c], False) for c in range(3)] for dz in depths}
+                    terms[dx, dy] = strength * patch[(1 + c) * ENTRIES + k]
+                return lattice_sums(terms, c == 0)
+
+            acc = {dz: sums_of(dz, 0) for dz in depths}
+            acc_u = {dz: [sums_of(dz, 1 + c) for c in range(3)] for dz in depths}
 
             for dz in depths:
 

time: 17.9 us -> 17.8 us (level)
  starting transfers between devices: 6.56 us -> 6.24 us
  waiting for transfers between devices: 3.51 us -> 3.78 us
    ppermute x4, starting transfers between devices: 6.56 us -> 6.24 us  [swap(): return lax.ppermute(array, ('gx', 'gy'), pairs)]
    ppermute x4, waiting for transfers between devices: 3.51 us -> 3.78 us  [swap(): return lax.ppermute(array, ('gx', 'gy'), pairs)]
where the time goes in v6:
time: 17.8 us; the launch traced here: 17.7 us
  Pallas kernels  6.98 us (39%)
  starting transfers between devices  6.24 us (35%)
  waiting for transfers between devices  3.78 us (21%)
  between operations  0.66 us (4%)
    ppermute x4, starting transfers between devices, swap(): return lax.ppermute(array, ('gx', 'gy'), pairs)  6.24 us
    pallas_call x1, Pallas kernels, local(): pl.pallas_call(functools.partial(main_kernel, nx, ny), out_shape=(jax.Sha...  5.26 us
    ppermute x4, waiting for transfers between devices, swap(): return lax.ppermute(array, ('gx', 'gy'), pairs)  3.78 us
    pallas_call x1, Pallas kernels, local(): pl.pallas_call(functools.partial(pack_kernel, nx, ny), out_shape=(jax.Sha...  1 us
    pallas_call x1, Pallas kernels, local(): pl.pallas_call(functools.partial(moves_kernel, nx, ny), out_shape=move_sh...  0.53 us
  transfers between devices with their start and end apart: 4, of which 2 were waited for; matrix products, arithmetic and copies ran while one was open for 0% of the time, Pallas kernels for 3%

profile of v6, /device:TPU:0, one launch (start us, length us, event | category | flops | bytes accessed | tf_op | source)
XLA Modules:
  0.0 17.7 jit_solution(6504807375278028136)
XLA Ops:
  0.6 1.0 %pack.1 = (f32[192,128]{1,0:T(8,128)S(1)}, f32[42,128]{1,0:T(8,128)S(1)}, f32[42,128]{1,0:T(8,128)S(1)}) custom-call(f32[8,3,4,128]{3,2,1,0:T(4,128)} %bitcast.6, f32[8,4,128]{2,1,0:T(4,128)} %vol.1, f32[8,4,128]{2,1,0:T(4,128)} %health.1, s32[8,4,128]{2,1,0:T(4,128)} %damage.1, s32[4,162]{1,0:T(4,128)} %bitcast.7), custom_call_target="tpu_custom_call" | custom-call | tf_op jit(solution)/shard_map/pack/pallas_call | solution.py:786
  1.6 0.5 %collective-permute-start.1 = (f32[42,128]{1,0:T(8,128)S(1)}, f32[42,128]{1,0:T(8,128)S(1)}, u32[]{:S(2)}, u32[]{:S(2)}) collective-permute-start(f32[42,128]{1,0:T(8,128)S(1)} %get-tuple-element.16), channel_id=1, source_target_pairs={{4,8},{5,9},{6,10},{7,11},{8,4},{9,5},{10,6},{11,7},{12,16},{13,17... | collective-permute-start | bytes 64520 | tf_op jit(solution)/shard_map/ppermute | solution.py:85
  2.2 4.0 %collective-permute-start = (f32[42,128]{1,0:T(8,128)S(1)}, f32[42,128]{1,0:T(8,128)S(1)}, u32[]{:S(2)}, u32[]{:S(2)}) collective-permute-start(f32[42,128]{1,0:T(8,128)S(1)} %get-tuple-element.15.x_mine.after), channel_id=1, source_target_pairs={{0,4},{1,5},{2,6},{3,7},{4,0},{5,1},{6,2},{7,3},{8,12},{9,13},{10,... | collective-permute-start | bytes 64520 | tf_op jit(solution)/shard_map/ppermute | solution.py:85
  6.2 0.0 collective-permute-done.1.x_odd
  6.2 1.8 %collective-permute-done.x_even = f32[42,128]{1,0:T(8,128)S(1)} collective-permute-done((f32[42,128]{1,0:T(8,128)S(1)}, f32[42,128]{1,0:T(8,128)S(1)}, u32[]{:S(2)}, u32[]{:S(2)}) %collective-permute-start) | collective-permute-done | bytes 21536 | tf_op jit(solution)/shard_map/ppermute | solution.py:85
  8.0 0.2 %middle.1 = (f32[110,128]{1,0:T(8,128)S(1)}, f32[110,128]{1,0:T(8,128)S(1)}, f32[96,128]{1,0:T(8,128)S(1)}) custom-call(f32[192,128]{1,0:T(8,128)S(1)} %get-tuple-element.14.own, f32[42,128]{1,0:T(8,128)S(1)} %get-tuple-element.15.x_mine.after, f32[42,128]{1,0:T(8,128)S(1)} %collective-permute-done.x_even, f32[42,128]{1,0:T(8,128)S(1)} %collective-permute-done.1.x_odd), custom_call_target="tpu_custom_call" | custom-call | tf_op jit(solution)/shard_map/middle/pallas_call | solution.py:816
  8.2 0.1 collective-permute-start.3
  8.3 1.6 %collective-permute-start.2 = (f32[110,128]{1,0:T(8,128)S(1)}, f32[110,128]{1,0:T(8,128)S(1)}, u32[]{:S(2)}, u32[]{:S(2)}) collective-permute-start(f32[110,128]{1,0:T(8,128)S(1)} %get-tuple-element.18.y_mine), channel_id=1, source_target_pairs={{0,1},{1,0},{2,3},{3,2},{4,5},{5,4},{6,7},{7,6},{8,9},{9,8},{10,11... | collective-permute-start | bytes 168968 | tf_op jit(solution)/shard_map/ppermute | solution.py:85
  9.9 0.5 %moves.1 = (bf16[256,1408]{1,0:T(8,128)(2,1)S(1)}, bf16[256,1664]{1,0:T(8,128)(2,1)S(1)}, bf16[512,256]{1,0:T(8,128)(2,1)S(1)}, bf16[384,512]{1,0:T(8,128)(2,1)S(1)}) custom-call(f32[42,128]{1,0:T(8,128)S(1)} %get-tuple-element.15.x_mine.after), custom_call_target="tpu_custom_call" | custom-call | tf_op jit(solution)/shard_map/moves/pallas_call | solution.py:808
  10.4 2.0 %collective-permute-done.3.y_odd = f32[110,128]{1,0:T(8,128)S(1)} collective-permute-done((f32[110,128]{1,0:T(8,128)S(1)}, f32[110,128]{1,0:T(8,128)S(1)}, u32[]{:S(2)}, u32[]{:S(2)}) %collective-permute-start.3) | collective-permute-done | bytes 56352 | tf_op jit(solution)/shard_map/ppermute | solution.py:85
  12.4 0.0 collective-permute-done.2.y_even
  12.4 5.3 %main.1 = (f32[8,9,4,128]{3,2,1,0:T(4,128)}, f32[8,3,4,128]{3,2,1,0:T(4,128)}) custom-call(f32[192,128]{1,0:T(8,128)S(1)} %get-tuple-element.14.own, f32[96,128]{1,0:T(8,128)S(1)} %get-tuple-element.17.beside, f32[110,128]{1,0:T(8,128)S(1)} %get-tuple-element.18.y_mine, f32[110,128]{1,0:T(8,128)S(1)} %collective-permute-done.2.y_even, ...), custom_call_target="tpu_custom_call" | custom-call | tf_op jit(solution)/shard_map/main/pallas_call | solution.py:827
Async XLA Ops:
  1.6 4.6 %collective-permute-start.1 = (f32[42,128]{1,0:T(8,128)S(1)}, f32[42,128]{1,0:T(8,128)S(1)}, u32[]{:S(2)}, u32[]{:S(2)}) collective-permute-start(f32[42,128]{1,0:T(8,128)S(1)} %get-tuple-element.16), channel_id=1, source_target_pairs={{4,8},{5,9},{6,10},{7,11},{8,4},{9,5},{10,6},{11,7},{12,16},{13,17... | collective-permute-start | bytes 64520 | tf_op jit(solution)/shard_map/ppermute | solution.py:85
  2.2 5.8 %collective-permute-start = (f32[42,128]{1,0:T(8,128)S(1)}, f32[42,128]{1,0:T(8,128)S(1)}, u32[]{:S(2)}, u32[]{:S(2)}) collective-permute-start(f32[42,128]{1,0:T(8,128)S(1)} %get-tuple-element.15.x_mine.after), channel_id=1, source_target_pairs={{0,4},{1,5},{2,6},{3,7},{4,0},{5,1},{6,2},{7,3},{8,12},{9,13},{10,... | collective-permute-start | bytes 64520 | tf_op jit(solution)/shard_map/ppermute | solution.py:85
  8.2 4.2 %collective-permute-start.3 = (f32[110,128]{1,0:T(8,128)S(1)}, f32[110,128]{1,0:T(8,128)S(1)}, u32[]{:S(2)}, u32[]{:S(2)}) collective-permute-start(f32[110,128]{1,0:T(8,128)S(1)} %get-tuple-element.19), channel_id=1, source_target_pairs={{1,2},{2,1},{5,6},{6,5},{9,10},{10,9},{13,14},{14,13},{17,18},{18,... | collective-permute-start | bytes 168968 | tf_op jit(solution)/shard_map/ppermute | solution.py:85
  8.3 4.1 %collective-permute-start.2 = (f32[110,128]{1,0:T(8,128)S(1)}, f32[110,128]{1,0:T(8,128)S(1)}, u32[]{:S(2)}, u32[]{:S(2)}) collective-permute-start(f32[110,128]{1,0:T(8,128)S(1)} %get-tuple-element.18.y_mine), channel_id=1, source_target_pairs={{0,1},{1,0},{2,3},{3,2},{4,5},{5,4},{6,7},{7,6},{8,9},{9,8},{10,11... | collective-permute-start | bytes 168968 | tf_op jit(solution)/shard_map/ppermute | solution.py:85

commit v7 on v6

--- a/solution.py
+++ b/solution.py
@@ -273,18 +273,20 @@
                 beside[row + part * half : row + (part + 1) * half, :] = value
             beside[row + ny : row + 2 * ny, :] = rows[ROWS + field * ny : ROWS + (field + 1) * ny]
 
-    def line(target, row, field, y):
+    def line(target, row, field, low, high):
+        y = low + high * (ny - 1 - 2 * low)
         base = field * 4 * ny
         for e, column in ((0, 0), (1, 1), (nx + 2, 3), (nx + 3, 2)):
             target[row + e : row + e + 1, :] = beside[pl.ds(base + column * ny + y, 1), :]
-        target[row + RING : row + RING + nx, :] = own[pl.ds(field * nx * ny + y, nx, stride=ny), :]
+        ends = [own[pl.ds(field * nx * ny + at, nx, stride=ny), :] for at in (low, ny - 1 - low)]
+        target[row + RING : row + RING + nx, :] = jnp.where(high == 1, ends[1], ends[0])
 
     for target, high in ((to_even, 1 - odd_y), (to_odd, odd_y)):
         target[0:ROWS, :] = table
         for field in range(FIELDS):
-            line(target, ROWS + field * ext_x, field, high * (ny - 1))
+            line(target, ROWS + field * ext_x, field, 0, high)
         for field in range(FAR):
-            line(far, field * ext_x, field, 1 + high * (ny - 3))
+            line(far, field * ext_x, field, 1, high)
         halves = [
             jnp.concatenate(
                 [

time: 17.8 us -> 17.8 us (level)
  no operation moved by 1% of the time
where the time goes in v7:
time: 17.8 us; the launch traced here: 17.7 us
  Pallas kernels  6.97 us (39%)
  starting transfers between devices  6.24 us (35%)
  waiting for transfers between devices  3.78 us (21%)
  between operations  0.66 us (4%)
    ppermute x4, starting transfers between devices, swap(): return lax.ppermute(array, ('gx', 'gy'), pairs)  6.24 us
    pallas_call x1, Pallas kernels, local(): pl.pallas_call(functools.partial(main_kernel, nx, ny), out_shape=(jax.Sha...  5.26 us
    ppermute x4, waiting for transfers between devices, swap(): return lax.ppermute(array, ('gx', 'gy'), pairs)  3.78 us
    pallas_call x1, Pallas kernels, local(): pl.pallas_call(functools.partial(pack_kernel, nx, ny), out_shape=(jax.Sha...  1 us
    pallas_call x1, Pallas kernels, local(): pl.pallas_call(functools.partial(moves_kernel, nx, ny), out_shape=move_sh...  0.53 us
  transfers between devices with their start and end apart: 4, of which 2 were waited for; matrix products, arithmetic and copies ran while one was open for 0% of the time, Pallas kernels for 3%

profile of v7, /device:TPU:0, one launch (start us, length us, event | category | flops | bytes accessed | tf_op | source)
XLA Modules:
  0.0 17.7 jit_solution(6548988222902551645)
XLA Ops:
  0.6 1.0 %pack.1 = (f32[192,128]{1,0:T(8,128)S(1)}, f32[42,128]{1,0:T(8,128)S(1)}, f32[42,128]{1,0:T(8,128)S(1)}) custom-call(f32[8,3,4,128]{3,2,1,0:T(4,128)} %bitcast.6, f32[8,4,128]{2,1,0:T(4,128)} %vol.1, f32[8,4,128]{2,1,0:T(4,128)} %health.1, s32[8,4,128]{2,1,0:T(4,128)} %damage.1, s32[4,162]{1,0:T(4,128)} %bitcast.7), custom_call_target="tpu_custom_call" | custom-call | tf_op jit(solution)/shard_map/pack/pallas_call | solution.py:788
  1.6 0.5 %collective-permute-start.1 = (f32[42,128]{1,0:T(8,128)S(1)}, f32[42,128]{1,0:T(8,128)S(1)}, u32[]{:S(2)}, u32[]{:S(2)}) collective-permute-start(f32[42,128]{1,0:T(8,128)S(1)} %get-tuple-element.16), channel_id=1, source_target_pairs={{4,8},{5,9},{6,10},{7,11},{8,4},{9,5},{10,6},{11,7},{12,16},{13,17... | collective-permute-start | bytes 64520 | tf_op jit(solution)/shard_map/ppermute | solution.py:85
  2.2 4.0 %collective-permute-start = (f32[42,128]{1,0:T(8,128)S(1)}, f32[42,128]{1,0:T(8,128)S(1)}, u32[]{:S(2)}, u32[]{:S(2)}) collective-permute-start(f32[42,128]{1,0:T(8,128)S(1)} %get-tuple-element.15.x_mine.after), channel_id=1, source_target_pairs={{0,4},{1,5},{2,6},{3,7},{4,0},{5,1},{6,2},{7,3},{8,12},{9,13},{10,... | collective-permute-start | bytes 64520 | tf_op jit(solution)/shard_map/ppermute | solution.py:85
  6.2 0.0 collective-permute-done.1.x_odd
  6.2 1.8 %collective-permute-done.x_even = f32[42,128]{1,0:T(8,128)S(1)} collective-permute-done((f32[42,128]{1,0:T(8,128)S(1)}, f32[42,128]{1,0:T(8,128)S(1)}, u32[]{:S(2)}, u32[]{:S(2)}) %collective-permute-start) | collective-permute-done | bytes 21536 | tf_op jit(solution)/shard_map/ppermute | solution.py:85
  8.0 0.2 %middle.1 = (f32[110,128]{1,0:T(8,128)S(1)}, f32[110,128]{1,0:T(8,128)S(1)}, f32[96,128]{1,0:T(8,128)S(1)}) custom-call(f32[192,128]{1,0:T(8,128)S(1)} %get-tuple-element.14.own, f32[42,128]{1,0:T(8,128)S(1)} %get-tuple-element.15.x_mine.after, f32[42,128]{1,0:T(8,128)S(1)} %collective-permute-done.x_even, f32[42,128]{1,0:T(8,128)S(1)} %collective-permute-done.1.x_odd), custom_call_target="tpu_custom_call" | custom-call | tf_op jit(solution)/shard_map/middle/pallas_call | solution.py:818
  8.2 0.1 collective-permute-start.3
  8.3 1.6 %collective-permute-start.2 = (f32[110,128]{1,0:T(8,128)S(1)}, f32[110,128]{1,0:T(8,128)S(1)}, u32[]{:S(2)}, u32[]{:S(2)}) collective-permute-start(f32[110,128]{1,0:T(8,128)S(1)} %get-tuple-element.18.y_mine), channel_id=1, source_target_pairs={{0,1},{1,0},{2,3},{3,2},{4,5},{5,4},{6,7},{7,6},{8,9},{9,8},{10,11... | collective-permute-start | bytes 168968 | tf_op jit(solution)/shard_map/ppermute | solution.py:85
  9.9 0.5 %moves.1 = (bf16[256,1408]{1,0:T(8,128)(2,1)S(1)}, bf16[256,1664]{1,0:T(8,128)(2,1)S(1)}, bf16[512,256]{1,0:T(8,128)(2,1)S(1)}, bf16[384,512]{1,0:T(8,128)(2,1)S(1)}) custom-call(f32[42,128]{1,0:T(8,128)S(1)} %get-tuple-element.15.x_mine.after), custom_call_target="tpu_custom_call" | custom-call | tf_op jit(solution)/shard_map/moves/pallas_call | solution.py:810
  10.4 2.0 %collective-permute-done.3.y_odd = f32[110,128]{1,0:T(8,128)S(1)} collective-permute-done((f32[110,128]{1,0:T(8,128)S(1)}, f32[110,128]{1,0:T(8,128)S(1)}, u32[]{:S(2)}, u32[]{:S(2)}) %collective-permute-start.3) | collective-permute-done | bytes 56352 | tf_op jit(solution)/shard_map/ppermute | solution.py:85
  12.4 0.0 collective-permute-done.2.y_even
  12.4 5.3 %main.1 = (f32[8,9,4,128]{3,2,1,0:T(4,128)}, f32[8,3,4,128]{3,2,1,0:T(4,128)}) custom-call(f32[192,128]{1,0:T(8,128)S(1)} %get-tuple-element.14.own, f32[96,128]{1,0:T(8,128)S(1)} %get-tuple-element.17.beside, f32[110,128]{1,0:T(8,128)S(1)} %get-tuple-element.18.y_mine, f32[110,128]{1,0:T(8,128)S(1)} %collective-permute-done.2.y_even, ...), custom_call_target="tpu_custom_call" | custom-call | tf_op jit(solution)/shard_map/main/pallas_call | solution.py:829
Async XLA Ops:
  1.6 4.6 %collective-permute-start.1 = (f32[42,128]{1,0:T(8,128)S(1)}, f32[42,128]{1,0:T(8,128)S(1)}, u32[]{:S(2)}, u32[]{:S(2)}) collective-permute-start(f32[42,128]{1,0:T(8,128)S(1)} %get-tuple-element.16), channel_id=1, source_target_pairs={{4,8},{5,9},{6,10},{7,11},{8,4},{9,5},{10,6},{11,7},{12,16},{13,17... | collective-permute-start | bytes 64520 | tf_op jit(solution)/shard_map/ppermute | solution.py:85
  2.2 5.8 %collective-permute-start = (f32[42,128]{1,0:T(8,128)S(1)}, f32[42,128]{1,0:T(8,128)S(1)}, u32[]{:S(2)}, u32[]{:S(2)}) collective-permute-start(f32[42,128]{1,0:T(8,128)S(1)} %get-tuple-element.15.x_mine.after), channel_id=1, source_target_pairs={{0,4},{1,5},{2,6},{3,7},{4,0},{5,1},{6,2},{7,3},{8,12},{9,13},{10,... | collective-permute-start | bytes 64520 | tf_op jit(solution)/shard_map/ppermute | solution.py:85
  8.2 4.2 %collective-permute-start.3 = (f32[110,128]{1,0:T(8,128)S(1)}, f32[110,128]{1,0:T(8,128)S(1)}, u32[]{:S(2)}, u32[]{:S(2)}) collective-permute-start(f32[110,128]{1,0:T(8,128)S(1)} %get-tuple-element.19), channel_id=1, source_target_pairs={{1,2},{2,1},{5,6},{6,5},{9,10},{10,9},{13,14},{14,13},{17,18},{18,... | collective-permute-start | bytes 168968 | tf_op jit(solution)/shard_map/ppermute | solution.py:85
  8.3 4.1 %collective-permute-start.2 = (f32[110,128]{1,0:T(8,128)S(1)}, f32[110,128]{1,0:T(8,128)S(1)}, u32[]{:S(2)}, u32[]{:S(2)}) collective-permute-start(f32[110,128]{1,0:T(8,128)S(1)} %get-tuple-element.18.y_mine), channel_id=1, source_target_pairs={{0,1},{1,0},{2,3},{3,2},{4,5},{5,4},{6,7},{7,6},{8,9},{9,8},{10,11... | collective-permute-start | bytes 168968 | tf_op jit(solution)/shard_map/ppermute | solution.py:85
